TPU v7x, 32 devices: a whole 2x2x4 slice. The times are simulated.
32 devices in a mesh: node: 16 (over z, x, core), local: 2 (over y).
Axes of the slice: x: 2, y: 2, z: 4, core: 2. Of those that a mesh axis runs over, the one named last changes fastest.
Arguments:
- grad_values: bfloat16 [32, 8192, 512], P(('node', 'local')), may hold values from -1.75 to 1.75
- grad_exponents: int32 [32, 4, 8192], P(('node', 'local')), may hold values from -1 to 2
- proj: float32 [8192, 256], P(('local', 'node')), may hold values from -0.75 to 0.75
- weights: float32 [8192, 512], P(('local', 'node')), may hold values from -4 to 4
- moment1: float32 [256, 512], P('node'), may hold values from -6 to 6
- moment2: float32 [256, 512], P('node'), may hold values from 1 to 100
Outputs:
- quant_values: bfloat16 [8192, 512], P('local')
- quant_scales: bfloat16 [4, 8192], P(None, 'local')
- new_weights: float32 [8192, 512], P(('local', 'node'))
- new_moment1: float32 [256, 512], P('node')
- new_moment2: float32 [256, 512], P('node')
All inputs are finite; a program needn't handle non-finite values. Where the computation divides by a largest or mean magnitude, that divisor is 1e-20 or more.
Results may differ from a plain program's by a relative error of at most 0.0085.
Values may be sent and summed in bfloat16 or wider, within the bound.
No kernel may reach another device: no remote copies, remote signals or barrier semaphores. Data moves between devices by JAX's collectives and lax.ppermute only.
A program may use at most 128 MiB of HBM per device.

v0:
```python
import jax
import jax.numpy as jnp
from jax import lax
from jax.sharding import PartitionSpec as P

bias_first = 1.0 - 0.9**10
bias_second = 1.0 - 0.999**10


def moments_update(owned, moment1, moment2):
    first = 0.9 * moment1 + 0.1 * owned
    second = 0.999 * moment2 + 0.001 * owned * owned
    tilde = first / bias_first / (jnp.sqrt(second / bias_second) + 1e-08)
    return (first, second, tilde)


def shards(grad_values, grad_exponents, proj, weights, moment1, moment2):
    exponent = grad_exponents[0]
    width, columns = (grad_values.shape[1], grad_values.shape[2])
    nblocks = exponent.shape[0]
    blocksize = columns // nblocks
    factor = jnp.transpose(jnp.exp2(exponent.astype(jnp.float32)))
    local_count = lax.axis_size("local")
    mantissa = grad_values[0].astype(jnp.float32)
    dequant = (mantissa.reshape(width, nblocks, blocksize) * factor[:, :, None]).reshape(
        width, columns
    )
    across = lax.psum_scatter(
        dequant.reshape(local_count, width // local_count, columns),
        "node",
        scatter_dimension=1,
        tiled=True,
    )
    owned_grad = lax.psum_scatter(across, "local", scatter_dimension=0, tiled=True)[0]
    partial_value = jnp.dot(
        jnp.transpose(proj),
        owned_grad,
        precision=lax.Precision.HIGHEST,
        preferred_element_type=jnp.float32,
    )
    owned_proj = lax.psum_scatter(partial_value, "node", scatter_dimension=0, tiled=True)
    owned_proj = lax.psum(owned_proj, "local")
    first, second, tilde = moments_update(owned_proj, moment1, moment2)
    raw_sq, tilde_sq = lax.psum(
        (jnp.sum(owned_proj * owned_proj, 0), jnp.sum(tilde * tilde, 0)), "node"
    )
    col_scale = jnp.sqrt(tilde_sq) / jnp.sqrt(raw_sq + 1e-06)
    new_weights = weights - 8.0 * owned_grad * col_scale[None, :]
    row_count = new_weights.shape[0]
    blocks = new_weights.reshape(row_count, nblocks, blocksize)
    block_max = (jnp.max(jnp.abs(blocks), 2) + 1e-06).astype(jnp.bfloat16)
    values = (
        (blocks / block_max.astype(jnp.float32)[:, :, None])
        .reshape(row_count, columns)
        .astype(jnp.bfloat16)
    )
    quant_values, quant_scales = (
        lax.all_gather(values, "node", axis=0, tiled=True),
        lax.all_gather(jnp.transpose(block_max), "node", axis=1, tiled=True),
    )
    return (quant_values, quant_scales, new_weights, first, second)


def solution(mesh):
    return jax.shard_map(
        shards,
        mesh=mesh,
        in_specs=(
            P(("node", "local"), None, None),
            P(("node", "local"), None, None),
            P(("local", "node"), None),
            P(("local", "node"), None),
            P("node", None),
            P("node", None),
        ),
        out_specs=(
            P("local", None),
            P(None, "local"),
            P(("local", "node"), None),
            P("node", None),
            P("node", None),
        ),
        check_vma=False,
    )
```

profile of v0, /device:TPU:1, one launch (start us, length us, event | category | flops | bytes accessed | tf_op | source)
XLA Modules:
  0.0 429.6 jit_solution(7726922637633145372)
XLA Ops:
  7.2 0.0 copy-start
  7.2 0.0 reduce-scatter.6.cloned.1.call-start
  7.2 1.0 exponential_bitcast_fusion
  8.2 2.7 copy.27
  10.9 16.6 %mul.58 = f32[8192,4,128]{2,1,0:T(4,128)} broadcast(f32[8192,4]{1,0:T(8,128)} %copy.27), dimensions={0,1} | broadcast | bytes 16908288 | tf_op jit(solution)/shard_map/mul | solution.py:25
  27.5 19.9 %mul.59 = f32[2,4096,512]{2,1,0:T(8,128)} reshape(f32[8192,4,128]{2,1,0:T(4,128)} %mul.58) | data formatting | bytes 33554432 | tf_op jit(solution)/shard_map/mul | solution.py:25
  47.4 13.9 %convert_multiply_fusion = f32[2,4096,512]{2,1,0:T(8,128)} fusion(f32[2,4096,512]{2,1,0:T(8,128)} %mul.59, bf16[2,4096,512]{2,1,0:T(8,128)(2,1)} %bitcast.24), kind=kLoop, calls=%fused_computation | loop fusion | flops 8388608 | bytes 41943040 | tf_op jit(solution)/shard_map/mul | solution.py:25
  61.3 0.0 reduce-scatter.6.cloned.1.call-update
  61.4 0.0 reduce-scatter.8.cloned.1.call-start
  61.4 180.8 %reduce-scatter.6.cloned.1.call-done = f32[2,256,512]{2,1,0:T(8,128)} async-done(((f32[2,4096,512]{2,1,0:T(8,128)}), f32[2,256,512]{2,1,0:T(8,128)}) %reduce-scatter.6.cloned.1.call-update) | async-done | bytes 1048592 | tf_op jit(solution)/shard_map/reduce_scatter | solution.py:28
  242.2 0.0 reduce-scatter.8.cloned.1.call-update
  242.2 0.0 reduce-scatter.10.cloned.1.call-start
  242.3 21.5 %reduce-scatter.8.cloned.1.call-done = f32[1,256,512]{2,1,0:T(8,128)} async-done(((f32[2,256,512]{2,1,0:T(8,128)}), f32[1,256,512]{2,1,0:T(8,128)}) %reduce-scatter.8.cloned.1.call-update) | async-done | bytes 524304 | tf_op jit(solution)/shard_map/reduce_scatter | solution.py:34
  263.8 2.0 convolution_bitcast_fusion
  265.8 1.0 copy.30
  266.8 0.0 reduce-scatter.10.cloned.1.call-update
  266.8 0.0 all-gather.2.cloned.1.call-start
  266.9 55.3 %reduce-scatter.10.cloned.1.call-done = f32[16,512]{1,0:T(8,128)} async-done(((f32[256,512]{1,0:T(8,128)}), f32[16,512]{1,0:T(8,128)}) %reduce-scatter.10.cloned.1.call-update) | async-done | bytes 32784 | tf_op jit(solution)/shard_map/reduce_scatter | solution.py:41
  322.1 7.0 %psum.21 = f32[16,512]{1,0:T(8,128)S(1)} all-reduce(f32[16,512]{1,0:T(8,128)} %reduce-scatter.10.cloned.1.call-done), channel_id=1, replica_groups=mesh['node'=16,'local'=2] {'local'}, use_global_device_ids=true, to_apply=%region_3.0 | all-reduce | flops 8192 | bytes 65536 | tf_op jit(solution)/shard_map/psum | solution.py:42
  329.1 0.6 multiply_reduce_fusion.1
  329.8 33.4 %all-reduce = (f32[512]{0:T(512)S(1)}, f32[512]{0:T(512)S(1)}) all-reduce(f32[512]{0:T(512)S(1)} %get-tuple-element.29, f32[512]{0:T(512)S(1)} %get-tuple-element.24), channel_id=1, replica_groups=mesh['node'=16,'local'=2] {'node'}, use_global_device_ids=true, to_apply=%region_7.0 | all-reduce | flops 1024 | bytes 8192 | tf_op jit(solution)/shard_map/psum | solution.py:44
  363.2 1.2 fusion.6
  364.4 0.0 copy-start.1
  364.4 0.2 abs.7
  364.6 0.3 reduce_max.9
  365.0 0.3 div.35
  365.3 0.8 fusion
  366.1 0.0 all-gather.2.cloned.1.call-update
  366.1 24.6 %all_gather.7 = bf16[4,4096]{0,1:T(8,128)(2,1)S(1)} all-gather(bf16[4,256]{0,1:T(8,128)(2,1)S(1)} %get-tuple-element.27), channel_id=1, replica_groups=mesh['node'=16,'local'=2] {'node'}, dimensions={1}, use_global_device_ids=true | all-gather | bytes 34816 | tf_op jit(solution)/shard_map/all_gather | solution.py:59
  390.7 1.0 copy.29
  391.7 26.9 %all-gather.2.cloned.1.call-done = bf16[4096,512]{1,0:T(8,128)(2,1)} async-done(((bf16[256,512]{1,0:T(8,128)(2,1)}), bf16[4096,512]{1,0:T(8,128)(2,1)}) %all-gather.2.cloned.1.call-update) | async-done | bytes 4194320 | tf_op jit(solution)/shard_map/all_gather | solution.py:58
  418.6 4.5 %copy.35 = bf16[4096,512]{1,0:T(8,128)(2,1)} copy(bf16[4096,512]{1,0:T(8,128)(2,1)} %all-gather.2.cloned.1.call-done) | data formatting | bytes 8388608
  (10 shorter events, 0.0 us)
Async XLA Ops:
  7.2 256.6 %copy-start = (f32[256,256]{1,0:T(8,128)S(1)}, f32[256,256]{1,0:T(8,128)}, u32[]{:S(2)}) copy-start(f32[256,256]{1,0:T(8,128)} %param.8) | copy-start | bytes 786436
  7.2 235.0 %reduce-scatter.6.cloned.1.call-start = ((), (), s32[]{:S(2)}) async-start(), calls=%async_computation.3 | async-start | bytes 17825792 | tf_op jit(solution)/shard_map/reduce_scatter | solution.py:28
  61.3 267.8 %copy-start.3 = (f32[16,512]{1,0:T(8,128)S(1)}, f32[16,512]{1,0:T(8,128)}, u32[]{:S(2)}) copy-start(f32[16,512]{1,0:T(8,128)} %param.10) | copy-start | bytes 98308
  61.3 267.8 %copy-start.4 = (f32[16,512]{1,0:T(8,128)S(1)}, f32[16,512]{1,0:T(8,128)}, u32[]{:S(2)}) copy-start(f32[16,512]{1,0:T(8,128)} %param.11) | copy-start | bytes 98308
  61.3 301.9 %copy-start.2 = (f32[256,512]{1,0:T(8,128)S(1)}, f32[256,512]{1,0:T(8,128)}, u32[]{:S(2)}) copy-start(f32[256,512]{1,0:T(8,128)} %param.9) | copy-start | bytes 1572868
  61.4 202.4 %reduce-scatter.8.cloned.1.call-start = ((), (), s32[]{:S(2)}) async-start(), calls=%async_computation.4 | async-start | bytes 1572864 | tf_op jit(solution)/shard_map/reduce_scatter | solution.py:34
  242.2 79.9 %reduce-scatter.10.cloned.1.call-start = ((), (), s32[]{:S(2)}) async-start(), calls=%async_computation.6 | async-start | bytes 557056 | tf_op jit(solution)/shard_map/reduce_scatter | solution.py:41
  266.8 151.7 %all-gather.2.cloned.1.call-start = ((), (), s32[]{:S(2)}) async-start(), calls=%async_computation.5 | async-start | bytes 4456448 | tf_op jit(solution)/shard_map/all_gather | solution.py:58
  364.4 58.7 %copy-start.1 = (f32[256,512]{1,0:T(8,128)}, f32[256,512]{1,0:T(8,128)S(1)}, u32[]{:S(2)}) copy-start(f32[256,512]{1,0:T(8,128)S(1)} %get-tuple-element.37) | copy-start | bytes 1572868
Sparse Core Ops, SparseCore 0:
  61.5 180.6 reduce-scatter.5
  244.5 19.2 reduce-scatter.7
  268.3 53.7 reduce-scatter.9
  366.2 52.2 all-gather.1
where the time goes:
time: 431 us; the launch traced here: 430 us
  waiting for transfers between devices  284 us (66%)
  blocking collectives  64.9 us (15%)
  local copies, waits for them, and re-layouts  46.2 us (11%)
  other arithmetic  17.9 us (4%)
  between operations  13.9 us (3%)
    reduce_scatter x1, waiting for transfers between devices, shards(): lax.psum_scatter(dequant.reshape(local_count, width // local_count, colum...  181 us
    reduce_scatter x1, waiting for transfers between devices, shards(): lax.psum_scatter(partial_value, 'node', scatter_dimension=0, tiled=True)  55.3 us
    mul x2, local copies, waits for them, and re-layouts, shards(): mantissa.reshape(width, nblocks, blocksize) * factor[:, :, None]  36.5 us
    psum x1, blocking collectives, shards(): lax.psum((jnp.sum(owned_proj * owned_proj, 0), jnp.sum(tilde * tilde, 0))...  33.4 us
    all_gather x1, waiting for transfers between devices, shards(): lax.all_gather(values, 'node', axis=0, tiled=True)  26.9 us
    all_gather x1, blocking collectives, shards(): lax.all_gather(jnp.transpose(block_max), 'node', axis=1, tiled=True)  24.6 us
    reduce_scatter x1, waiting for transfers between devices, shards(): lax.psum_scatter(across, 'local', scatter_dimension=0, tiled=True)[0]  21.5 us
    mul x1, other arithmetic, shards(): mantissa.reshape(width, nblocks, blocksize) * factor[:, :, None]  13.9 us
  transfers between devices with their start and end apart: 4, of which 4 were waited for; matrix products, arithmetic and copies ran while one was open for 0% of the time, Pallas kernels for 0%

commit v1 on v0

v1 whole, which is shorter than its diff:
```python
import functools

import jax
import jax.numpy as jnp
from jax import lax
from jax.experimental import pallas as pl
from jax.experimental.pallas import tpu as pltpu
from jax.sharding import PartitionSpec as P

f32, bf16 = jnp.float32, jnp.bfloat16
bias_first = 1.0 - 0.9**10
bias_second = 1.0 - 0.999**10
AXES = ("node", "local")
GROUPS = 2
PAD = 16
ALL = slice(None)
MIB = 2**20


def total(terms):
    return functools.reduce(lambda a, b: a + b, [t.astype(f32) for t in terms])


def at(array, index, axis):
    return lax.dynamic_index_in_dim(array, index, axis, False)


def vmem(array):
    return pltpu.with_memory_space_constraint(array, pltpu.VMEM)


def call(kernel, name, where, arrays, outs, scratch=(), limit=8, flops=0):
    nbytes = sum(a.size * a.dtype.itemsize for a in arrays)
    return pl.pallas_call(
        kernel,
        out_shape=outs,
        in_specs=[pl.BlockSpec(memory_space=pltpu.SMEM)]
        + [pl.BlockSpec(memory_space=pltpu.VMEM)] * len(arrays),
        out_specs=jax.tree.map(lambda _: pl.BlockSpec(memory_space=pltpu.VMEM), outs),
        scratch_shapes=scratch,
        compiler_params=pltpu.CompilerParams(vmem_limit_bytes=limit * MIB),
        cost_estimate=pl.CostEstimate(flops=flops, bytes_accessed=nbytes, transcendentals=0),
        name=name,
    )(where, *[vmem(a) for a in arrays])


def dequant(values, exponents, where, away, dims, blocksize, first, parts, part):
    cores, local, rest, pair, rows = dims
    nblocks = exponents.shape[0]
    columns = part * parts
    if rows % 128:
        which = lax.rem(where[2] + away, cores)
        power = jnp.exp2(exponents.astype(f32)).astype(bf16)
        picked = power.reshape(-1, local, rest, pair, cores, rows)
        picked = jnp.moveaxis(at(picked, which, 4), 0, -1)
        mant = at(values.reshape(local, rest, pair, cores, rows, -1, blocksize), which, 3)
        out = (mant * picked[..., None]).reshape(local, rest, pair, rows, -1)
        return [out[..., first + k * part : first + (k + 1) * part] for k in range(parts)]

    def kernel(where, exps, mant, *refs):
        outs, held, sems = refs[:parts], refs[parts], refs[parts + 1]
        which = lax.rem(where[2] + away, cores)
        copies = {}
        for l in range(local):
            for r in range(rest):
                copies[l, r] = pltpu.make_async_copy(
                    mant.at[l, r, :, which, :, pl.ds(first, columns)],
                    held.at[l, r],
                    sems.at[l, r],
                )
                copies[l, r].start()
        spread = lax.broadcasted_iota(jnp.int32, (nblocks, columns), 1) + first
        spread = spread // blocksize == lax.broadcasted_iota(jnp.int32, (nblocks, columns), 0)
        spread = spread.astype(bf16)
        for l in range(local):
            for r in range(rest):
                copies[l, r].wait()
                for i in range(pair):
                    start = (((l * rest + r) * pair + i) * cores + which) * rows
                    power = exps[:, pl.ds(pl.multiple_of(start, 128), rows)].astype(f32)
                    factor = lax.dot_general(
                        jnp.exp2(power).astype(bf16),
                        spread,
                        (((0,), (0,)), ((), ())),
                        preferred_element_type=f32,
                    )
                    scaled = (held[l, r, i].astype(f32) * factor).astype(bf16)
                    for k in range(parts):
                        outs[k][l, r, i] = scaled[:, k * part : (k + 1) * part]

    mant = values.reshape(local, rest, pair, cores, rows, -1)
    return pl.pallas_call(
        kernel,
        out_shape=[pltpu.VMEM((local, rest, pair, rows, part), bf16)] * parts,
        in_specs=[
            pl.BlockSpec(memory_space=pltpu.SMEM),
            pl.BlockSpec(memory_space=pltpu.VMEM),
            pl.BlockSpec(memory_space=pl.ANY),
        ],
        out_specs=[pl.BlockSpec(memory_space=pltpu.VMEM)] * parts,
        scratch_shapes=[
            pltpu.VMEM((local, rest, pair, rows, columns), bf16),
            pltpu.SemaphoreType.DMA((local, rest)),
        ],
        compiler_params=pltpu.CompilerParams(vmem_limit_bytes=16 * MIB),
        cost_estimate=pl.CostEstimate(
            flops=2 * values.size // cores,
            bytes_accessed=4 * values.shape[0] * columns // cores,
            transcendentals=0,
        ),
        name="dequant",
    )(where, vmem(exponents), pltpu.with_memory_space_constraint(mant, pltpu.HBM))


def fold(where, terms, shape):
    def kernel(where, *refs):
        place = [where[i] for i in range(4)]
        *arrays, out = refs
        out[...] = total([a[pick(*place)] for a, (_, pick) in zip(arrays, terms)]).astype(bf16)

    return call(kernel, "fold", where, [a for a, _ in terms], pltpu.VMEM(shape, bf16))


def project(where, first, second, packs, dims, ranks, nodes):
    cores, local, rest, pair, rows = dims
    half = first[0][0].shape[-1]
    group = 2 * half
    each = ranks // nodes

    def kernel(where, *refs):
        place = [where[i] for i in range(4)]
        arrays, refs = refs[: len(first) + len(second)], refs[len(first) + len(second) :]
        projs, refs = refs[:rest], refs[rest:]
        sends, outs, scratch = refs[:rest], refs[rest:-1], refs[-1]
        acc = None
        for d in range(rest):
            k = lax.rem(place[0] - d + rest, rest)
            for lo, terms, held in (
                (0, first, arrays[: len(first)]),
                (half, second, arrays[len(first) :]),
            ):
                parts = [a[pick(*place, k)] for a, (_, pick) in zip(held, terms)]
                sends[d][:, lo : lo + half] = total(parts).astype(bf16)
            term = lax.dot_general(
                projs[d][:rows], sends[d][...], (((0,), (0,)), ((), ())), preferred_element_type=f32
            )
            acc = term if acc is None else acc + term
        scratch[...] = acc.reshape(scratch.shape)
        for d, out in enumerate(outs):
            out[...] = scratch[:, lax.rem(place[2] + d, cores)].reshape(out.shape)

    out = call(
        kernel,
        "project",
        where,
        [a for a, _ in first + second] + packs,
        [pltpu.VMEM((rows, group), bf16)] * rest
        + [pltpu.VMEM((ranks // cores, group), f32)] * cores,
        [pltpu.VMEM((nodes // cores, cores, each, group), f32)],
        limit=12,
        flops=2 * rest * rows * ranks * group,
    )
    return out[:rest], out[rest:]


def add(where, terms, name):
    def kernel(where, *refs):
        *arrays, out = refs
        out[...] = total([a[...] for a in arrays]).astype(bf16)

    return call(kernel, name, where, terms, pltpu.VMEM(terms[0].shape, bf16))


def pack(where, proj, pairs):
    rows, ranks = proj.shape
    deep, columns = pairs[0].shape
    cuts = columns // ranks

    def kernel(where, *refs):
        proj, *pairs, out = refs
        out[:rows] = proj[...].astype(bf16)
        for j, held in enumerate(pairs):
            for h in range(cuts):
                start = rows + (j * cuts + h) * deep
                out[start : start + deep] = held[:, h * ranks : (h + 1) * ranks]

    shape = (rows + len(pairs) * cuts * deep, ranks)
    return call(kernel, "pack", where, [proj] + pairs, pltpu.VMEM(shape, bf16))


def normalize(where, parts, packs, dims, first, columns, nodes):
    cores, local, rest, pair, rows = dims
    ranks = packs[0].shape[1]
    group = parts[0].shape[1]
    each = ranks // nodes
    cuts = columns // ranks

    def kernel(where, *refs):
        z, x = where[0], where[1]
        arrays, held, (sums, mine, scratch) = refs[:rest], refs[rest : 2 * rest], refs[2 * rest :]
        scratch[...] = total([a[...] for a in arrays]).reshape(scratch.shape)
        mine[...] = scratch[z * pair + x]
        raw, tilde = 0.0, 0.0
        for dz in range(rest):
            for dx in range(pair):
                k = lax.rem(z - dz + rest, rest) * pair + lax.rem(x - dx + pair, pair)
                value = scratch[k]
                old = []
                for h in range(cuts):
                    start = rows + (dx * cuts + h) * 2 * each
                    old.append(held[dz][start : start + 2 * each].astype(f32))
                old = jnp.concatenate(old, 1)[:, first : first + group]
                m1 = 0.9 * old[:each] + 0.1 * value
                m2 = 0.999 * old[each:] + 0.001 * value * value
                ratio = m1 / bias_first / (jnp.sqrt(m2 / bias_second) + 1e-08)
                raw += jnp.sum(value * value, 0, keepdims=True)
                tilde += jnp.sum(ratio * ratio, 0, keepdims=True)
        sums[...] = jnp.concatenate([raw, tilde, jnp.zeros((6, group), f32)], 0)

    return call(
        kernel,
        "normalize",
        where,
        parts + packs,
        [pltpu.VMEM((8, group), f32), pltpu.VMEM((each, group), f32)],
        [pltpu.VMEM((rest * pair, each, group), f32)],
    )


def update(where, weights, moments, grads, sums, mines, blocksize):
    rows, columns = weights.shape
    count, each = len(grads), len(grads[0])
    group = columns // count

    def kernel(where, weights, moment1, moment2, *refs):
        grads, refs = refs[: count * each], refs[count * each :]
        sums, refs = refs[: count * len(sums_in[0])], refs[count * len(sums_in[0]) :]
        mines, (new_out, packed, new1, new2) = refs[:count], refs[count:]
        packed[rows:, :] = jnp.zeros((PAD, columns), bf16)
        lane = lax.broadcasted_iota(jnp.int32, (rows, 128), 1)
        scales = jnp.zeros((rows, 128), f32)
        for g in range(count):
            per = len(sums_in[0])
            added = total([s[...] for s in sums[g * per : (g + 1) * per]])
            col_scale = jnp.sqrt(added[1:2]) / jnp.sqrt(added[0:1] + 1e-06)
            for k in range(group // blocksize):
                inner = slice(k * blocksize, (k + 1) * blocksize)
                cols = slice(g * group + k * blocksize, g * group + (k + 1) * blocksize)
                grad = total([t[:, inner] for t in grads[g * each : (g + 1) * each]])
                new = weights[:, cols] - 8.0 * grad * col_scale[:, inner]
                new_out[:, cols] = new
                scale = (jnp.max(jnp.abs(new), 1, keepdims=True) + 1e-06).astype(bf16).astype(f32)
                packed[:rows, cols] = (new / scale).astype(bf16)
                scales = jnp.where(lane == g * (group // blocksize) + k, scale, scales)
            cols = slice(g * group, (g + 1) * group)
            mine = mines[g][...]
            new1[:, cols] = 0.9 * moment1[:, cols] + 0.1 * mine
            new2[:, cols] = 0.999 * moment2[:, cols] + 0.001 * mine * mine
        packed[rows:, :rows] = jnp.transpose(scales)[:PAD].astype(bf16)

    sums_in = sums
    return call(
        kernel,
        "update",
        where,
        [weights, *moments] + [t for g in grads for t in g] + [s for g in sums for s in g] + mines,
        [
            jax.ShapeDtypeStruct((rows, columns), f32),
            pltpu.VMEM((rows + PAD, columns), bf16),
            jax.ShapeDtypeStruct(moments[0].shape, f32),
            jax.ShapeDtypeStruct(moments[0].shape, f32),
        ],
    )


def lay(where, shards, places, nblocks):
    rows, columns = shards[0].shape[0] - PAD, shards[0].shape[1]
    count = len(shards)
    if rows % 128:
        places = jnp.stack([place(*[where[i] for i in range(4)]) for place in places])
        order = jnp.zeros(count, jnp.int32).at[places].set(jnp.arange(count, dtype=jnp.int32))
        stacked = jnp.take(jnp.stack(shards), order, axis=0)
        values = stacked[:, :rows].reshape(count * rows, columns)
        scales = jnp.moveaxis(stacked[:, rows : rows + nblocks, :rows], 0, 1)
        return values, scales.reshape(nblocks, count * rows)

    def kernel(where, *refs):
        held, (values, scales, sems) = refs[:count], refs[count:]
        place = [where[i] for i in range(4)]
        copies = []
        for k in range(count):
            start = pl.multiple_of(places[k](*place) * rows, 128)
            copies.append(
                pltpu.make_async_copy(
                    held[k].at[pl.ds(0, rows)], values.at[pl.ds(start, rows)], sems.at[k]
                )
            )
            copies[-1].start()
        for k in range(count):
            start = pl.multiple_of(places[k](*place) * rows, 128)
            tail = held[k][rows:, :rows].astype(f32)[:nblocks]
            scales[:, pl.ds(start, rows)] = tail.astype(bf16)
        for copy in copies:
            copy.wait()

    return pl.pallas_call(
        kernel,
        out_shape=[
            pltpu.HBM((count * rows, columns), bf16),
            jax.ShapeDtypeStruct((nblocks, count * rows), bf16),
        ],
        in_specs=[pl.BlockSpec(memory_space=pltpu.SMEM)]
        + [pl.BlockSpec(memory_space=pltpu.VMEM)] * count,
        out_specs=[pl.BlockSpec(memory_space=pl.ANY), pl.BlockSpec(memory_space=pltpu.VMEM)],
        scratch_shapes=[pltpu.SemaphoreType.DMA((count,))],
        compiler_params=pltpu.CompilerParams(vmem_limit_bytes=8 * MIB),
        cost_estimate=pl.CostEstimate(
            flops=0, bytes_accessed=4 * count * rows * columns, transcendentals=0
        ),
        name="lay",
    )(where, *[vmem(s) for s in shards])


def shards(grad_values, grad_exponents, proj, weights, moment1, moment2):
    nodes, local = lax.axis_size("node"), lax.axis_size("local")
    cores = 2 if nodes % 2 == 0 else 1
    pair = 2 if nodes // cores % 2 == 0 else 1
    rest = nodes // cores // pair
    node, y = lax.axis_index("node"), lax.axis_index("local")
    c, x, z = node % cores, node // cores % pair, node // cores // pair
    where = jnp.stack([z, x, c, y]).astype(jnp.int32)
    values, exponents = grad_values[0], grad_exponents[0]
    width, columns = values.shape
    nblocks = exponents.shape[0]
    blocksize = columns // nblocks
    rows = width // nodes // local
    ranks = proj.shape[1]
    dims = (cores, local, rest, pair, rows)

    def to(array, dz=0, dx=0, dc=0, dy=0):
        pairs = []
        for n in range(nodes):
            cc, xx, zz = n % cores, n // cores % pair, n // cores // pair
            there = ((zz + dz) % rest * pair + (xx + dx) % pair) * cores + (cc + dc) % cores
            for l in range(local):
                pairs.append((n * local + l, there * local + (l + dy) % local))
        return lax.ppermute(array, AXES, pairs)

    both = jnp.concatenate([moment1, moment2]).astype(bf16)
    packs = [pack(where, proj, [to(both, dx=d) if d else both for d in range(pair)])]
    packs += [to(packs[0], dz=d) for d in range(1, rest)]

    group = columns // GROUPS
    half = group // 2
    grads, sums, mines = [], [], []
    for g in range(GROUPS):
        cut = [[], []]
        for d in range(cores):
            for k, part in enumerate(
                dequant(values, exponents, where, d, dims, blocksize, g * group, 2, half)
            ):
                cut[k].append(to(part, dc=d) if d else part)
        first, second = cut

        over_x = []
        for d in range(1, pair):
            pick = lambda z, x, c, y, d=d: (ALL, ALL, lax.rem(x + d, pair))
            over_x.append(
                to(fold(where, [(t, pick) for t in first], (local, rest, rows, half)), dx=d)
            )
        over_y = []
        for d in range(1, local):
            pick = lambda z, x, c, y, d=d: (lax.rem(y + d, local), ALL, x)
            pick_x = lambda z, x, c, y, d=d: (lax.rem(y + d, local),)
            terms = [(t, pick) for t in first] + [(t, pick_x) for t in over_x]
            over_y.append(to(fold(where, terms, (rest, rows, half)), dy=d))
        first = (
            [(t, lambda z, x, c, y, k: (y, k, x)) for t in first]
            + [(t, lambda z, x, c, y, k: (y, k)) for t in over_x]
            + [(t, lambda z, x, c, y, k: (k,)) for t in over_y]
        )

        over_y = []
        for d in range(1, local):
            pick = lambda z, x, c, y, d=d: (lax.rem(y + d, local),)
            over_y.append(
                to(fold(where, [(t, pick) for t in second], (rest, pair, rows, half)), dy=d)
            )
        over_x = []
        for d in range(1, pair):
            pick = lambda z, x, c, y, d=d: (y, ALL, lax.rem(x + d, pair))
            pick_y = lambda z, x, c, y, d=d: (ALL, lax.rem(x + d, pair))
            terms = [(t, pick) for t in second] + [(t, pick_y) for t in over_y]
            over_x.append(to(fold(where, terms, (rest, rows, half)), dx=d))
        second = (
            [(t, lambda z, x, c, y, k: (y, k, x)) for t in second]
            + [(t, lambda z, x, c, y, k: (k, x)) for t in over_y]
            + [(t, lambda z, x, c, y, k: (k,)) for t in over_x]
        )

        parts, projected = project(where, first, second, packs, dims, ranks, nodes)
        grads.append([parts[0]] + [to(parts[rest - d], dz=d) for d in range(1, rest)])

        received = [to(projected[d], dc=d) for d in range(1, cores)]
        projected = add(where, [projected[0]] + received, "add_cores")
        by_y = []
        for dy in range(local):
            for dx in range(pair):
                by_y.append(to(projected, dx=dx, dy=dy) if dx or dy else projected)
        if local > 2:
            stacked = jnp.stack(by_y).reshape((local, pair) + projected.shape)
            stacked = jnp.take(stacked, (y - jnp.arange(local)) % local, axis=0)
            by_y = [stacked[i, j] for i in range(local) for j in range(pair)]
        projected = add_pairs(where, by_y, pair)
        projected = [projected] + [to(projected, dz=d) for d in range(1, rest)]
        added, mine = normalize(where, projected, packs, dims, g * group, columns, nodes)
        sums.append([added] + [to(added, dc=d) for d in range(1, cores)])
        mines.append(mine)

    new, packed, new1, new2 = update(
        where, weights, [moment1, moment2], grads, sums, mines, blocksize
    )

    held, places = [], []
    for dz in range(rest):
        for dx in range(pair):
            for dc in range(cores):
                if dc:
                    shard = to(held[-dc], dc=dc)
                elif dx:
                    shard = to(held[-dx * cores], dx=dx)
                else:
                    shard = to(packed, dz=dz) if dz else packed
                held.append(shard)

                def place(z, x, c, y, dz=dz, dx=dx, dc=dc):
                    zx = lax.rem(z - dz + rest, rest) * pair + lax.rem(x - dx + pair, pair)
                    return zx * cores + lax.rem(c - dc + cores, cores)

                places.append(place)
    quant, scales = lay(where, held, places, nblocks)
    return quant, scales, new, new1, new2


def add_pairs(where, terms, pair):
    def kernel(where, *refs):
        *arrays, out = refs
        runs = [total([a[...] for a in arrays[i : i + pair]]) for i in range(0, len(arrays), pair)]
        out[...] = total(runs).astype(bf16)

    return call(kernel, "add_chips", where, terms, pltpu.VMEM(terms[0].shape, bf16))


def solution(mesh):
    return jax.shard_map(
        shards,
        mesh=mesh,
        in_specs=(
            P(("node", "local"), None, None),
            P(("node", "local"), None, None),
            P(("local", "node"), None),
            P(("local", "node"), None),
            P("node", None),
            P("node", None),
        ),
        out_specs=(
            P("local", None),
            P(None, "local"),
            P(("local", "node"), None),
            P("node", None),
            P("node", None),
        ),
        check_vma=False,
    )
```

time: 431 us -> 168 us (0.39)
  waiting for transfers between devices: 284 us -> 77.1 us
  blocking collectives: 64.9 us -> 0 us
  starting transfers between devices: 0.16 us -> 56.1 us
  local copies, waits for them, and re-layouts: 46.2 us -> 0.93 us
  Pallas kernels: 0 us -> 31.9 us
  other arithmetic: 17.9 us -> 0.09 us
  between operations: 13.9 us -> 1.01 us
    reduce_scatter x3 -> x0, waiting for transfers between devices: 258 us -> none  [the longest x1 181 us: shards(): lax.psum_scatter(dequant.reshape(local_count, width // local_count, colum...]
    ppermute x0 -> x53, waiting for transfers between devices: none -> 77.1 us  [to(): return lax.ppermute(array, AXES, pairs)]
    ppermute x0 -> x53, starting transfers between devices: none -> 56.1 us  [to(): return lax.ppermute(array, AXES, pairs)]
    psum x2 -> x0, blocking collectives: 40.4 us -> none  [the longest x1 33.4 us: shards(): lax.psum((jnp.sum(owned_proj * owned_proj, 0), jnp.sum(tilde * tilde, 0))...]
    mul x2 -> x0, local copies, waits for them, and re-layouts: 36.5 us -> none  [shards(): mantissa.reshape(width, nblocks, blocksize) * factor[:, :, None]]
    pallas_call x0 -> x23, Pallas kernels: none -> 31.9 us  [the longest x4 15 us: dequant(): pl.pallas_call(kernel, out_shape=[pltpu.VMEM((local, rest, pair, rows, pa...]
    all_gather x1 -> x0, waiting for transfers between devices: 26.9 us -> none  [shards(): lax.all_gather(values, 'node', axis=0, tiled=True)]
    all_gather x1 -> x0, blocking collectives: 24.6 us -> none  [shards(): lax.all_gather(jnp.transpose(block_max), 'node', axis=1, tiled=True)]
  transfers between devices with their start and end apart: 4 -> 53, of which waited for: 4 -> 13; matrix products, arithmetic and copies ran while one was open for 0% -> 0% of each run, Pallas kernels for 0% -> 14%
where the time goes in v1:
time: 168 us; the launch traced here: 167 us
  waiting for transfers between devices  77.1 us (46%)
  starting transfers between devices  56.1 us (33%)
  Pallas kernels  31.9 us (19%)
    ppermute x53, waiting for transfers between devices, to(): return lax.ppermute(array, AXES, pairs)  77.1 us
    ppermute x53, starting transfers between devices, to(): return lax.ppermute(array, AXES, pairs)  56.1 us
    pallas_call x4, Pallas kernels, dequant(): pl.pallas_call(kernel, out_shape=[pltpu.VMEM((local, rest, pair, rows, pa...  15 us
    pallas_call x18, Pallas kernels, call(): pl.pallas_call(kernel, out_shape=outs, in_specs=[pl.BlockSpec(memory_spac...  13.6 us
  transfers between devices with their start and end apart: 53, of which 13 were waited for; matrix products, arithmetic and copies ran while one was open for 0% of the time, Pallas kernels for 14%

profile of v1, /device:TPU:1, one launch (start us, length us, event | category | flops | bytes accessed | tf_op | source)
XLA Modules:
  0.0 167.1 jit_solution(10651434995951617206)
XLA Ops:
  1.7 3.8 %dequant.7 = (bf16[2,4,2,256,128]{4,3,2,1,0:T(8,128)(2,1)S(1)}, bf16[2,4,2,256,128]{4,3,2,1,0:T(8,128)(2,1)S(1)}) custom-call(s32[4]{0:T(128)S(1)} %pad_add_fusion.where, s32[4,8192]{1,0:T(4,128)S(1)} %bitcast.6, bf16[2,4,2,2,256,512]{5,4,3,2,1,0:T(8,128)(2,1)} %bitcast.10), custom_call_target="tpu_custom_call" | custom-call | flops 4194304 | bytes 4194304 | tf_op jit(solution)/shard_map/dequant/pallas_call | solution.py:92
  6.0 3.8 %dequant.5 = (bf16[2,4,2,256,128]{4,3,2,1,0:T(8,128)(2,1)S(1)}, bf16[2,4,2,256,128]{4,3,2,1,0:T(8,128)(2,1)S(1)}) custom-call(s32[4]{0:T(128)S(1)} %pad_add_fusion.where, s32[4,8192]{1,0:T(4,128)S(1)} %bitcast.7, bf16[2,4,2,2,256,512]{5,4,3,2,1,0:T(8,128)(2,1)} %bitcast.11), custom_call_target="tpu_custom_call" | custom-call | flops 4194304 | bytes 4194304 | tf_op jit(solution)/shard_map/dequant/pallas_call | solution.py:92
  10.3 3.8 %dequant.6 = (bf16[2,4,2,256,128]{4,3,2,1,0:T(8,128)(2,1)S(1)}, bf16[2,4,2,256,128]{4,3,2,1,0:T(8,128)(2,1)S(1)}) custom-call(s32[4]{0:T(128)S(1)} %pad_add_fusion.where, s32[4,8192]{1,0:T(4,128)S(1)} %bitcast.8, bf16[2,4,2,2,256,512]{5,4,3,2,1,0:T(8,128)(2,1)} %bitcast.12), custom_call_target="tpu_custom_call" | custom-call | flops 4194304 | bytes 4194304 | tf_op jit(solution)/shard_map/dequant/pallas_call | solution.py:92
  14.8 2.4 %collective-permute-start.17 = (bf16[4,2,256,128]{3,2,1,0:T(8,128)(2,1)S(1)}, bf16[4,2,256,128]{3,2,1,0:T(8,128)(2,1)S(1)}, u32[]{:S(2)}, u32[]{:S(2)}) collective-permute-start(bf16[4,2,256,128]{3,2,1,0:T(8,128)(2,1)S(1)} %fold.14), channel_id=1, source_target_pairs={{0,1},{1,0},{2,3},{3,2},{4,5},{5,4},{6,7},{7,6},{8,9},{9,8},{10,11... | collective-permute-start | bytes 1572872 | tf_op jit(solution)/shard_map/ppermute | solution.py:347
  17.2 3.8 %dequant.4 = (bf16[2,4,2,256,128]{4,3,2,1,0:T(8,128)(2,1)S(1)}, bf16[2,4,2,256,128]{4,3,2,1,0:T(8,128)(2,1)S(1)}) custom-call(s32[4]{0:T(128)S(1)} %pad_add_fusion.where, s32[4,8192]{1,0:T(4,128)S(1)} %bitcast.9, bf16[2,4,2,2,256,512]{5,4,3,2,1,0:T(8,128)(2,1)} %bitcast.13), custom_call_target="tpu_custom_call" | custom-call | flops 4194304 | bytes 4194304 | tf_op jit(solution)/shard_map/dequant/pallas_call | solution.py:92
  21.6 1.3 collective-permute-start.14
  24.7 1.5 collective-permute-start.6
  26.2 20.2 %collective-permute-done.6.refs_2_ = bf16[32,512]{1,0:T(8,128)(2,1)S(1)} collective-permute-done((bf16[32,512]{1,0:T(8,128)(2,1)S(1)}, bf16[32,512]{1,0:T(8,128)(2,1)S(1)}, u32[]{:S(2)}, u32[]{:S(2)}) %collective-permute-start.6) | collective-permute-done | bytes 32800 | tf_op jit(solution)/shard_map/ppermute | solution.py:347
  47.0 3.4 %collective-permute-start.9 = (bf16[384,256]{1,0:T(8,128)(2,1)S(1)}, bf16[384,256]{1,0:T(8,128)(2,1)S(1)}, u32[]{:S(2)}, u32[]{:S(2)}) collective-permute-start(bf16[384,256]{1,0:T(8,128)(2,1)S(1)} %pack.1.refs_8_.refs_4_), channel_id=1, source_target_pairs={{0,24},{1,25},{2,26},{3,27},{4,28},{5,29},{6,30},{7,31},{8,0},{9,1... | collective-permute-start | bytes 589832 | tf_op jit(solution)/shard_map/ppermute | solution.py:347
  51.0 1.3 collective-permute-start.18
  55.4 11.2 %collective-permute-done.8.refs_10_.refs_6_ = bf16[384,256]{1,0:T(8,128)(2,1)S(1)} collective-permute-done((bf16[384,256]{1,0:T(8,128)(2,1)S(1)}, bf16[384,256]{1,0:T(8,128)(2,1)S(1)}, u32[]{:S(2)}, u32[]{:S(2)}) %collective-permute-start.8) | collective-permute-done | bytes 196640 | tf_op jit(solution)/shard_map/ppermute | solution.py:347
  68.0 1.7 %collective-permute-start.30 = (f32[128,256]{1,0:T(8,128)S(1)}, f32[128,256]{1,0:T(8,128)S(1)}, u32[]{:S(2)}, u32[]{:S(2)}) collective-permute-start(f32[128,256]{1,0:T(8,128)S(1)} %get-tuple-element.55), channel_id=1, source_target_pairs={{0,2},{1,3},{2,0},{3,1},{4,6},{5,7},{6,4},{7,5},{8,10},{9,11},{10,... | collective-permute-start | bytes 393224 | tf_op jit(solution)/shard_map/ppermute | solution.py:347
  69.8 3.2 %collective-permute-done.2.refs_3_ = bf16[4,256,128]{2,1,0:T(8,128)(2,1)S(1)} collective-permute-done((bf16[4,256,128]{2,1,0:T(8,128)(2,1)S(1)}, bf16[4,256,128]{2,1,0:T(8,128)(2,1)S(1)}, u32[]{:S(2)}, u32[]{:S(2)}) %collective-permute-start.2) | collective-permute-done | bytes 262176 | tf_op jit(solution)/shard_map/ppermute | solution.py:347
  74.2 2.4 %collective-permute-start.22 = (f32[128,256]{1,0:T(8,128)S(1)}, f32[128,256]{1,0:T(8,128)S(1)}, u32[]{:S(2)}, u32[]{:S(2)}) collective-permute-start(f32[128,256]{1,0:T(8,128)S(1)} %get-tuple-element.52), channel_id=1, source_target_pairs={{0,2},{1,3},{2,0},{3,1},{4,6},{5,7},{6,4},{7,5},{8,10},{9,11},{10,... | collective-permute-start | bytes 393224 | tf_op jit(solution)/shard_map/ppermute | solution.py:347
  84.1 2.9 %collective-permute-start.36 = (bf16[128,256]{1,0:T(8,128)(2,1)S(1)}, bf16[128,256]{1,0:T(8,128)(2,1)S(1)}, u32[]{:S(2)}, u32[]{:S(2)}) collective-permute-start(bf16[128,256]{1,0:T(8,128)(2,1)S(1)} %add_chips.3.refs_0_), channel_id=1, source_target_pairs={{0,24},{1,25},{2,26},{3,27},{4,28},{5,29},{6,30},{7,31},{8,0},{9,1... | collective-permute-start | bytes 196616 | tf_op jit(solution)/shard_map/ppermute | solution.py:347
  87.0 1.3 collective-permute-start.34
  88.9 2.1 %collective-permute-start.28 = (bf16[128,256]{1,0:T(8,128)(2,1)S(1)}, bf16[128,256]{1,0:T(8,128)(2,1)S(1)}, u32[]{:S(2)}, u32[]{:S(2)}) collective-permute-start(bf16[128,256]{1,0:T(8,128)(2,1)S(1)} %add_chips.2.refs_0_), channel_id=1, source_target_pairs={{0,24},{1,25},{2,26},{3,27},{4,28},{5,29},{6,30},{7,31},{8,0},{9,1... | collective-permute-start | bytes 196616 | tf_op jit(solution)/shard_map/ppermute | solution.py:347
  91.5 1.9 %collective-permute-start.20 = (bf16[256,256]{1,0:T(8,128)(2,1)S(1)}, bf16[256,256]{1,0:T(8,128)(2,1)S(1)}, u32[]{:S(2)}, u32[]{:S(2)}) collective-permute-start(bf16[256,256]{1,0:T(8,128)(2,1)S(1)} %get-tuple-element.49), channel_id=1, source_target_pairs={{0,16},{1,17},{2,18},{3,19},{4,20},{5,21},{6,22},{7,23},{8,24},{9,... | collective-permute-start | bytes 393224 | tf_op jit(solution)/shard_map/ppermute | solution.py:347
  93.5 2.3 %collective-permute-start.21 = (bf16[256,256]{1,0:T(8,128)(2,1)S(1)}, bf16[256,256]{1,0:T(8,128)(2,1)S(1)}, u32[]{:S(2)}, u32[]{:S(2)}) collective-permute-start(bf16[256,256]{1,0:T(8,128)(2,1)S(1)} %get-tuple-element.50), channel_id=1, source_target_pairs={{0,24},{1,25},{2,26},{3,27},{4,28},{5,29},{6,30},{7,31},{8,0},{9,1... | collective-permute-start | bytes 393224 | tf_op jit(solution)/shard_map/ppermute | solution.py:347
  95.8 3.8 %collective-permute-done.27.refs_2_ = bf16[128,256]{1,0:T(8,128)(2,1)S(1)} collective-permute-done((bf16[128,256]{1,0:T(8,128)(2,1)S(1)}, bf16[128,256]{1,0:T(8,128)(2,1)S(1)}, u32[]{:S(2)}, u32[]{:S(2)}) %collective-permute-start.27) | collective-permute-done | bytes 65568 | tf_op jit(solution)/shard_map/ppermute | solution.py:347
  99.6 2.4 %collective-permute-start.12 = (bf16[256,256]{1,0:T(8,128)(2,1)S(1)}, bf16[256,256]{1,0:T(8,128)(2,1)S(1)}, u32[]{:S(2)}, u32[]{:S(2)}) collective-permute-start(bf16[256,256]{1,0:T(8,128)(2,1)S(1)} %get-tuple-element.42), channel_id=1, source_target_pairs={{0,24},{1,25},{2,26},{3,27},{4,28},{5,29},{6,30},{7,31},{8,0},{9,1... | collective-permute-start | bytes 393224 | tf_op jit(solution)/shard_map/ppermute | solution.py:347
  103.4 4.2 %collective-permute-done.20.refs_6_ = bf16[256,256]{1,0:T(8,128)(2,1)S(1)} collective-permute-done((bf16[256,256]{1,0:T(8,128)(2,1)S(1)}, bf16[256,256]{1,0:T(8,128)(2,1)S(1)}, u32[]{:S(2)}, u32[]{:S(2)}) %collective-permute-start.20) | collective-permute-done | bytes 131104 | tf_op jit(solution)/shard_map/ppermute | solution.py:347
  107.6 4.5 %collective-permute-start.37 = (f32[8,256]{1,0:T(8,128)S(1)}, f32[8,256]{1,0:T(8,128)S(1)}, u32[]{:S(2)}, u32[]{:S(2)}) collective-permute-start(f32[8,256]{1,0:T(8,128)S(1)} %get-tuple-element.56.refs_10_), channel_id=1, source_target_pairs={{0,2},{1,3},{2,0},{3,1},{4,6},{5,7},{6,4},{7,5},{8,10},{9,11},{10,... | collective-permute-start | bytes 24584 | tf_op jit(solution)/shard_map/ppermute | solution.py:347
  112.3 3.8 %collective-permute-done.11.refs_2_ = bf16[256,256]{1,0:T(8,128)(2,1)S(1)} collective-permute-done((bf16[256,256]{1,0:T(8,128)(2,1)S(1)}, bf16[256,256]{1,0:T(8,128)(2,1)S(1)}, u32[]{:S(2)}, u32[]{:S(2)}) %collective-permute-start.11) | collective-permute-done | bytes 131104 | tf_op jit(solution)/shard_map/ppermute | solution.py:347
  116.1 1.7 %update.1 = (f32[256,512]{1,0:T(8,128)}, bf16[272,512]{1,0:T(8,128)(2,1)S(1)}, f32[16,512]{1,0:T(8,128)}, f32[16,512]{1,0:T(8,128)}) custom-call(s32[4]{0:T(128)S(1)} %pad_add_fusion.where, f32[256,512]{1,0:T(8,128)S(1)} %copy-done.1, f32[16,512]{1,0:T(8,128)S(1)} %copy-done.3, f32[16,512]{1,0:T(8,128)S(1)} %copy-done.4, ...), custom_call_target="tpu_custom_call" | custom-call | bytes 1703936 | tf_op jit(solution)/shard_map/update/pallas_call | solution.py:34
  117.8 5.2 %collective-permute-start.49 = (bf16[272,512]{1,0:T(8,128)(2,1)S(1)}, bf16[272,512]{1,0:T(8,128)(2,1)S(1)}, u32[]{:S(2)}, u32[]{:S(2)}) collective-permute-start(bf16[272,512]{1,0:T(8,128)(2,1)S(1)} %get-tuple-element.59.refs_0_), channel_id=1, source_target_pairs={{0,24},{1,25},{2,26},{3,27},{4,28},{5,29},{6,30},{7,31},{8,0},{9,1... | collective-permute-start | bytes 835592 | tf_op jit(solution)/shard_map/ppermute | solution.py:347
  124.1 2.6 %collective-permute-start.38 = (bf16[272,512]{1,0:T(8,128)(2,1)S(1)}, bf16[272,512]{1,0:T(8,128)(2,1)S(1)}, u32[]{:S(2)}, u32[]{:S(2)}) collective-permute-start(bf16[272,512]{1,0:T(8,128)(2,1)S(1)} %get-tuple-element.59.refs_0_), channel_id=1, source_target_pairs={{0,2},{1,3},{2,0},{3,1},{4,6},{5,7},{6,4},{7,5},{8,10},{9,11},{10,... | collective-permute-start | bytes 835592 | tf_op jit(solution)/shard_map/ppermute | solution.py:347
  128.1 17.1 %collective-permute-done.45.refs_8_ = bf16[272,512]{1,0:T(8,128)(2,1)S(1)} collective-permute-done((bf16[272,512]{1,0:T(8,128)(2,1)S(1)}, bf16[272,512]{1,0:T(8,128)(2,1)S(1)}, u32[]{:S(2)}, u32[]{:S(2)}) %collective-permute-start.45) | collective-permute-done | bytes 278560 | tf_op jit(solution)/shard_map/ppermute | solution.py:347
  145.2 2.3 %collective-permute-start.50 = (bf16[272,512]{1,0:T(8,128)(2,1)S(1)}, bf16[272,512]{1,0:T(8,128)(2,1)S(1)}, u32[]{:S(2)}, u32[]{:S(2)}) collective-permute-start(bf16[272,512]{1,0:T(8,128)(2,1)S(1)} %collective-permute-done.49.refs_12_), channel_id=1, source_target_pairs={{0,2},{1,3},{2,0},{3,1},{4,6},{5,7},{6,4},{7,5},{8,10},{9,11},{10,... | collective-permute-start | bytes 835592 | tf_op jit(solution)/shard_map/ppermute | solution.py:347
  149.9 5.9 %collective-permute-done.47.refs_10_ = bf16[272,512]{1,0:T(8,128)(2,1)S(1)} collective-permute-done((bf16[272,512]{1,0:T(8,128)(2,1)S(1)}, bf16[272,512]{1,0:T(8,128)(2,1)S(1)}, u32[]{:S(2)}, u32[]{:S(2)}) %collective-permute-start.47) | collective-permute-done | bytes 278560 | tf_op jit(solution)/shard_map/ppermute | solution.py:347
  157.0 4.8 %collective-permute-done.43.refs_6_ = bf16[272,512]{1,0:T(8,128)(2,1)S(1)} collective-permute-done((bf16[272,512]{1,0:T(8,128)(2,1)S(1)}, bf16[272,512]{1,0:T(8,128)(2,1)S(1)}, u32[]{:S(2)}, u32[]{:S(2)}) %collective-permute-start.43) | collective-permute-done | bytes 278560 | tf_op jit(solution)/shard_map/ppermute | solution.py:347
  163.8 3.3 %lay.1 = (bf16[4096,512]{1,0:T(8,128)(2,1)}, bf16[4,4096]{1,0:T(4,128)(2,1)}) custom-call(s32[4]{0:T(128)S(1)} %pad_add_fusion.where, bf16[272,512]{1,0:T(8,128)(2,1)S(1)} %get-tuple-element.59.refs_0_, bf16[272,512]{1,0:T(8,128)(2,1)S(1)} %collective-permute-done.38.refs_1_, bf16[272,512]{1,0:T(8,128)(2,1)S(1)} %collective-permute-done.39.refs_2_, ...), custom_call_target="tpu_custom_call" | custom-call | bytes 8388608 | tf_op jit(solution)/shard_map/lay/pallas_call | solution.py:306
  (111 shorter events, 30.4 us)
Async XLA Ops:
  5.4 8.7 %collective-permute-start.16 = (bf16[2,4,2,256,128]{4,3,2,1,0:T(8,128)(2,1)S(1)}, bf16[2,4,2,256,128]{4,3,2,1,0:T(8,128)(2,1)S(1)}, u32[]{:S(2)}, u32[]{:S(2)}) collective-permute-start(bf16[2,4,2,256,128]{4,3,2,1,0:T(8,128)(2,1)S(1)} %get-tuple-element.46), channel_id=1, source_target_pairs={{0,2},{1,3},{2,0},{3,1},{4,6},{5,7},{6,4},{7,5},{8,10},{9,11},{10,... | collective-permute-start | bytes 3145736 | tf_op jit(solution)/shard_map/ppermute | solution.py:347
  5.5 15.4 %collective-permute-start.13 = (bf16[2,4,2,256,128]{4,3,2,1,0:T(8,128)(2,1)S(1)}, bf16[2,4,2,256,128]{4,3,2,1,0:T(8,128)(2,1)S(1)}, u32[]{:S(2)}, u32[]{:S(2)}) collective-permute-start(bf16[2,4,2,256,128]{4,3,2,1,0:T(8,128)(2,1)S(1)} %get-tuple-element.44), channel_id=1, source_target_pairs={{0,2},{1,3},{2,0},{3,1},{4,6},{5,7},{6,4},{7,5},{8,10},{9,11},{10,... | collective-permute-start | bytes 3145736 | tf_op jit(solution)/shard_map/ppermute | solution.py:347
  9.8 13.2 %collective-permute-start.3 = (bf16[2,4,2,256,128]{4,3,2,1,0:T(8,128)(2,1)S(1)}, bf16[2,4,2,256,128]{4,3,2,1,0:T(8,128)(2,1)S(1)}, u32[]{:S(2)}, u32[]{:S(2)}) collective-permute-start(bf16[2,4,2,256,128]{4,3,2,1,0:T(8,128)(2,1)S(1)} %get-tuple-element.38), channel_id=1, source_target_pairs={{0,2},{1,3},{2,0},{3,1},{4,6},{5,7},{6,4},{7,5},{8,10},{9,11},{10,... | collective-permute-start | bytes 3145736 | tf_op jit(solution)/shard_map/ppermute | solution.py:347
  9.9 14.0 %collective-permute-start = (bf16[2,4,2,256,128]{4,3,2,1,0:T(8,128)(2,1)S(1)}, bf16[2,4,2,256,128]{4,3,2,1,0:T(8,128)(2,1)S(1)}, u32[]{:S(2)}, u32[]{:S(2)}) collective-permute-start(bf16[2,4,2,256,128]{4,3,2,1,0:T(8,128)(2,1)S(1)} %get-tuple-element.36), channel_id=1, source_target_pairs={{0,2},{1,3},{2,0},{3,1},{4,6},{5,7},{6,4},{7,5},{8,10},{9,11},{10,... | collective-permute-start | bytes 3145736 | tf_op jit(solution)/shard_map/ppermute | solution.py:347
  14.8 35.5 %collective-permute-start.17 = (bf16[4,2,256,128]{3,2,1,0:T(8,128)(2,1)S(1)}, bf16[4,2,256,128]{3,2,1,0:T(8,128)(2,1)S(1)}, u32[]{:S(2)}, u32[]{:S(2)}) collective-permute-start(bf16[4,2,256,128]{3,2,1,0:T(8,128)(2,1)S(1)} %fold.14), channel_id=1, source_target_pairs={{0,1},{1,0},{2,3},{3,2},{4,5},{5,4},{6,7},{7,6},{8,9},{9,8},{10,11... | collective-permute-start | bytes 1572872 | tf_op jit(solution)/shard_map/ppermute | solution.py:347
  21.6 29.4 %collective-permute-start.14 = (bf16[2,4,256,128]{3,2,1,0:T(8,128)(2,1)S(1)}, bf16[2,4,256,128]{3,2,1,0:T(8,128)(2,1)S(1)}, u32[]{:S(2)}, u32[]{:S(2)}) collective-permute-start(bf16[2,4,256,128]{3,2,1,0:T(8,128)(2,1)S(1)} %fold.12), channel_id=1, source_target_pairs={{0,4},{1,5},{2,6},{3,7},{4,0},{5,1},{6,2},{7,3},{8,12},{9,13},{10,... | collective-permute-start | bytes 1572872 | tf_op jit(solution)/shard_map/ppermute | solution.py:347
  23.6 29.3 %collective-permute-start.4 = (bf16[4,2,256,128]{3,2,1,0:T(8,128)(2,1)S(1)}, bf16[4,2,256,128]{3,2,1,0:T(8,128)(2,1)S(1)}, u32[]{:S(2)}, u32[]{:S(2)}) collective-permute-start(bf16[4,2,256,128]{3,2,1,0:T(8,128)(2,1)S(1)} %fold.10), channel_id=1, source_target_pairs={{0,1},{1,0},{2,3},{3,2},{4,5},{5,4},{6,7},{7,6},{8,9},{9,8},{10,11... | collective-permute-start | bytes 1572872 | tf_op jit(solution)/shard_map/ppermute | solution.py:347
  24.6 29.3 %collective-permute-start.1 = (bf16[2,4,256,128]{3,2,1,0:T(8,128)(2,1)S(1)}, bf16[2,4,256,128]{3,2,1,0:T(8,128)(2,1)S(1)}, u32[]{:S(2)}, u32[]{:S(2)}) collective-permute-start(bf16[2,4,256,128]{3,2,1,0:T(8,128)(2,1)S(1)} %fold.8), channel_id=1, source_target_pairs={{0,4},{1,5},{2,6},{3,7},{4,0},{5,1},{6,2},{7,3},{8,12},{9,13},{10,... | collective-permute-start | bytes 1572872 | tf_op jit(solution)/shard_map/ppermute | solution.py:347
  24.7 21.7 %collective-permute-start.6 = (bf16[32,512]{1,0:T(8,128)(2,1)S(1)}, bf16[32,512]{1,0:T(8,128)(2,1)S(1)}, u32[]{:S(2)}, u32[]{:S(2)}) collective-permute-start(bf16[32,512]{1,0:T(8,128)(2,1)S(1)} %pad_maximum_fusion.refs_1_), channel_id=1, source_target_pairs={{0,4},{1,5},{2,6},{3,7},{4,0},{5,1},{6,2},{7,3},{8,12},{9,13},{10,... | collective-permute-start | bytes 98312 | tf_op jit(solution)/shard_map/ppermute | solution.py:347
  50.3 16.3 %collective-permute-start.8 = (bf16[384,256]{1,0:T(8,128)(2,1)S(1)}, bf16[384,256]{1,0:T(8,128)(2,1)S(1)}, u32[]{:S(2)}, u32[]{:S(2)}) collective-permute-start(bf16[384,256]{1,0:T(8,128)(2,1)S(1)} %pack.1.refs_8_.refs_4_), channel_id=1, source_target_pairs={{0,16},{1,17},{2,18},{3,19},{4,20},{5,21},{6,22},{7,23},{8,24},{9,... | collective-permute-start | bytes 589832 | tf_op jit(solution)/shard_map/ppermute | solution.py:347
  51.0 15.8 %collective-permute-start.18 = (bf16[4,256,128]{2,1,0:T(8,128)(2,1)S(1)}, bf16[4,256,128]{2,1,0:T(8,128)(2,1)S(1)}, u32[]{:S(2)}, u32[]{:S(2)}) collective-permute-start(bf16[4,256,128]{2,1,0:T(8,128)(2,1)S(1)} %fold.15), channel_id=1, source_target_pairs={{0,4},{1,5},{2,6},{3,7},{4,0},{5,1},{6,2},{7,3},{8,12},{9,13},{10,... | collective-permute-start | bytes 786440 | tf_op jit(solution)/shard_map/ppermute | solution.py:347
  52.9 13.9 %collective-permute-start.15 = (bf16[4,256,128]{2,1,0:T(8,128)(2,1)S(1)}, bf16[4,256,128]{2,1,0:T(8,128)(2,1)S(1)}, u32[]{:S(2)}, u32[]{:S(2)}) collective-permute-start(bf16[4,256,128]{2,1,0:T(8,128)(2,1)S(1)} %fold.13), channel_id=1, source_target_pairs={{0,1},{1,0},{2,3},{3,2},{4,5},{5,4},{6,7},{7,6},{8,9},{9,8},{10,11... | collective-permute-start | bytes 786440 | tf_op jit(solution)/shard_map/ppermute | solution.py:347
  53.9 12.9 %collective-permute-start.7 = (bf16[384,256]{1,0:T(8,128)(2,1)S(1)}, bf16[384,256]{1,0:T(8,128)(2,1)S(1)}, u32[]{:S(2)}, u32[]{:S(2)}) collective-permute-start(bf16[384,256]{1,0:T(8,128)(2,1)S(1)} %pack.1.refs_8_.refs_4_), channel_id=1, source_target_pairs={{0,8},{1,9},{2,10},{3,11},{4,12},{5,13},{6,14},{7,15},{8,16},{9,17... | collective-permute-start | bytes 589832 | tf_op jit(solution)/shard_map/ppermute | solution.py:347
  55.1 14.7 %collective-permute-start.5 = (bf16[4,256,128]{2,1,0:T(8,128)(2,1)S(1)}, bf16[4,256,128]{2,1,0:T(8,128)(2,1)S(1)}, u32[]{:S(2)}, u32[]{:S(2)}) collective-permute-start(bf16[4,256,128]{2,1,0:T(8,128)(2,1)S(1)} %fold.11), channel_id=1, source_target_pairs={{0,4},{1,5},{2,6},{3,7},{4,0},{5,1},{6,2},{7,3},{8,12},{9,13},{10,... | collective-permute-start | bytes 786440 | tf_op jit(solution)/shard_map/ppermute | solution.py:347
  68.0 8.5 %collective-permute-start.30 = (f32[128,256]{1,0:T(8,128)S(1)}, f32[128,256]{1,0:T(8,128)S(1)}, u32[]{:S(2)}, u32[]{:S(2)}) collective-permute-start(f32[128,256]{1,0:T(8,128)S(1)} %get-tuple-element.55), channel_id=1, source_target_pairs={{0,2},{1,3},{2,0},{3,1},{4,6},{5,7},{6,4},{7,5},{8,10},{9,11},{10,... | collective-permute-start | bytes 393224 | tf_op jit(solution)/shard_map/ppermute | solution.py:347
  79.6 11.4 %collective-permute-start.19 = (bf16[256,256]{1,0:T(8,128)(2,1)S(1)}, bf16[256,256]{1,0:T(8,128)(2,1)S(1)}, u32[]{:S(2)}, u32[]{:S(2)}) collective-permute-start(bf16[256,256]{1,0:T(8,128)(2,1)S(1)} %get-tuple-element.48), channel_id=1, source_target_pairs={{0,8},{1,9},{2,10},{3,11},{4,12},{5,13},{6,14},{7,15},{8,16},{9,17... | collective-permute-start | bytes 393224 | tf_op jit(solution)/shard_map/ppermute | solution.py:347
  91.0 8.6 %collective-permute-start.27 = (bf16[128,256]{1,0:T(8,128)(2,1)S(1)}, bf16[128,256]{1,0:T(8,128)(2,1)S(1)}, u32[]{:S(2)}, u32[]{:S(2)}) collective-permute-start(bf16[128,256]{1,0:T(8,128)(2,1)S(1)} %add_chips.2.refs_0_), channel_id=1, source_target_pairs={{0,16},{1,17},{2,18},{3,19},{4,20},{5,21},{6,22},{7,23},{8,24},{9,... | collective-permute-start | bytes 196616 | tf_op jit(solution)/shard_map/ppermute | solution.py:347
  91.5 16.1 %collective-permute-start.20 = (bf16[256,256]{1,0:T(8,128)(2,1)S(1)}, bf16[256,256]{1,0:T(8,128)(2,1)S(1)}, u32[]{:S(2)}, u32[]{:S(2)}) collective-permute-start(bf16[256,256]{1,0:T(8,128)(2,1)S(1)} %get-tuple-element.49), channel_id=1, source_target_pairs={{0,16},{1,17},{2,18},{3,19},{4,20},{5,21},{6,22},{7,23},{8,24},{9,... | collective-permute-start | bytes 393224 | tf_op jit(solution)/shard_map/ppermute | solution.py:347
  93.5 18.7 %collective-permute-start.21 = (bf16[256,256]{1,0:T(8,128)(2,1)S(1)}, bf16[256,256]{1,0:T(8,128)(2,1)S(1)}, u32[]{:S(2)}, u32[]{:S(2)}) collective-permute-start(bf16[256,256]{1,0:T(8,128)(2,1)S(1)} %get-tuple-element.50), channel_id=1, source_target_pairs={{0,24},{1,25},{2,26},{3,27},{4,28},{5,29},{6,30},{7,31},{8,0},{9,1... | collective-permute-start | bytes 393224 | tf_op jit(solution)/shard_map/ppermute | solution.py:347
  95.8 16.5 %collective-permute-start.10 = (bf16[256,256]{1,0:T(8,128)(2,1)S(1)}, bf16[256,256]{1,0:T(8,128)(2,1)S(1)}, u32[]{:S(2)}, u32[]{:S(2)}) collective-permute-start(bf16[256,256]{1,0:T(8,128)(2,1)S(1)} %get-tuple-element.40), channel_id=1, source_target_pairs={{0,8},{1,9},{2,10},{3,11},{4,12},{5,13},{6,14},{7,15},{8,16},{9,17... | collective-permute-start | bytes 393224 | tf_op jit(solution)/shard_map/ppermute | solution.py:347
  99.6 16.5 %collective-permute-start.11 = (bf16[256,256]{1,0:T(8,128)(2,1)S(1)}, bf16[256,256]{1,0:T(8,128)(2,1)S(1)}, u32[]{:S(2)}, u32[]{:S(2)}) collective-permute-start(bf16[256,256]{1,0:T(8,128)(2,1)S(1)} %get-tuple-element.41), channel_id=1, source_target_pairs={{0,16},{1,17},{2,18},{3,19},{4,20},{5,21},{6,22},{7,23},{8,24},{9,... | collective-permute-start | bytes 393224 | tf_op jit(solution)/shard_map/ppermute | solution.py:347
  99.6 16.5 %collective-permute-start.12 = (bf16[256,256]{1,0:T(8,128)(2,1)S(1)}, bf16[256,256]{1,0:T(8,128)(2,1)S(1)}, u32[]{:S(2)}, u32[]{:S(2)}) collective-permute-start(bf16[256,256]{1,0:T(8,128)(2,1)S(1)} %get-tuple-element.42), channel_id=1, source_target_pairs={{0,24},{1,25},{2,26},{3,27},{4,28},{5,29},{6,30},{7,31},{8,0},{9,1... | collective-permute-start | bytes 393224 | tf_op jit(solution)/shard_map/ppermute | solution.py:347
  117.8 9.7 %collective-permute-start.49 = (bf16[272,512]{1,0:T(8,128)(2,1)S(1)}, bf16[272,512]{1,0:T(8,128)(2,1)S(1)}, u32[]{:S(2)}, u32[]{:S(2)}) collective-permute-start(bf16[272,512]{1,0:T(8,128)(2,1)S(1)} %get-tuple-element.59.refs_0_), channel_id=1, source_target_pairs={{0,24},{1,25},{2,26},{3,27},{4,28},{5,29},{6,30},{7,31},{8,0},{9,1... | collective-permute-start | bytes 835592 | tf_op jit(solution)/shard_map/ppermute | solution.py:347
  122.9 22.3 %collective-permute-start.45 = (bf16[272,512]{1,0:T(8,128)(2,1)S(1)}, bf16[272,512]{1,0:T(8,128)(2,1)S(1)}, u32[]{:S(2)}, u32[]{:S(2)}) collective-permute-start(bf16[272,512]{1,0:T(8,128)(2,1)S(1)} %get-tuple-element.59.refs_0_), channel_id=1, source_target_pairs={{0,16},{1,17},{2,18},{3,19},{4,20},{5,21},{6,22},{7,23},{8,24},{9,... | collective-permute-start | bytes 835592 | tf_op jit(solution)/shard_map/ppermute | solution.py:347
  122.9 24.6 %collective-permute-start.41 = (bf16[272,512]{1,0:T(8,128)(2,1)S(1)}, bf16[272,512]{1,0:T(8,128)(2,1)S(1)}, u32[]{:S(2)}, u32[]{:S(2)}) collective-permute-start(bf16[272,512]{1,0:T(8,128)(2,1)S(1)} %get-tuple-element.59.refs_0_), channel_id=1, source_target_pairs={{0,8},{1,9},{2,10},{3,11},{4,12},{5,13},{6,14},{7,15},{8,16},{9,17... | collective-permute-start | bytes 835592 | tf_op jit(solution)/shard_map/ppermute | solution.py:347
  123.2 25.3 %collective-permute-start.39 = (bf16[272,512]{1,0:T(8,128)(2,1)S(1)}, bf16[272,512]{1,0:T(8,128)(2,1)S(1)}, u32[]{:S(2)}, u32[]{:S(2)}) collective-permute-start(bf16[272,512]{1,0:T(8,128)(2,1)S(1)} %get-tuple-element.59.refs_0_), channel_id=1, source_target_pairs={{0,4},{1,5},{2,6},{3,7},{4,0},{5,1},{6,2},{7,3},{8,12},{9,13},{10,... | collective-permute-start | bytes 835592 | tf_op jit(solution)/shard_map/ppermute | solution.py:347
  124.1 24.8 %collective-permute-start.38 = (bf16[272,512]{1,0:T(8,128)(2,1)S(1)}, bf16[272,512]{1,0:T(8,128)(2,1)S(1)}, u32[]{:S(2)}, u32[]{:S(2)}) collective-permute-start(bf16[272,512]{1,0:T(8,128)(2,1)S(1)} %get-tuple-element.59.refs_0_), channel_id=1, source_target_pairs={{0,2},{1,3},{2,0},{3,1},{4,6},{5,7},{6,4},{7,5},{8,10},{9,11},{10,... | collective-permute-start | bytes 835592 | tf_op jit(solution)/shard_map/ppermute | solution.py:347
  127.4 21.9 %collective-permute-start.51 = (bf16[272,512]{1,0:T(8,128)(2,1)S(1)}, bf16[272,512]{1,0:T(8,128)(2,1)S(1)}, u32[]{:S(2)}, u32[]{:S(2)}) collective-permute-start(bf16[272,512]{1,0:T(8,128)(2,1)S(1)} %collective-permute-done.49.refs_12_), channel_id=1, source_target_pairs={{0,4},{1,5},{2,6},{3,7},{4,0},{5,1},{6,2},{7,3},{8,12},{9,13},{10,... | collective-permute-start | bytes 835592 | tf_op jit(solution)/shard_map/ppermute | solution.py:347
  148.6 8.4 %collective-permute-start.46 = (bf16[272,512]{1,0:T(8,128)(2,1)S(1)}, bf16[272,512]{1,0:T(8,128)(2,1)S(1)}, u32[]{:S(2)}, u32[]{:S(2)}) collective-permute-start(bf16[272,512]{1,0:T(8,128)(2,1)S(1)} %collective-permute-done.45.refs_8_), channel_id=1, source_target_pairs={{0,2},{1,3},{2,0},{3,1},{4,6},{5,7},{6,4},{7,5},{8,10},{9,11},{10,... | collective-permute-start | bytes 835592 | tf_op jit(solution)/shard_map/ppermute | solution.py:347
  148.9 13.0 %collective-permute-start.43 = (bf16[272,512]{1,0:T(8,128)(2,1)S(1)}, bf16[272,512]{1,0:T(8,128)(2,1)S(1)}, u32[]{:S(2)}, u32[]{:S(2)}) collective-permute-start(bf16[272,512]{1,0:T(8,128)(2,1)S(1)} %collective-permute-done.41.refs_4_), channel_id=1, source_target_pairs={{0,4},{1,5},{2,6},{3,7},{4,0},{5,1},{6,2},{7,3},{8,12},{9,13},{10,... | collective-permute-start | bytes 835592 | tf_op jit(solution)/shard_map/ppermute | solution.py:347
  149.3 13.3 %collective-permute-start.42 = (bf16[272,512]{1,0:T(8,128)(2,1)S(1)}, bf16[272,512]{1,0:T(8,128)(2,1)S(1)}, u32[]{:S(2)}, u32[]{:S(2)}) collective-permute-start(bf16[272,512]{1,0:T(8,128)(2,1)S(1)} %collective-permute-done.41.refs_4_), channel_id=1, source_target_pairs={{0,2},{1,3},{2,0},{3,1},{4,6},{5,7},{6,4},{7,5},{8,10},{9,11},{10,... | collective-permute-start | bytes 835592 | tf_op jit(solution)/shard_map/ppermute | solution.py:347
  149.8 12.8 %collective-permute-start.40 = (bf16[272,512]{1,0:T(8,128)(2,1)S(1)}, bf16[272,512]{1,0:T(8,128)(2,1)S(1)}, u32[]{:S(2)}, u32[]{:S(2)}) collective-permute-start(bf16[272,512]{1,0:T(8,128)(2,1)S(1)} %collective-permute-done.39.refs_2_), channel_id=1, source_target_pairs={{0,2},{1,3},{2,0},{3,1},{4,6},{5,7},{6,4},{7,5},{8,10},{9,11},{10,... | collective-permute-start | bytes 835592 | tf_op jit(solution)/shard_map/ppermute | solution.py:347
  (26 other events, 236.7 us)

commit v2 on v0

v2 whole, which is shorter than its diff:
```python
import functools

import jax
import jax.numpy as jnp
from jax import lax
from jax.experimental import pallas as pl
from jax.experimental.pallas import tpu as pltpu
from jax.sharding import PartitionSpec as P

f32, bf16 = jnp.float32, jnp.bfloat16
bias_first = 1.0 - 0.9**10
bias_second = 1.0 - 0.999**10
AXES = ("node", "local")
KNOBS = {'orders': ('xyw', 'ywx', 'wxy', 'xyw'), 'plan': ('0x', '1y', '2w', 'pack', '3x', '0y', '1w', '2x', '3y', '0w', '1x', '2y', '3w'), 'cost': {}, 'turn': False, 'late': (), 'early': False, 'sums': 1, 'cube': False, 'ag': {'lays': 2, 'ties': (), 'halves': False}}
ORDERS = KNOBS["orders"]
PLAN = KNOBS["plan"]
COST = KNOBS["cost"]
TIES = [tuple(t) for t in KNOBS["ag"]["ties"]]
PAD = 16
ALL = slice(None)
MIB = 2**20


def total(terms):
    return functools.reduce(lambda a, b: a + b, [t.astype(f32) for t in terms])


def at(array, index, axis):
    return lax.dynamic_index_in_dim(array, index, axis, False)


def vmem(array):
    return pltpu.with_memory_space_constraint(array, pltpu.VMEM)


class Grid:
    def __init__(self):
        nodes, local = lax.axis_size("node"), lax.axis_size("local")
        size, left = {"y": local}, nodes
        for axis in "cxw":
            size[axis] = 2 if left % 2 == 0 else 1
            left //= size[axis]
        size["v"] = left
        self.size, self.nodes = size, nodes

    def split(self, node):
        place = {}
        for axis in "cxwv":
            place[axis], node = node % self.size[axis], node // self.size[axis]
        return place

    def node(self, place):
        node = 0
        for axis in "vwxc":
            node = node * self.size[axis] + place[axis]
        return node

    def place(self):
        place, node = {"y": lax.axis_index("local")}, lax.axis_index("node")
        for axis in "cxwv":
            place[axis] = lax.rem(node, self.size[axis])
            node = lax.div(node, self.size[axis])
        return place

    def step(self, axis, here, d):
        size = self.size[axis]
        if size & (size - 1):
            if isinstance(here, int):
                return (here + d) % size
            return lax.rem(here + (d + size) % size, size)
        if isinstance(here, int):
            return here ^ abs(d)
        return lax.bitwise_xor(here, jnp.int32(abs(d)))

    def others(self, axis):
        return range(1, self.size[axis])

    def send(self, array, **steps):
        local, pairs = self.size["y"], []
        for n in range(self.nodes):
            for y in range(local):
                place = self.split(n) | {"y": y}
                there = {a: self.step(a, i, steps.get(a, 0)) for a, i in place.items()}
                pairs.append((n * local + y, self.node(there) * local + there["y"]))
        return lax.ppermute(array, AXES, pairs)


class Turn:
    last = None


def touch(*arrays):
    def kernel(out):
        out[...] = jnp.zeros((8, 128), f32)

    return call(kernel, "touch", [], pltpu.VMEM((8, 128), f32), extra=arrays)


def tie(array, *others):
    return pl.pallas_call(
        lambda *refs: None,
        out_shape=pltpu.VMEM(array.shape, array.dtype),
        in_specs=[pl.BlockSpec(memory_space=pl.ANY)] * (1 + len(others)),
        out_specs=pl.BlockSpec(memory_space=pl.ANY),
        input_output_aliases={0: 0},
        cost_estimate=pl.CostEstimate(flops=0, bytes_accessed=1, transcendentals=0),
        name="tie",
    )(vmem(array), *[vmem(a) for a in others])


def call(kernel, name, arrays, outs, scratch=(), limit=8, extra=()):
    after = list(extra)
    if Turn.last is not None and KNOBS["turn"]:
        after.append(Turn.last)
    count, more = len(arrays), len(after)

    def body(*refs):
        kernel(*refs[:count], *refs[count + more :])

    arrays = list(arrays) + after
    out = pl.pallas_call(
        body,
        out_shape=outs,
        in_specs=[pl.BlockSpec(memory_space=pltpu.VMEM)] * count
        + [pl.BlockSpec(memory_space=pl.ANY)] * more,
        out_specs=jax.tree.map(lambda _: pl.BlockSpec(memory_space=pltpu.VMEM), outs),
        scratch_shapes=scratch,
        compiler_params=pltpu.CompilerParams(vmem_limit_bytes=limit * MIB),
        cost_estimate=pl.CostEstimate(flops=0, bytes_accessed=COST.get(name[:4], 1), transcendentals=0),
        name=name,
    )(*[vmem(a) for a in arrays])
    Turn.last = jax.tree.leaves(out)[-1]
    return out


def dequant(grid, values, exponents, away, rows, blocksize, parts):
    cores, local, pair = (grid.size[a] for a in "cyx")
    rest = grid.size["v"] * grid.size["w"]
    shape = tuple(grid.size[a] for a in "yvwx") + (rows, values.shape[1] // parts)
    nblocks, columns = exponents.shape[0], values.shape[1]
    part = columns // parts
    if rows % 128:
        which = grid.step("c", grid.place()["c"], away)
        power = jnp.exp2(exponents.astype(f32)).astype(bf16)
        picked = power.reshape(-1, local, rest, pair, cores, rows)
        picked = jnp.moveaxis(at(picked, which, 4), 0, -1)
        mant = at(values.reshape(local, rest, pair, cores, rows, -1, blocksize), which, 3)
        out = (mant * picked[..., None]).reshape(local, rest, pair, rows, -1)
        return [out[..., k * part : (k + 1) * part].reshape(shape) for k in range(parts)]

    def kernel(exps, mant, *refs):
        outs, (held, sems) = refs[:parts], refs[parts:]
        which = grid.step("c", grid.place()["c"], away)
        copies = {}
        for l in range(local):
            for r in range(rest):
                copies[l, r] = pltpu.make_async_copy(
                    mant.at[l, r, :, which], held.at[l, r], sems.at[l, r]
                )
                copies[l, r].start()
        spread = lax.broadcasted_iota(jnp.int32, (nblocks, columns), 1) // blocksize
        spread = spread == lax.broadcasted_iota(jnp.int32, (nblocks, columns), 0)
        spread = spread.astype(bf16)
        for l in range(local):
            for r in range(rest):
                copies[l, r].wait()
                for i in range(pair):
                    start = (((l * rest + r) * pair + i) * cores + which) * rows
                    power = exps[:, pl.ds(pl.multiple_of(start, 128), rows)].astype(f32)
                    factor = lax.dot_general(
                        jnp.exp2(power).astype(bf16),
                        spread,
                        (((0,), (0,)), ((), ())),
                        preferred_element_type=f32,
                    )
                    scaled = (held[l, r, i].astype(f32) * factor).astype(bf16)
                    for k in range(parts):
                        outs[k][l, r // shape[2], r % shape[2], i] = scaled[
                            :, k * part : (k + 1) * part
                        ]

    mant = values.reshape(local, rest, pair, cores, rows, columns)
    return pl.pallas_call(
        kernel,
        out_shape=[pltpu.VMEM(shape, bf16)] * parts,
        in_specs=[
            pl.BlockSpec(memory_space=pltpu.VMEM),
            pl.BlockSpec(memory_space=pl.ANY),
        ],
        out_specs=[pl.BlockSpec(memory_space=pltpu.VMEM)] * parts,
        scratch_shapes=[
            pltpu.VMEM((local, rest, pair, rows, columns), bf16),
            pltpu.SemaphoreType.DMA((local, rest)),
        ],
        compiler_params=pltpu.CompilerParams(vmem_limit_bytes=16 * MIB),
        cost_estimate=pl.CostEstimate(flops=0, bytes_accessed=1, transcendentals=0),
        name="dequant",
    )(vmem(exponents), pltpu.with_memory_space_constraint(mant, pltpu.HBM))


class Unit:
    def __init__(self, grid, terms):
        self.grid, self.left = grid, "yvwx"
        self.terms = [(t, "yvwx") for t in terms]

    @staticmethod
    def entry(axes, where):
        return tuple(where.get(a, ALL) for a in axes)

    def hop(self, axis):
        grid, left = self.grid, self.left.replace(axis, "")
        arrays = [t for t, _ in self.terms]
        shape = tuple(grid.size[a] for a in left) + arrays[0].shape[-2:]

        def kernel(*refs):
            held, outs = refs[: len(arrays)], refs[len(arrays) :]
            place = grid.place()
            for d, out in zip(grid.others(axis), outs):
                where = {a: i for a, i in place.items() if a not in self.left}
                where[axis] = grid.step(axis, place[axis], d)
                parts = [t[self.entry(axes, where)] for t, (_, axes) in zip(held, self.terms)]
                out[...] = total(parts).astype(bf16)

        outs = [pltpu.VMEM(shape, bf16) for _ in grid.others(axis)]
        if outs:
            outs = call(kernel, "fold_" + axis, arrays, outs)
        self.left = left
        for d, out in zip(grid.others(axis), outs):
            self.terms.append((grid.send(out, **{axis: d}), left))


def send_rows(grid, units):
    rows, part = units[0].terms[0][0].shape[-2:]
    arrays = [t for u in units for t, _ in u.terms]

    def kernel(*refs):
        held, outs = iter(refs[: len(arrays)]), refs[len(arrays) :]
        place = grid.place()
        for i, unit in enumerate(units):
            terms = [(next(held), axes) for _, axes in unit.terms]
            for d, out in zip(grid.others("v"), outs):
                where = place | {"v": grid.step("v", place["v"], d)}
                value = total([t[Unit.entry(axes, where)] for t, axes in terms])
                out[:, i * part : (i + 1) * part] = value.astype(bf16)

    outs = [pltpu.VMEM((rows, part * len(units)), bf16) for _ in grid.others("v")]
    outs = call(kernel, "fold_v", arrays, outs) if outs else outs
    return [grid.send(t, v=d) for d, t in zip(grid.others("v"), outs)]


def project(grid, units, packs, ranks, sent):
    size = grid.size
    rows, part = units[0].terms[0][0].shape[-2:]
    each = ranks // grid.nodes
    group = part * len(units)
    arrays = [t for u in units for t, _ in u.terms]
    late = [i for i in range(len(units)) if i not in sent]
    n_sends = size["v"] - 1 if late else 0

    def kernel(*refs):
        held, refs = iter(refs[: len(arrays)]), refs[len(arrays) :]
        projs, refs = refs[: size["v"]], refs[size["v"] :]
        own, later, refs = refs[0], refs[1 : 1 + n_sends], refs[1 + n_sends :]
        outs, acc, sends = refs[: size["c"]], refs[size["c"]], refs[size["c"] + 1 :]
        sends = [own, *sends]
        place = grid.place()
        dims = (((0,), (0,)), ((), ()))
        for i, unit in enumerate(units):
            terms = [(next(held), axes) for _, axes in unit.terms]
            cols = slice(i * part, (i + 1) * part)
            for d in range(size["v"]):
                where = place | {"v": grid.step("v", place["v"], d)}
                value = total([t[Unit.entry(axes, where)] for t, axes in terms])
                sends[d][:, cols] = value.astype(bf16)
                if d and i in late:
                    j = late.index(i)
                    later[d - 1][:, j * part : (j + 1) * part] = value.astype(bf16)
        sums = [
            lax.dot_general(came[:rows], send[...], dims, preferred_element_type=f32)
            for came, send in zip(projs, sends)
        ]
        acc[...] = total(sums)
        for d, out in enumerate(outs):
            core = grid.step("c", place["c"], d)
            for e in range(size["x"]):
                for f in range(size["w"]):
                    there = {"c": core, "x": grid.step("x", place["x"], e)}
                    there["w"] = grid.step("w", place["w"], f)
                    for v in range(size["v"]):
                        start = pl.multiple_of(grid.node(there | {"v": v}) * each, each)
                        out[e, f, v * each : (v + 1) * each] = acc[pl.ds(start, each)]

    out = call(
        kernel,
        "project",
        arrays + packs,
        [pltpu.VMEM((rows, group), bf16)]
        + [pltpu.VMEM((rows, part * len(late)), bf16)] * n_sends
        + [pltpu.VMEM((size["x"], size["w"], size["v"] * each, group), f32)] * size["c"],
        [pltpu.VMEM((ranks, group), f32)] + [pltpu.VMEM((rows, group), bf16)] * (size["v"] - 1),
        limit=12,
    )
    return out[0], out[1 : 1 + n_sends], out[1 + n_sends :]


def add_cut(terms, name, run=1, flat=False):
    if flat:
        return add_flat(terms, name)
    count = terms[0].shape[0]

    def kernel(*refs):
        arrays, outs = refs[: len(terms)], refs[len(terms) :]
        for e, out in enumerate(outs):
            parts = [a[e] for a in arrays]
            runs = [total(parts[i : i + run]) for i in range(0, len(parts), run)]
            out[...] = total(runs).astype(out.dtype)

    return call(kernel, name, terms, [pltpu.VMEM(terms[0].shape[1:], bf16)] * count)


def add_flat(terms, name):
    pair, wide = terms[0].shape[:2]

    def kernel(*refs):
        arrays, outs = refs[: len(terms)], refs[len(terms) :]
        for k, out in enumerate(outs):
            out[...] = total([a[k // wide, k % wide] for a in arrays]).astype(out.dtype)

    outs = [pltpu.VMEM(terms[0].shape[2:], bf16)] * (pair * wide)
    return call(kernel, name, terms, outs)


def add_runs(terms, name, run):
    def kernel(*refs):
        *arrays, out = refs
        runs = [total([a[...] for a in arrays[i : i + run]]) for i in range(0, len(arrays), run)]
        out[...] = total(runs).astype(bf16)

    return call(kernel, name, terms, pltpu.VMEM(terms[0].shape, bf16))


def add(terms, name, dtype):
    def kernel(*refs):
        *arrays, out = refs
        out[...] = total([a[...] for a in arrays]).astype(dtype)

    return call(kernel, name, terms, pltpu.VMEM(terms[0].shape, dtype))


def pack(proj, moments):
    rows, ranks = proj.shape
    each, columns = moments[0].shape
    cuts = columns // ranks

    def kernel(proj, moment1, moment2, out):
        out[:rows] = proj[...].astype(bf16)
        both = jnp.concatenate([moment1[...], moment2[...]], 0).astype(bf16)
        for h in range(cuts):
            start = rows + h * 2 * each
            out[start : start + 2 * each] = both[:, h * ranks : (h + 1) * ranks]

    shape = (rows + cuts * 2 * each, ranks)
    return call(kernel, "pack", [proj, *moments], pltpu.VMEM(shape, bf16))


def normalize(grid, parts, packs, rows, first, columns, extra=()):
    ranks = packs[0].shape[1]
    group = parts[0].shape[1]
    each = ranks // grid.nodes
    cuts = columns // ranks
    rest = grid.size["v"]

    def kernel(*refs):
        v = grid.place()["v"]
        arrays, held, (sums, mine, scratch) = refs[:rest], refs[rest : 2 * rest], refs[2 * rest :]
        scratch[...] = total([a[...] for a in arrays]).reshape(scratch.shape)
        mine[...] = scratch[v]
        raw, tilde = 0.0, 0.0
        for d in range(rest):
            value = scratch[grid.step("v", v, d)]
            old = []
            for h in range(cuts):
                start = rows + h * 2 * each
                old.append(held[d][start : start + 2 * each].astype(f32))
            old = jnp.concatenate(old, 1)[:, first : first + group]
            m1 = 0.9 * old[:each] + 0.1 * value
            m2 = 0.999 * old[each:] + 0.001 * value * value
            ratio = m1 / bias_first / (jnp.sqrt(m2 / bias_second) + 1e-08)
            raw += jnp.sum(value * value, 0, keepdims=True)
            tilde += jnp.sum(ratio * ratio, 0, keepdims=True)
        sums[...] = jnp.concatenate([raw, tilde, jnp.zeros((6, group), f32)], 0)

    return call(
        kernel,
        "normalize",
        parts + packs,
        [pltpu.VMEM((8, group), f32), pltpu.VMEM((each, group), f32)],
        [pltpu.VMEM((rest, each, group), f32)],
        extra=extra,
    )


def update(weights, moments, grads, sums, mine, blocksize):
    rows, columns = weights.shape
    halved = KNOBS["ag"]["halves"] and rows % 256 == 0

    def kernel(weights, moment1, moment2, *refs):
        grad_refs, refs = refs[: len(grads)], refs[len(grads) :]
        sum_refs, refs = refs[: len(sums)], refs[len(sums) :]
        mine, new_out, new1, new2, packed, *halves = refs
        packed[rows:, :] = jnp.zeros((PAD, columns), bf16)
        lane = lax.broadcasted_iota(jnp.int32, (rows, 128), 1)
        scales = jnp.zeros((rows, 128), f32)
        added = total([s[...] for s in sum_refs])
        col_scale = jnp.sqrt(added[1:2]) / jnp.sqrt(added[0:1] + 1e-06)
        for k in range(columns // blocksize):
            cols = slice(k * blocksize, (k + 1) * blocksize)
            parts = []
            for ref, (_, blocks) in zip(grad_refs, grads):
                for lo, there, width in blocks:
                    if lo <= cols.start < lo + width:
                        start = there + cols.start - lo
                        parts.append(ref[:, start : start + blocksize])
            grad = total(parts)
            new = weights[:, cols] - 8.0 * grad * col_scale[:, cols]
            new_out[:, cols] = new
            scale = (jnp.max(jnp.abs(new), 1, keepdims=True) + 1e-06).astype(bf16).astype(f32)
            packed[:rows, cols] = (new / scale).astype(bf16)
            scales = jnp.where(lane == k, scale, scales)
        new1[...] = 0.9 * moment1[...] + 0.1 * mine[...]
        new2[...] = 0.999 * moment2[...] + 0.001 * mine[...] * mine[...]
        packed[rows:, :rows] = jnp.transpose(scales)[:PAD].astype(bf16)
        for i, half in enumerate(halves):
            half[...] = packed[i * rows // 2 : i * rows // 2 + half.shape[0]]

    return call(
        kernel,
        "update",
        [weights, *moments, *[g for g, _ in grads], *sums, mine],
        [
            jax.ShapeDtypeStruct((rows, columns), f32),
            jax.ShapeDtypeStruct(moments[0].shape, f32),
            jax.ShapeDtypeStruct(moments[0].shape, f32),
            pltpu.VMEM((rows + PAD, columns), bf16),
        ]
        + [pltpu.VMEM((rows // 2 + i * PAD, columns), bf16) for i in range(2) if halved],
    )


def lay(grid, held, nblocks, whole, *begun):
    shards = [t[0] for t in held]
    spans = [t[1:4] for t in held]
    steps = [t[4] for t in held]
    columns, count = shards[0].shape[1], len(shards)
    rows = max(lo + n for lo, n, _ in spans)

    def node_of(k):
        place = grid.place()
        return grid.node({a: grid.step(a, place[a], -steps[k].get(a, 0)) for a in "vwxc"})

    if rows % 128:
        places = jnp.stack([node_of(k) for k in range(count)])
        order = jnp.zeros(count, jnp.int32).at[places].set(jnp.arange(count, dtype=jnp.int32))
        stacked = jnp.take(jnp.stack(shards), order, axis=0)
        values = stacked[:, :rows].reshape(count * rows, columns)
        scales = jnp.moveaxis(stacked[:, rows : rows + nblocks, :rows], 0, 1)
        return values, scales.reshape(nblocks, count * rows)

    def kernel(*refs):
        held, (values, scales, sems) = refs[:count], refs[count + len(begun) :]
        copies = []
        for k, (lo, n, _) in enumerate(spans):
            start = pl.multiple_of(node_of(k) * rows + lo, 128)
            copies.append(
                pltpu.make_async_copy(
                    held[k].at[pl.ds(0, n)], values.at[pl.ds(start, n)], sems.at[k]
                )
            )
            copies[-1].start()
        for k, (lo, n, full) in enumerate(spans):
            if full:
                start = pl.multiple_of(node_of(k) * rows, 128)
                tail = held[k][n:, :rows].astype(f32)[:nblocks]
                scales[:, pl.ds(start, rows)] = tail.astype(bf16)
        for copy in copies:
            copy.wait()

    return pl.pallas_call(
        kernel,
        out_shape=[
            pltpu.HBM((whole * rows, columns), bf16),
            pltpu.VMEM((nblocks, whole * rows), bf16),
        ],
        in_specs=[pl.BlockSpec(memory_space=pltpu.VMEM)] * count
        + [pl.BlockSpec(memory_space=pl.ANY), pl.BlockSpec(memory_space=pltpu.VMEM)][: len(begun)],
        input_output_aliases={count + i: i for i in range(len(begun))},
        out_specs=[pl.BlockSpec(memory_space=pl.ANY), pl.BlockSpec(memory_space=pltpu.VMEM)],
        scratch_shapes=[pltpu.SemaphoreType.DMA((count,))],
        compiler_params=pltpu.CompilerParams(vmem_limit_bytes=8 * MIB),
        cost_estimate=pl.CostEstimate(
            flops=0, bytes_accessed=COST.get("lay", 1), transcendentals=0
        ),
        name="lay",
    )(*[vmem(s) for s in shards], *begun)


def shards(grad_values, grad_exponents, proj, weights, moment1, moment2):
    grid = Grid()
    size = grid.size
    values, exponents = grad_values[0], grad_exponents[0]
    width, columns = values.shape
    nblocks = exponents.shape[0]
    blocksize = columns // nblocks
    rows = width // grid.nodes // size["y"]
    ranks = proj.shape[1]
    parts = len(ORDERS)

    other = dequant(grid, values, exponents, 1, rows, blocksize, parts) if size["c"] > 1 else []
    other = [grid.send(t, c=1) for t in other]
    mine = dequant(grid, values, exponents, 0, rows, blocksize, parts)
    units = [Unit(grid, list(terms)) for terms in zip(mine, *([other] if other else []))]
    Turn.last = None
    received, sent, part = [], [], columns // parts
    for turn in PLAN:
        if turn == "touch":
            touch(*packs[1:])
        elif turn[0] == "t":
            touch(*[t for i in turn[1:] for t, _ in units[int(i)].terms[-1:]])
        elif turn[0] == "b":
            chosen = [int(i) for i in turn[1:]]
            blocks = [(i * part, k * part, part) for k, i in enumerate(chosen)]
            received += [(t, blocks) for t in send_rows(grid, [units[i] for i in chosen])]
            sent += chosen
        elif turn == "pack":
            packs = [pack(proj, [moment1, moment2])]
            packs += [grid.send(packs[0], v=-d) for d in grid.others("v")]
        else:
            units[int(turn[0])].hop(turn[1])

    own, sends, projected = project(grid, units, packs, ranks, sent)
    blocks = [(i * part, k * part, part) for k, i in enumerate(i for i in range(parts) if i not in sent)]
    if "bulk" not in KNOBS["late"]:
        received += [(grid.send(t, v=d), blocks) for d, t in zip(grid.others("v"), sends)]

    terms = [projected[0]] + [grid.send(projected[d], c=d) for d in grid.others("c")]
    by_x = add_cut(terms, "add_cores", flat=KNOBS["cube"])
    by_y = []
    for dy in range(size["y"]):
        for dx in range(size["x"]):
            for dw in range(size["w"] if KNOBS["cube"] else 1):
                piece = by_x[dx * size["w"] + dw] if KNOBS["cube"] else by_x[dx]
                by_y.append(grid.send(piece, x=dx, y=dy, w=dw) if dx or dy or dw else piece)
    if size["y"] > 2:
        stacked = jnp.stack(by_y).reshape((size["y"], -1) + by_y[0].shape)
        came = jnp.stack([grid.step("y", grid.place()["y"], -d) for d in range(size["y"])])
        order = jnp.zeros(size["y"], jnp.int32).at[came].set(jnp.arange(size["y"], dtype=jnp.int32))
        stacked = jnp.take(stacked, order, axis=0)
        by_y = [stacked[i, j] for i in range(size["y"]) for j in range(stacked.shape[1])]
    if KNOBS["cube"]:
        by_w = [add_runs(by_y, "add_chips", len(by_y) // size["y"])]
    else:
        by_w = add_cut(by_y, "add_chips", size["x"])
    if "bulk" in KNOBS["late"]:
        received += [(grid.send(tie(t, by_w[0]), v=d), blocks) for d, t in zip(grid.others("v"), sends)]
    summed = by_w[0]
    if not KNOBS["cube"]:
        received_w = [grid.send(by_w[d], w=d) for d in grid.others("w")]
        summed = add([by_w[0]] + received_w, "add_w", bf16)
    summed = [summed] + [grid.send(summed, v=d) for d in grid.others("v")]
    extra = [t for t, _ in received] if KNOBS["early"] else []
    added, kept = normalize(grid, summed, packs, rows, 0, columns, extra)
    if KNOBS["sums"] == 0:
        sums = [added] + [
            grid.send(added, x=dx, w=dw)
            for dx in range(size["x"])
            for dw in range(size["w"])
            if dx or dw
        ]
        added = add(sums, "add_sums", f32)
        sums = [added] + [grid.send(added, c=d) for d in grid.others("c")]
    else:
        added = add([added] + [grid.send(added, c=d) for d in grid.others("c")], "add_sums", f32)
        sums = [added] + [
            grid.send(added, x=dx, w=dw)
            for dx in range(size["x"])
            for dw in range(size["w"])
            if dx or dw
        ]
    new, new1, new2, *packed = update(
        weights, [moment1, moment2], [(own, [(0, 0, columns)]), *received], sums, kept, blocksize
    )

    ag = KNOBS["ag"]
    whole = (packed[0], 0, rows, True)
    halves = [whole]
    if len(packed) > 1:
        halves = [(packed[1], 0, rows // 2, False), (packed[2], rows // 2, rows // 2, True)]

    def sent(shards, **step):
        return [(grid.send(t, **step), *rest) for t, *rest in shards]

    def tied(shards, *others):
        return [(tie(t, *others), *rest) for t, *rest in shards]

    first = {d: sent(halves, v=d) if d else [whole] for d in range(size["v"])}
    stages = [[(0, d) for d in range(size["w"])]]
    stages += [[(d, 0) for d in grid.others("v")]]
    stages += [[(d, e) for d in grid.others("v") for e in grid.others("w")]]
    came = {(d, e): sent(first[d], w=e) if e else first[d] for s in stages for d, e in s}
    done, count, over = [], grid.nodes, []
    for k, stage in enumerate(stages):
        held = []
        for dv, dw in stage:
            shards = came[dv, dw]
            if (k, 0) in TIES and done:
                shards = tied(shards, done[-1][1])
            if (k, 1) in TIES and len(done) > 1:
                shards = tied(shards, done[-2][1])
            if (k, 2) in TIES and over:
                shards = tied(shards, over[-1])
            for dx in range(size["x"]):
                moved = sent(shards, x=dx) if dx else shards
                if dx:
                    over.append(moved[-1][0])
                    if (k, 3) in TIES and done:
                        moved = tied(moved, done[-1][1])
                for dc in range(size["c"]):
                    there = {"v": dv, "w": dw, "x": dx, "c": dc}
                    held += [(*t, there) for t in (sent(moved, c=dc) if dc else moved)]
        done.append(held)
        if (ag["lays"] == 1 or rows % 128) and k < len(stages) - 1:
            continue
        if ag["lays"] == 2 and k == 0:
            continue
        held = [t for h in done if isinstance(h, list) for t in h]
        if not held:
            continue
        begun = [h for h in done if not isinstance(h, list)][-1:]
        result = lay(grid, held, nblocks, count, *(begun[0] if begun else ()))
        done = [h for h in done if not isinstance(h, list)] + [result]
    quant, scales = done[-1]
    return quant, scales, new, new1, new2


def solution(mesh):
    return jax.shard_map(
        shards,
        mesh=mesh,
        in_specs=(
            P(("node", "local"), None, None),
            P(("node", "local"), None, None),
            P(("local", "node"), None),
            P(("local", "node"), None),
            P("node", None),
            P("node", None),
        ),
        out_specs=(
            P("local", None),
            P(None, "local"),
            P(("local", "node"), None),
            P("node", None),
            P("node", None),
        ),
        check_vma=False,
    )
```

time: 431 us -> 119 us (0.28)
  waiting for transfers between devices: 284 us -> 48 us
  blocking collectives: 64.9 us -> 0 us
  starting transfers between devices: 0.16 us -> 55.3 us
  local copies, waits for them, and re-layouts: 46.2 us -> 1.54 us
  other arithmetic: 17.9 us -> 0 us
  Pallas kernels: 0 us -> 13.4 us
  between operations: 13.9 us -> 0.86 us
    reduce_scatter x3 -> x0, waiting for transfers between devices: 258 us -> none  [the longest x1 181 us: shards(): lax.psum_scatter(dequant.reshape(local_count, width // local_count, colum...]
    ppermute x0 -> x43, starting transfers between devices: none -> 55.3 us  [send(): return lax.ppermute(array, AXES, pairs)]
    ppermute x0 -> x43, waiting for transfers between devices: none -> 48 us  [send(): return lax.ppermute(array, AXES, pairs)]
    psum x2 -> x0, blocking collectives: 40.4 us -> none  [the longest x1 33.4 us: shards(): lax.psum((jnp.sum(owned_proj * owned_proj, 0), jnp.sum(tilde * tilde, 0))...]
    mul x2 -> x0, local copies, waits for them, and re-layouts: 36.5 us -> none  [shards(): mantissa.reshape(width, nblocks, blocksize) * factor[:, :, None]]
    all_gather x1 -> x0, waiting for transfers between devices: 26.9 us -> none  [shards(): lax.all_gather(values, 'node', axis=0, tiled=True)]
    all_gather x1 -> x0, blocking collectives: 24.6 us -> none  [shards(): lax.all_gather(jnp.transpose(block_max), 'node', axis=1, tiled=True)]
    mul x2 -> x0, other arithmetic: 13.9 us -> none  [the longest x1 13.9 us: shards(): mantissa.reshape(width, nblocks, blocksize) * factor[:, :, None]]
  transfers between devices with their start and end apart: 4 -> 43, of which waited for: 4 -> 18; matrix products, arithmetic and copies ran while one was open for 0% -> 0% of each run, Pallas kernels for 0% -> 6%
where the time goes in v2:
time: 119 us
  starting transfers between devices  55.3 us (46%)
  waiting for transfers between devices  48 us (40%)
  Pallas kernels  13.4 us (11%)
  local copies, waits for them, and re-layouts  1.54 us (1%)
    ppermute x43, starting transfers between devices, send(): return lax.ppermute(array, AXES, pairs)  55.3 us
    ppermute x43, waiting for transfers between devices, send(): return lax.ppermute(array, AXES, pairs)  48 us
    pallas_call x2, Pallas kernels, dequant(): pl.pallas_call(kernel, out_shape=[pltpu.VMEM(shape, bf16)] * parts, in_sp...  7.49 us
    pallas_call x20, Pallas kernels, call(): pl.pallas_call(body, out_shape=outs, in_specs=[pl.BlockSpec(memory_space=...  3.15 us
    pallas_call x2, Pallas kernels, lay(): pl.pallas_call(kernel, out_shape=[pltpu.HBM((whole * rows, columns), bf16...  2.81 us
  transfers between devices with their start and end apart: 43, of which 18 were waited for; matrix products, arithmetic and copies ran while one was open for 0% of the time, Pallas kernels for 6%

profile of v2, /device:TPU:1, one launch (start us, length us, event | category | flops | bytes accessed | tf_op | source)
XLA Modules:
  0.0 119.2 jit_solution(8388473570689603611)
XLA Ops:
  1.5 3.7 %dequant.3 = (bf16[2,2,2,2,256,128]{5,4,3,2,1,0:T(8,128)(2,1)S(1)}, bf16[2,2,2,2,256,128]{5,4,3,2,1,0:T(8,128)(2,1)S(1)}, bf16[2,2,2,2,256,128]{5,4,3,2,1,0:T(8,...) custom-call(s32[4,8192]{1,0:T(4,128)S(1)} %bitcast.2, bf16[2,4,2,2,256,512]{5,4,3,2,1,0:T(8,128)(2,1)} %bitcast.4), custom_call_target="tpu_custom_call" | custom-call | bytes 1 | tf_op jit(solution)/shard_map/dequant/pallas_call | solution.py:183
  6.4 3.7 %dequant.2 = (bf16[2,2,2,2,256,128]{5,4,3,2,1,0:T(8,128)(2,1)S(1)}, bf16[2,2,2,2,256,128]{5,4,3,2,1,0:T(8,128)(2,1)S(1)}, bf16[2,2,2,2,256,128]{5,4,3,2,1,0:T(8,...) custom-call(s32[4,8192]{1,0:T(4,128)S(1)} %bitcast.3, bf16[2,4,2,2,256,512]{5,4,3,2,1,0:T(8,128)(2,1)} %bitcast.5), custom_call_target="tpu_custom_call" | custom-call | bytes 1 | tf_op jit(solution)/shard_map/dequant/pallas_call | solution.py:183
  10.3 2.4 %collective-permute-start.13 = (bf16[2,2,2,256,128]{4,3,2,1,0:T(8,128)(2,1)S(1)}, bf16[2,2,2,256,128]{4,3,2,1,0:T(8,128)(2,1)S(1)}, u32[]{:S(2)}, u32[]{:S(2)}) collective-permute-start(bf16[2,2,2,256,128]{4,3,2,1,0:T(8,128)(2,1)S(1)} %fold_x.7), channel_id=1, source_target_pairs={{0,4},{1,5},{2,6},{3,7},{4,0},{5,1},{6,2},{7,3},{8,12},{9,13},{10,... | collective-permute-start | bytes 1572872 | tf_op jit(solution)/shard_map/ppermute | solution.py:85
  12.8 1.4 %collective-permute-start.9 = (bf16[2,2,2,256,128]{4,3,2,1,0:T(8,128)(2,1)S(1)}, bf16[2,2,2,256,128]{4,3,2,1,0:T(8,128)(2,1)S(1)}, u32[]{:S(2)}, u32[]{:S(2)}) collective-permute-start(bf16[2,2,2,256,128]{4,3,2,1,0:T(8,128)(2,1)S(1)} %fold_w.6), channel_id=1, source_target_pairs={{0,8},{1,9},{2,10},{3,11},{4,12},{5,13},{6,14},{7,15},{8,0},{9,1},... | collective-permute-start | bytes 1572872 | tf_op jit(solution)/shard_map/ppermute | solution.py:85
  14.3 1.3 %collective-permute-start.5 = (bf16[2,2,2,256,128]{4,3,2,1,0:T(8,128)(2,1)S(1)}, bf16[2,2,2,256,128]{4,3,2,1,0:T(8,128)(2,1)S(1)}, u32[]{:S(2)}, u32[]{:S(2)}) collective-permute-start(bf16[2,2,2,256,128]{4,3,2,1,0:T(8,128)(2,1)S(1)} %fold_y.5), channel_id=1, source_target_pairs={{0,1},{1,0},{2,3},{3,2},{4,5},{5,4},{6,7},{7,6},{8,9},{9,8},{10,11... | collective-permute-start | bytes 1572872 | tf_op jit(solution)/shard_map/ppermute | solution.py:85
  16.0 8.6 %collective-permute-done.13.refs_2_.refs_17_ = bf16[2,2,2,256,128]{4,3,2,1,0:T(8,128)(2,1)S(1)} collective-permute-done((bf16[2,2,2,256,128]{4,3,2,1,0:T(8,128)(2,1)S(1)}, bf16[2,2,2,256,128]{4,3,2,1,0:T(8,128)(2,1)S(1)}, u32[]{:S(2)}, u32[]{:S(2)}) %collective-permute-start.13) | collective-permute-done | bytes 524320 | tf_op jit(solution)/shard_map/ppermute | solution.py:85
  26.0 1.3 %collective-permute-start.10 = (bf16[2,2,256,128]{3,2,1,0:T(8,128)(2,1)S(1)}, bf16[2,2,256,128]{3,2,1,0:T(8,128)(2,1)S(1)}, u32[]{:S(2)}, u32[]{:S(2)}) collective-permute-start(bf16[2,2,256,128]{3,2,1,0:T(8,128)(2,1)S(1)} %fold_x.6), channel_id=1, source_target_pairs={{0,4},{1,5},{2,6},{3,7},{4,0},{5,1},{6,2},{7,3},{8,12},{9,13},{10,... | collective-permute-start | bytes 786440 | tf_op jit(solution)/shard_map/ppermute | solution.py:85
  27.4 1.4 %collective-permute-start.6 = (bf16[2,2,256,128]{3,2,1,0:T(8,128)(2,1)S(1)}, bf16[2,2,256,128]{3,2,1,0:T(8,128)(2,1)S(1)}, u32[]{:S(2)}, u32[]{:S(2)}) collective-permute-start(bf16[2,2,256,128]{3,2,1,0:T(8,128)(2,1)S(1)} %fold_w.5), channel_id=1, source_target_pairs={{0,8},{1,9},{2,10},{3,11},{4,12},{5,13},{6,14},{7,15},{8,0},{9,1},... | collective-permute-start | bytes 786440 | tf_op jit(solution)/shard_map/ppermute | solution.py:85
  28.8 7.0 %collective-permute-done.1.refs_2_ = bf16[2,2,2,256,128]{4,3,2,1,0:T(8,128)(2,1)S(1)} collective-permute-done((bf16[2,2,2,256,128]{4,3,2,1,0:T(8,128)(2,1)S(1)}, bf16[2,2,2,256,128]{4,3,2,1,0:T(8,128)(2,1)S(1)}, u32[]{:S(2)}, u32[]{:S(2)}) %collective-permute-start.1) | collective-permute-done | bytes 524320 | tf_op jit(solution)/shard_map/ppermute | solution.py:85
  37.2 2.4 %collective-permute-start.16 = (bf16[320,256]{1,0:T(8,128)(2,1)S(1)}, bf16[320,256]{1,0:T(8,128)(2,1)S(1)}, u32[]{:S(2)}, u32[]{:S(2)}) collective-permute-start(bf16[320,256]{1,0:T(8,128)(2,1)S(1)} %pack.1.refs_20_.refs_2_), channel_id=1, source_target_pairs={{0,16},{1,17},{2,18},{3,19},{4,20},{5,21},{6,22},{7,23},{8,24},{9,... | collective-permute-start | bytes 491528 | tf_op jit(solution)/shard_map/ppermute | solution.py:85
  39.6 1.4 %collective-permute-start.15 = (bf16[2,256,128]{2,1,0:T(8,128)(2,1)S(1)}, bf16[2,256,128]{2,1,0:T(8,128)(2,1)S(1)}, u32[]{:S(2)}, u32[]{:S(2)}) collective-permute-start(bf16[2,256,128]{2,1,0:T(8,128)(2,1)S(1)} %fold_w.7), channel_id=1, source_target_pairs={{0,8},{1,9},{2,10},{3,11},{4,12},{5,13},{6,14},{7,15},{8,0},{9,1},... | collective-permute-start | bytes 393224 | tf_op jit(solution)/shard_map/ppermute | solution.py:85
  44.2 1.4 %collective-permute-start.3 = (bf16[2,256,128]{2,1,0:T(8,128)(2,1)S(1)}, bf16[2,256,128]{2,1,0:T(8,128)(2,1)S(1)}, u32[]{:S(2)}, u32[]{:S(2)}) collective-permute-start(bf16[2,256,128]{2,1,0:T(8,128)(2,1)S(1)} %fold_w.4), channel_id=1, source_target_pairs={{0,8},{1,9},{2,10},{3,11},{4,12},{5,13},{6,14},{7,15},{8,0},{9,1},... | collective-permute-start | bytes 393224 | tf_op jit(solution)/shard_map/ppermute | solution.py:85
  45.7 1.3 %collective-permute-done.7.refs_9_ = bf16[2,256,128]{2,1,0:T(8,128)(2,1)S(1)} collective-permute-done((bf16[2,256,128]{2,1,0:T(8,128)(2,1)S(1)}, bf16[2,256,128]{2,1,0:T(8,128)(2,1)S(1)}, u32[]{:S(2)}, u32[]{:S(2)}) %collective-permute-start.7) | collective-permute-done | bytes 131104 | tf_op jit(solution)/shard_map/ppermute | solution.py:85
  47.0 2.3 %collective-permute-done.3.refs_4_ = bf16[2,256,128]{2,1,0:T(8,128)(2,1)S(1)} collective-permute-done((bf16[2,256,128]{2,1,0:T(8,128)(2,1)S(1)}, bf16[2,256,128]{2,1,0:T(8,128)(2,1)S(1)}, u32[]{:S(2)}, u32[]{:S(2)}) %collective-permute-start.3) | collective-permute-done | bytes 131104 | tf_op jit(solution)/shard_map/ppermute | solution.py:85
  50.1 2.1 %collective-permute-start.18 = (f32[2,2,32,512]{3,2,1,0:T(8,128)S(1)}, f32[2,2,32,512]{3,2,1,0:T(8,128)S(1)}, u32[]{:S(2)}, u32[]{:S(2)}) collective-permute-start(f32[2,2,32,512]{3,2,1,0:T(8,128)S(1)} %get-tuple-element.42), channel_id=1, source_target_pairs={{0,2},{1,3},{2,0},{3,1},{4,6},{5,7},{6,4},{7,5},{8,10},{9,11},{10,... | collective-permute-start | bytes 786440 | tf_op jit(solution)/shard_map/ppermute | solution.py:85
  52.2 2.0 %collective-permute-start.17 = (bf16[256,512]{1,0:T(8,128)(2,1)S(1)}, bf16[256,512]{1,0:T(8,128)(2,1)S(1)}, u32[]{:S(2)}, u32[]{:S(2)}) collective-permute-start(bf16[256,512]{1,0:T(8,128)(2,1)S(1)} %get-tuple-element.40), channel_id=1, source_target_pairs={{0,16},{1,17},{2,18},{3,19},{4,20},{5,21},{6,22},{7,23},{8,24},{9,... | collective-permute-start | bytes 786440 | tf_op jit(solution)/shard_map/ppermute | solution.py:85
  57.7 1.3 %collective-permute-done.21.refs_3_ = bf16[2,32,512]{2,1,0:T(8,128)(2,1)S(1)} collective-permute-done((bf16[2,32,512]{2,1,0:T(8,128)(2,1)S(1)}, bf16[2,32,512]{2,1,0:T(8,128)(2,1)S(1)}, u32[]{:S(2)}, u32[]{:S(2)}) %collective-permute-start.21) | collective-permute-done | bytes 65568 | tf_op jit(solution)/shard_map/ppermute | solution.py:85
  59.9 2.1 %collective-permute-start.22 = (bf16[32,512]{1,0:T(8,128)(2,1)S(1)}, bf16[32,512]{1,0:T(8,128)(2,1)S(1)}, u32[]{:S(2)}, u32[]{:S(2)}) collective-permute-start(bf16[32,512]{1,0:T(8,128)(2,1)S(1)} %get-tuple-element.46), channel_id=1, source_target_pairs={{0,8},{1,9},{2,10},{3,11},{4,12},{5,13},{6,14},{7,15},{8,0},{9,1},... | collective-permute-start | bytes 98312 | tf_op jit(solution)/shard_map/ppermute | solution.py:85
  62.0 5.6 %collective-permute-done.22.refs_1_ = bf16[32,512]{1,0:T(8,128)(2,1)S(1)} collective-permute-done((bf16[32,512]{1,0:T(8,128)(2,1)S(1)}, bf16[32,512]{1,0:T(8,128)(2,1)S(1)}, u32[]{:S(2)}, u32[]{:S(2)}) %collective-permute-start.22) | collective-permute-done | bytes 32800 | tf_op jit(solution)/shard_map/ppermute | solution.py:85
  68.5 2.9 %collective-permute-done.23.refs_1_ = bf16[32,512]{1,0:T(8,128)(2,1)S(1)} collective-permute-done((bf16[32,512]{1,0:T(8,128)(2,1)S(1)}, bf16[32,512]{1,0:T(8,128)(2,1)S(1)}, u32[]{:S(2)}, u32[]{:S(2)}) %collective-permute-start.23) | collective-permute-done | bytes 32800 | tf_op jit(solution)/shard_map/ppermute | solution.py:85
  71.5 2.1 %collective-permute-start.24 = (f32[8,512]{1,0:T(8,128)S(1)}, f32[8,512]{1,0:T(8,128)S(1)}, u32[]{:S(2)}, u32[]{:S(2)}) collective-permute-start(f32[8,512]{1,0:T(8,128)S(1)} %get-tuple-element.47.refs_0_), channel_id=1, source_target_pairs={{0,2},{1,3},{2,0},{3,1},{4,6},{5,7},{6,4},{7,5},{8,10},{9,11},{10,... | collective-permute-start | bytes 49160 | tf_op jit(solution)/shard_map/ppermute | solution.py:85
  74.5 1.3 %collective-permute-start.26 = (f32[8,512]{1,0:T(8,128)S(1)}, f32[8,512]{1,0:T(8,128)S(1)}, u32[]{:S(2)}, u32[]{:S(2)}) collective-permute-start(f32[8,512]{1,0:T(8,128)S(1)} %add_sums.1.refs_5_), channel_id=1, source_target_pairs={{0,4},{1,5},{2,6},{3,7},{4,0},{5,1},{6,2},{7,3},{8,12},{9,13},{10,... | collective-permute-start | bytes 49160 | tf_op jit(solution)/shard_map/ppermute | solution.py:85
  79.8 2.4 %collective-permute-start.28 = (bf16[272,512]{1,0:T(8,128)(2,1)S(1)}, bf16[272,512]{1,0:T(8,128)(2,1)S(1)}, u32[]{:S(2)}, u32[]{:S(2)}) collective-permute-start(bf16[272,512]{1,0:T(8,128)(2,1)S(1)} %get-tuple-element.49.refs_0_), channel_id=1, source_target_pairs={{0,16},{1,17},{2,18},{3,19},{4,20},{5,21},{6,22},{7,23},{8,24},{9,... | collective-permute-start | bytes 835592 | tf_op jit(solution)/shard_map/ppermute | solution.py:85
  82.6 2.4 %collective-permute-start.33 = (bf16[272,512]{1,0:T(8,128)(2,1)S(1)}, bf16[272,512]{1,0:T(8,128)(2,1)S(1)}, u32[]{:S(2)}, u32[]{:S(2)}) collective-permute-start(bf16[272,512]{1,0:T(8,128)(2,1)S(1)} %get-tuple-element.49.refs_0_), channel_id=1, source_target_pairs={{0,2},{1,3},{2,0},{3,1},{4,6},{5,7},{6,4},{7,5},{8,10},{9,11},{10,... | collective-permute-start | bytes 835592 | tf_op jit(solution)/shard_map/ppermute | solution.py:85
  85.0 9.7 %collective-permute-done.28.refs_8_ = bf16[272,512]{1,0:T(8,128)(2,1)S(1)} collective-permute-done((bf16[272,512]{1,0:T(8,128)(2,1)S(1)}, bf16[272,512]{1,0:T(8,128)(2,1)S(1)}, u32[]{:S(2)}, u32[]{:S(2)}) %collective-permute-start.28) | collective-permute-done | bytes 278560 | tf_op jit(solution)/shard_map/ppermute | solution.py:85
  94.7 1.9 %collective-permute-start.37 = (bf16[272,512]{1,0:T(8,128)(2,1)S(1)}, bf16[272,512]{1,0:T(8,128)(2,1)S(1)}, u32[]{:S(2)}, u32[]{:S(2)}) collective-permute-start(bf16[272,512]{1,0:T(8,128)(2,1)S(1)} %collective-permute-done.36.refs_4_), channel_id=1, source_target_pairs={{0,2},{1,3},{2,0},{3,1},{4,6},{5,7},{6,4},{7,5},{8,10},{9,11},{10,... | collective-permute-start | bytes 835592 | tf_op jit(solution)/shard_map/ppermute | solution.py:85
  96.6 1.7 %collective-permute-start.41 = (bf16[272,512]{1,0:T(8,128)(2,1)S(1)}, bf16[272,512]{1,0:T(8,128)(2,1)S(1)}, u32[]{:S(2)}, u32[]{:S(2)}) collective-permute-start(bf16[272,512]{1,0:T(8,128)(2,1)S(1)} %collective-permute-done.28.refs_8_), channel_id=1, source_target_pairs={{0,4},{1,5},{2,6},{3,7},{4,0},{5,1},{6,2},{7,3},{8,12},{9,13},{10,... | collective-permute-start | bytes 835592 | tf_op jit(solution)/shard_map/ppermute | solution.py:85
  98.6 3.0 %collective-permute-done.29.refs_0_ = bf16[272,512]{1,0:T(8,128)(2,1)S(1)} collective-permute-done((bf16[272,512]{1,0:T(8,128)(2,1)S(1)}, bf16[272,512]{1,0:T(8,128)(2,1)S(1)}, u32[]{:S(2)}, u32[]{:S(2)}) %collective-permute-start.29) | collective-permute-done | bytes 278560 | tf_op jit(solution)/shard_map/ppermute | solution.py:85
  101.6 4.5 %collective-permute-start.40 = (bf16[272,512]{1,0:T(8,128)(2,1)S(1)}, bf16[272,512]{1,0:T(8,128)(2,1)S(1)}, u32[]{:S(2)}, u32[]{:S(2)}) collective-permute-start(bf16[272,512]{1,0:T(8,128)(2,1)S(1)} %collective-permute-done.28.refs_8_), channel_id=1, source_target_pairs={{0,2},{1,3},{2,0},{3,1},{4,6},{5,7},{6,4},{7,5},{8,10},{9,11},{10,... | collective-permute-start | bytes 835592 | tf_op jit(solution)/shard_map/ppermute | solution.py:85
  106.9 5.2 %collective-permute-start.42 = (bf16[272,512]{1,0:T(8,128)(2,1)S(1)}, bf16[272,512]{1,0:T(8,128)(2,1)S(1)}, u32[]{:S(2)}, u32[]{:S(2)}) collective-permute-start(bf16[272,512]{1,0:T(8,128)(2,1)S(1)} %collective-permute-done.41.refs_10_), channel_id=1, source_target_pairs={{0,2},{1,3},{2,0},{3,1},{4,6},{5,7},{6,4},{7,5},{8,10},{9,11},{10,... | collective-permute-start | bytes 835592 | tf_op jit(solution)/shard_map/ppermute | solution.py:85
  112.9 2.8 %collective-permute-start.32 = (bf16[272,512]{1,0:T(8,128)(2,1)S(1)}, bf16[272,512]{1,0:T(8,128)(2,1)S(1)}, u32[]{:S(2)}, u32[]{:S(2)}) collective-permute-start(bf16[272,512]{1,0:T(8,128)(2,1)S(1)} %collective-permute-done.31.refs_2_), channel_id=1, source_target_pairs={{0,2},{1,3},{2,0},{3,1},{4,6},{5,7},{6,4},{7,5},{8,10},{9,11},{10,... | collective-permute-start | bytes 835592 | tf_op jit(solution)/shard_map/ppermute | solution.py:85
  115.7 1.8 %lay.2 = (bf16[4096,512]{1,0:T(8,128)(2,1)}, bf16[4,4096]{1,0:T(4,128)(2,1)S(1)}) custom-call(bf16[272,512]{1,0:T(8,128)(2,1)S(1)} %get-tuple-element.49.refs_0_, bf16[272,512]{1,0:T(8,128)(2,1)S(1)} %collective-permute-done.33.refs_1_, bf16[272,512]{1,0:T(8,128)(2,1)S(1)} %collective-permute-done.34.refs_2_, ...), custom_call_target="tpu_custom_call" | custom-call | bytes 1 | tf_op jit(solution)/shard_map/lay/pallas_call | solution.py:488
  (89 shorter events, 24.1 us)
Async XLA Ops:
  5.3 4.8 %collective-permute-start.12 = (bf16[2,2,2,2,256,128]{5,4,3,2,1,0:T(8,128)(2,1)S(1)}, bf16[2,2,2,2,256,128]{5,4,3,2,1,0:T(8,128)(2,1)S(1)}, u32[]{:S(2)}, u32[]{:S(2)}) collective-permute-start(bf16[2,2,2,2,256,128]{5,4,3,2,1,0:T(8,128)(2,1)S(1)} %get-tuple-element.38), channel_id=1, source_target_pairs={{0,2},{1,3},{2,0},{3,1},{4,6},{5,7},{6,4},{7,5},{8,10},{9,11},{10,... | collective-permute-start | bytes 3145736 | tf_op jit(solution)/shard_map/ppermute | solution.py:85
  5.4 7.2 %collective-permute-start.8 = (bf16[2,2,2,2,256,128]{5,4,3,2,1,0:T(8,128)(2,1)S(1)}, bf16[2,2,2,2,256,128]{5,4,3,2,1,0:T(8,128)(2,1)S(1)}, u32[]{:S(2)}, u32[]{:S(2)}) collective-permute-start(bf16[2,2,2,2,256,128]{5,4,3,2,1,0:T(8,128)(2,1)S(1)} %get-tuple-element.36), channel_id=1, source_target_pairs={{0,2},{1,3},{2,0},{3,1},{4,6},{5,7},{6,4},{7,5},{8,10},{9,11},{10,... | collective-permute-start | bytes 3145736 | tf_op jit(solution)/shard_map/ppermute | solution.py:85
  5.9 8.3 %collective-permute-start.4 = (bf16[2,2,2,2,256,128]{5,4,3,2,1,0:T(8,128)(2,1)S(1)}, bf16[2,2,2,2,256,128]{5,4,3,2,1,0:T(8,128)(2,1)S(1)}, u32[]{:S(2)}, u32[]{:S(2)}) collective-permute-start(bf16[2,2,2,2,256,128]{5,4,3,2,1,0:T(8,128)(2,1)S(1)} %get-tuple-element.34), channel_id=1, source_target_pairs={{0,2},{1,3},{2,0},{3,1},{4,6},{5,7},{6,4},{7,5},{8,10},{9,11},{10,... | collective-permute-start | bytes 3145736 | tf_op jit(solution)/shard_map/ppermute | solution.py:85
  5.9 9.6 %collective-permute-start = (bf16[2,2,2,2,256,128]{5,4,3,2,1,0:T(8,128)(2,1)S(1)}, bf16[2,2,2,2,256,128]{5,4,3,2,1,0:T(8,128)(2,1)S(1)}, u32[]{:S(2)}, u32[]{:S(2)}) collective-permute-start(bf16[2,2,2,2,256,128]{5,4,3,2,1,0:T(8,128)(2,1)S(1)} %get-tuple-element.32), channel_id=1, source_target_pairs={{0,2},{1,3},{2,0},{3,1},{4,6},{5,7},{6,4},{7,5},{8,10},{9,11},{10,... | collective-permute-start | bytes 3145736 | tf_op jit(solution)/shard_map/ppermute | solution.py:85
  10.3 14.3 %collective-permute-start.13 = (bf16[2,2,2,256,128]{4,3,2,1,0:T(8,128)(2,1)S(1)}, bf16[2,2,2,256,128]{4,3,2,1,0:T(8,128)(2,1)S(1)}, u32[]{:S(2)}, u32[]{:S(2)}) collective-permute-start(bf16[2,2,2,256,128]{4,3,2,1,0:T(8,128)(2,1)S(1)} %fold_x.7), channel_id=1, source_target_pairs={{0,4},{1,5},{2,6},{3,7},{4,0},{5,1},{6,2},{7,3},{8,12},{9,13},{10,... | collective-permute-start | bytes 1572872 | tf_op jit(solution)/shard_map/ppermute | solution.py:85
  12.8 13.2 %collective-permute-start.9 = (bf16[2,2,2,256,128]{4,3,2,1,0:T(8,128)(2,1)S(1)}, bf16[2,2,2,256,128]{4,3,2,1,0:T(8,128)(2,1)S(1)}, u32[]{:S(2)}, u32[]{:S(2)}) collective-permute-start(bf16[2,2,2,256,128]{4,3,2,1,0:T(8,128)(2,1)S(1)} %fold_w.6), channel_id=1, source_target_pairs={{0,8},{1,9},{2,10},{3,11},{4,12},{5,13},{6,14},{7,15},{8,0},{9,1},... | collective-permute-start | bytes 1572872 | tf_op jit(solution)/shard_map/ppermute | solution.py:85
  14.3 13.1 %collective-permute-start.5 = (bf16[2,2,2,256,128]{4,3,2,1,0:T(8,128)(2,1)S(1)}, bf16[2,2,2,256,128]{4,3,2,1,0:T(8,128)(2,1)S(1)}, u32[]{:S(2)}, u32[]{:S(2)}) collective-permute-start(bf16[2,2,2,256,128]{4,3,2,1,0:T(8,128)(2,1)S(1)} %fold_y.5), channel_id=1, source_target_pairs={{0,1},{1,0},{2,3},{3,2},{4,5},{5,4},{6,7},{7,6},{8,9},{9,8},{10,11... | collective-permute-start | bytes 1572872 | tf_op jit(solution)/shard_map/ppermute | solution.py:85
  15.7 20.1 %collective-permute-start.1 = (bf16[2,2,2,256,128]{4,3,2,1,0:T(8,128)(2,1)S(1)}, bf16[2,2,2,256,128]{4,3,2,1,0:T(8,128)(2,1)S(1)}, u32[]{:S(2)}, u32[]{:S(2)}) collective-permute-start(bf16[2,2,2,256,128]{4,3,2,1,0:T(8,128)(2,1)S(1)} %fold_x.4), channel_id=1, source_target_pairs={{0,4},{1,5},{2,6},{3,7},{4,0},{5,1},{6,2},{7,3},{8,12},{9,13},{10,... | collective-permute-start | bytes 1572872 | tf_op jit(solution)/shard_map/ppermute | solution.py:85
  24.7 14.8 %collective-permute-start.14 = (bf16[2,2,256,128]{3,2,1,0:T(8,128)(2,1)S(1)}, bf16[2,2,256,128]{3,2,1,0:T(8,128)(2,1)S(1)}, u32[]{:S(2)}, u32[]{:S(2)}) collective-permute-start(bf16[2,2,256,128]{3,2,1,0:T(8,128)(2,1)S(1)} %fold_y.7), channel_id=1, source_target_pairs={{0,1},{1,0},{2,3},{3,2},{4,5},{5,4},{6,7},{7,6},{8,9},{9,8},{10,11... | collective-permute-start | bytes 786440 | tf_op jit(solution)/shard_map/ppermute | solution.py:85
  26.0 15.4 %collective-permute-start.10 = (bf16[2,2,256,128]{3,2,1,0:T(8,128)(2,1)S(1)}, bf16[2,2,256,128]{3,2,1,0:T(8,128)(2,1)S(1)}, u32[]{:S(2)}, u32[]{:S(2)}) collective-permute-start(bf16[2,2,256,128]{3,2,1,0:T(8,128)(2,1)S(1)} %fold_x.6), channel_id=1, source_target_pairs={{0,4},{1,5},{2,6},{3,7},{4,0},{5,1},{6,2},{7,3},{8,12},{9,13},{10,... | collective-permute-start | bytes 786440 | tf_op jit(solution)/shard_map/ppermute | solution.py:85
  27.4 15.3 %collective-permute-start.6 = (bf16[2,2,256,128]{3,2,1,0:T(8,128)(2,1)S(1)}, bf16[2,2,256,128]{3,2,1,0:T(8,128)(2,1)S(1)}, u32[]{:S(2)}, u32[]{:S(2)}) collective-permute-start(bf16[2,2,256,128]{3,2,1,0:T(8,128)(2,1)S(1)} %fold_w.5), channel_id=1, source_target_pairs={{0,8},{1,9},{2,10},{3,11},{4,12},{5,13},{6,14},{7,15},{8,0},{9,1},... | collective-permute-start | bytes 786440 | tf_op jit(solution)/shard_map/ppermute | solution.py:85
  35.9 8.2 %collective-permute-start.2 = (bf16[2,2,256,128]{3,2,1,0:T(8,128)(2,1)S(1)}, bf16[2,2,256,128]{3,2,1,0:T(8,128)(2,1)S(1)}, u32[]{:S(2)}, u32[]{:S(2)}) collective-permute-start(bf16[2,2,256,128]{3,2,1,0:T(8,128)(2,1)S(1)} %fold_y.4), channel_id=1, source_target_pairs={{0,1},{1,0},{2,3},{3,2},{4,5},{5,4},{6,7},{7,6},{8,9},{9,8},{10,11... | collective-permute-start | bytes 786440 | tf_op jit(solution)/shard_map/ppermute | solution.py:85
  37.2 8.4 %collective-permute-start.16 = (bf16[320,256]{1,0:T(8,128)(2,1)S(1)}, bf16[320,256]{1,0:T(8,128)(2,1)S(1)}, u32[]{:S(2)}, u32[]{:S(2)}) collective-permute-start(bf16[320,256]{1,0:T(8,128)(2,1)S(1)} %pack.1.refs_20_.refs_2_), channel_id=1, source_target_pairs={{0,16},{1,17},{2,18},{3,19},{4,20},{5,21},{6,22},{7,23},{8,24},{9,... | collective-permute-start | bytes 491528 | tf_op jit(solution)/shard_map/ppermute | solution.py:85
  39.6 5.9 %collective-permute-start.15 = (bf16[2,256,128]{2,1,0:T(8,128)(2,1)S(1)}, bf16[2,256,128]{2,1,0:T(8,128)(2,1)S(1)}, u32[]{:S(2)}, u32[]{:S(2)}) collective-permute-start(bf16[2,256,128]{2,1,0:T(8,128)(2,1)S(1)} %fold_w.7), channel_id=1, source_target_pairs={{0,8},{1,9},{2,10},{3,11},{4,12},{5,13},{6,14},{7,15},{8,0},{9,1},... | collective-permute-start | bytes 393224 | tf_op jit(solution)/shard_map/ppermute | solution.py:85
  44.2 5.2 %collective-permute-start.3 = (bf16[2,256,128]{2,1,0:T(8,128)(2,1)S(1)}, bf16[2,256,128]{2,1,0:T(8,128)(2,1)S(1)}, u32[]{:S(2)}, u32[]{:S(2)}) collective-permute-start(bf16[2,256,128]{2,1,0:T(8,128)(2,1)S(1)} %fold_w.4), channel_id=1, source_target_pairs={{0,8},{1,9},{2,10},{3,11},{4,12},{5,13},{6,14},{7,15},{8,0},{9,1},... | collective-permute-start | bytes 393224 | tf_op jit(solution)/shard_map/ppermute | solution.py:85
  52.2 24.9 %collective-permute-start.17 = (bf16[256,512]{1,0:T(8,128)(2,1)S(1)}, bf16[256,512]{1,0:T(8,128)(2,1)S(1)}, u32[]{:S(2)}, u32[]{:S(2)}) collective-permute-start(bf16[256,512]{1,0:T(8,128)(2,1)S(1)} %get-tuple-element.40), channel_id=1, source_target_pairs={{0,16},{1,17},{2,18},{3,19},{4,20},{5,21},{6,22},{7,23},{8,24},{9,... | collective-permute-start | bytes 786440 | tf_op jit(solution)/shard_map/ppermute | solution.py:85
  59.9 7.7 %collective-permute-start.22 = (bf16[32,512]{1,0:T(8,128)(2,1)S(1)}, bf16[32,512]{1,0:T(8,128)(2,1)S(1)}, u32[]{:S(2)}, u32[]{:S(2)}) collective-permute-start(bf16[32,512]{1,0:T(8,128)(2,1)S(1)} %get-tuple-element.46), channel_id=1, source_target_pairs={{0,8},{1,9},{2,10},{3,11},{4,12},{5,13},{6,14},{7,15},{8,0},{9,1},... | collective-permute-start | bytes 98312 | tf_op jit(solution)/shard_map/ppermute | solution.py:85
  79.8 14.9 %collective-permute-start.28 = (bf16[272,512]{1,0:T(8,128)(2,1)S(1)}, bf16[272,512]{1,0:T(8,128)(2,1)S(1)}, u32[]{:S(2)}, u32[]{:S(2)}) collective-permute-start(bf16[272,512]{1,0:T(8,128)(2,1)S(1)} %get-tuple-element.49.refs_0_), channel_id=1, source_target_pairs={{0,16},{1,17},{2,18},{3,19},{4,20},{5,21},{6,22},{7,23},{8,24},{9,... | collective-permute-start | bytes 835592 | tf_op jit(solution)/shard_map/ppermute | solution.py:85
  82.2 12.5 %collective-permute-start.36 = (bf16[272,512]{1,0:T(8,128)(2,1)S(1)}, bf16[272,512]{1,0:T(8,128)(2,1)S(1)}, u32[]{:S(2)}, u32[]{:S(2)}) collective-permute-start(bf16[272,512]{1,0:T(8,128)(2,1)S(1)} %get-tuple-element.49.refs_0_), channel_id=1, source_target_pairs={{0,8},{1,9},{2,10},{3,11},{4,12},{5,13},{6,14},{7,15},{8,0},{9,1},... | collective-permute-start | bytes 835592 | tf_op jit(solution)/shard_map/ppermute | solution.py:85
  82.2 14.4 %collective-permute-start.34 = (bf16[272,512]{1,0:T(8,128)(2,1)S(1)}, bf16[272,512]{1,0:T(8,128)(2,1)S(1)}, u32[]{:S(2)}, u32[]{:S(2)}) collective-permute-start(bf16[272,512]{1,0:T(8,128)(2,1)S(1)} %get-tuple-element.49.refs_0_), channel_id=1, source_target_pairs={{0,4},{1,5},{2,6},{3,7},{4,0},{5,1},{6,2},{7,3},{8,12},{9,13},{10,... | collective-permute-start | bytes 835592 | tf_op jit(solution)/shard_map/ppermute | solution.py:85
  82.6 15.7 %collective-permute-start.33 = (bf16[272,512]{1,0:T(8,128)(2,1)S(1)}, bf16[272,512]{1,0:T(8,128)(2,1)S(1)}, u32[]{:S(2)}, u32[]{:S(2)}) collective-permute-start(bf16[272,512]{1,0:T(8,128)(2,1)S(1)} %get-tuple-element.49.refs_0_), channel_id=1, source_target_pairs={{0,2},{1,3},{2,0},{3,1},{4,6},{5,7},{6,4},{7,5},{8,10},{9,11},{10,... | collective-permute-start | bytes 835592 | tf_op jit(solution)/shard_map/ppermute | solution.py:85
  94.7 6.9 %collective-permute-start.29 = (bf16[272,512]{1,0:T(8,128)(2,1)S(1)}, bf16[272,512]{1,0:T(8,128)(2,1)S(1)}, u32[]{:S(2)}, u32[]{:S(2)}) collective-permute-start(bf16[272,512]{1,0:T(8,128)(2,1)S(1)} %collective-permute-done.28.refs_8_), channel_id=1, source_target_pairs={{0,8},{1,9},{2,10},{3,11},{4,12},{5,13},{6,14},{7,15},{8,0},{9,1},... | collective-permute-start | bytes 835592 | tf_op jit(solution)/shard_map/ppermute | solution.py:85
  94.7 6.9 %collective-permute-start.38 = (bf16[272,512]{1,0:T(8,128)(2,1)S(1)}, bf16[272,512]{1,0:T(8,128)(2,1)S(1)}, u32[]{:S(2)}, u32[]{:S(2)}) collective-permute-start(bf16[272,512]{1,0:T(8,128)(2,1)S(1)} %collective-permute-done.36.refs_4_), channel_id=1, source_target_pairs={{0,4},{1,5},{2,6},{3,7},{4,0},{5,1},{6,2},{7,3},{8,12},{9,13},{10,... | collective-permute-start | bytes 835592 | tf_op jit(solution)/shard_map/ppermute | solution.py:85
  94.7 11.5 %collective-permute-start.37 = (bf16[272,512]{1,0:T(8,128)(2,1)S(1)}, bf16[272,512]{1,0:T(8,128)(2,1)S(1)}, u32[]{:S(2)}, u32[]{:S(2)}) collective-permute-start(bf16[272,512]{1,0:T(8,128)(2,1)S(1)} %collective-permute-done.36.refs_4_), channel_id=1, source_target_pairs={{0,2},{1,3},{2,0},{3,1},{4,6},{5,7},{6,4},{7,5},{8,10},{9,11},{10,... | collective-permute-start | bytes 835592 | tf_op jit(solution)/shard_map/ppermute | solution.py:85
  96.6 10.4 %collective-permute-start.41 = (bf16[272,512]{1,0:T(8,128)(2,1)S(1)}, bf16[272,512]{1,0:T(8,128)(2,1)S(1)}, u32[]{:S(2)}, u32[]{:S(2)}) collective-permute-start(bf16[272,512]{1,0:T(8,128)(2,1)S(1)} %collective-permute-done.28.refs_8_), channel_id=1, source_target_pairs={{0,4},{1,5},{2,6},{3,7},{4,0},{5,1},{6,2},{7,3},{8,12},{9,13},{10,... | collective-permute-start | bytes 835592 | tf_op jit(solution)/shard_map/ppermute | solution.py:85
  98.3 13.8 %collective-permute-start.35 = (bf16[272,512]{1,0:T(8,128)(2,1)S(1)}, bf16[272,512]{1,0:T(8,128)(2,1)S(1)}, u32[]{:S(2)}, u32[]{:S(2)}) collective-permute-start(bf16[272,512]{1,0:T(8,128)(2,1)S(1)} %collective-permute-done.34.refs_2_), channel_id=1, source_target_pairs={{0,2},{1,3},{2,0},{3,1},{4,6},{5,7},{6,4},{7,5},{8,10},{9,11},{10,... | collective-permute-start | bytes 835592 | tf_op jit(solution)/shard_map/ppermute | solution.py:85
  101.6 11.3 %collective-permute-start.31 = (bf16[272,512]{1,0:T(8,128)(2,1)S(1)}, bf16[272,512]{1,0:T(8,128)(2,1)S(1)}, u32[]{:S(2)}, u32[]{:S(2)}) collective-permute-start(bf16[272,512]{1,0:T(8,128)(2,1)S(1)} %collective-permute-done.29.refs_0_), channel_id=1, source_target_pairs={{0,4},{1,5},{2,6},{3,7},{4,0},{5,1},{6,2},{7,3},{8,12},{9,13},{10,... | collective-permute-start | bytes 835592 | tf_op jit(solution)/shard_map/ppermute | solution.py:85
  101.6 14.1 %collective-permute-start.40 = (bf16[272,512]{1,0:T(8,128)(2,1)S(1)}, bf16[272,512]{1,0:T(8,128)(2,1)S(1)}, u32[]{:S(2)}, u32[]{:S(2)}) collective-permute-start(bf16[272,512]{1,0:T(8,128)(2,1)S(1)} %collective-permute-done.28.refs_8_), channel_id=1, source_target_pairs={{0,2},{1,3},{2,0},{3,1},{4,6},{5,7},{6,4},{7,5},{8,10},{9,11},{10,... | collective-permute-start | bytes 835592 | tf_op jit(solution)/shard_map/ppermute | solution.py:85
  106.1 9.5 %collective-permute-start.39 = (bf16[272,512]{1,0:T(8,128)(2,1)S(1)}, bf16[272,512]{1,0:T(8,128)(2,1)S(1)}, u32[]{:S(2)}, u32[]{:S(2)}) collective-permute-start(bf16[272,512]{1,0:T(8,128)(2,1)S(1)} %collective-permute-done.38.refs_6_), channel_id=1, source_target_pairs={{0,2},{1,3},{2,0},{3,1},{4,6},{5,7},{6,4},{7,5},{8,10},{9,11},{10,... | collective-permute-start | bytes 835592 | tf_op jit(solution)/shard_map/ppermute | solution.py:85
  106.9 8.8 %collective-permute-start.42 = (bf16[272,512]{1,0:T(8,128)(2,1)S(1)}, bf16[272,512]{1,0:T(8,128)(2,1)S(1)}, u32[]{:S(2)}, u32[]{:S(2)}) collective-permute-start(bf16[272,512]{1,0:T(8,128)(2,1)S(1)} %collective-permute-done.41.refs_10_), channel_id=1, source_target_pairs={{0,2},{1,3},{2,0},{3,1},{4,6},{5,7},{6,4},{7,5},{8,10},{9,11},{10,... | collective-permute-start | bytes 835592 | tf_op jit(solution)/shard_map/ppermute | solution.py:85
  112.1 5.4 %collective-permute-start.30 = (bf16[272,512]{1,0:T(8,128)(2,1)S(1)}, bf16[272,512]{1,0:T(8,128)(2,1)S(1)}, u32[]{:S(2)}, u32[]{:S(2)}) collective-permute-start(bf16[272,512]{1,0:T(8,128)(2,1)S(1)} %collective-permute-done.29.refs_0_), channel_id=1, source_target_pairs={{0,2},{1,3},{2,0},{3,1},{4,6},{5,7},{6,4},{7,5},{8,10},{9,11},{10,... | collective-permute-start | bytes 835592 | tf_op jit(solution)/shard_map/ppermute | solution.py:85
  112.9 4.6 %collective-permute-start.32 = (bf16[272,512]{1,0:T(8,128)(2,1)S(1)}, bf16[272,512]{1,0:T(8,128)(2,1)S(1)}, u32[]{:S(2)}, u32[]{:S(2)}) collective-permute-start(bf16[272,512]{1,0:T(8,128)(2,1)S(1)} %collective-permute-done.31.refs_2_), channel_id=1, source_target_pairs={{0,2},{1,3},{2,0},{3,1},{4,6},{5,7},{6,4},{7,5},{8,10},{9,11},{10,... | collective-permute-start | bytes 835592 | tf_op jit(solution)/shard_map/ppermute | solution.py:85
  (16 other events, 113.6 us)

commit v3 on v2

v3 whole, which is shorter than its diff:
```python
import functools

import jax
import jax.numpy as jnp
from jax import lax
from jax.experimental import pallas as pl
from jax.experimental.pallas import tpu as pltpu
from jax.sharding import PartitionSpec as P

f32, bf16 = jnp.float32, jnp.bfloat16
bias_first = 1.0 - 0.9**10
bias_second = 1.0 - 0.999**10
AXES = ("node", "local")
PIECES = ((0, 4, 0, 1), (1, 4, 0, 1), (2, 4, 0, 1), (3, 4, 0, 2), (3, 4, 1, 2))
ORDERS = ("xyw", "ywx", "wxy", "ywx", "wxy")
PAD = 16
ALL = slice(None)
MIB = 2**20


def total(terms):
    return functools.reduce(lambda a, b: a + b, [t.astype(f32) for t in terms])


def at(array, index, axis):
    return lax.dynamic_index_in_dim(array, index, axis, False)


def vmem(array):
    return pltpu.with_memory_space_constraint(array, pltpu.VMEM)


class Grid:
    def __init__(self):
        nodes, local = lax.axis_size("node"), lax.axis_size("local")
        size, left = {"y": local}, nodes
        for axis in "cxw":
            size[axis] = 2 if left % 2 == 0 else 1
            left //= size[axis]
        size["v"] = left
        self.size, self.nodes = size, nodes

    def split(self, node):
        place = {}
        for axis in "cxwv":
            place[axis], node = node % self.size[axis], node // self.size[axis]
        return place

    def node(self, place):
        node = 0
        for axis in "vwxc":
            node = node * self.size[axis] + place[axis]
        return node

    def place(self):
        place, node = {"y": lax.axis_index("local")}, lax.axis_index("node")
        for axis in "cxwv":
            place[axis] = lax.rem(node, self.size[axis])
            node = lax.div(node, self.size[axis])
        return place

    def step(self, axis, here, d):
        size = self.size[axis]
        if size & (size - 1):
            if isinstance(here, int):
                return (here + d) % size
            return lax.rem(here + (d + size) % size, size)
        if isinstance(here, int):
            return here ^ abs(d)
        return lax.bitwise_xor(here, jnp.int32(abs(d)))

    def others(self, axis):
        return range(1, self.size[axis])

    def send(self, array, **steps):
        local, pairs = self.size["y"], []
        for n in range(self.nodes):
            for y in range(local):
                place = self.split(n) | {"y": y}
                there = {a: self.step(a, i, steps.get(a, 0)) for a, i in place.items()}
                pairs.append((n * local + y, self.node(there) * local + there["y"]))
        return lax.ppermute(array, AXES, pairs)


def call(kernel, name, arrays, outs, scratch=(), limit=8):
    return pl.pallas_call(
        kernel,
        out_shape=outs,
        in_specs=[pl.BlockSpec(memory_space=pltpu.VMEM)] * len(arrays),
        out_specs=jax.tree.map(lambda _: pl.BlockSpec(memory_space=pltpu.VMEM), outs),
        scratch_shapes=scratch,
        compiler_params=pltpu.CompilerParams(vmem_limit_bytes=limit * MIB),
        cost_estimate=pl.CostEstimate(flops=0, bytes_accessed=1, transcendentals=0),
        name=name,
    )(*[vmem(a) for a in arrays])


def dequant(grid, values, exponents, away, rows, blocksize, pieces):
    cores, local, pair = (grid.size[a] for a in "cyx")
    rest = grid.size["v"] * grid.size["w"]
    lead, parts = tuple(grid.size[a] for a in "yvwx"), len(pieces)
    shapes = [lead + (p[0].stop - p[0].start, p[1].stop - p[1].start) for p in pieces]
    nblocks, columns = exponents.shape[0], values.shape[1]
    if rows % 128:
        which = grid.step("c", grid.place()["c"], away)
        power = jnp.exp2(exponents.astype(f32)).astype(bf16)
        picked = power.reshape(-1, local, rest, pair, cores, rows)
        picked = jnp.moveaxis(at(picked, which, 4), 0, -1)
        mant = at(values.reshape(local, rest, pair, cores, rows, -1, blocksize), which, 3)
        out = (mant * picked[..., None]).reshape(lead + (rows, columns))
        return [out[(..., *p)] for p in pieces]

    def kernel(exps, mant, *refs):
        outs, (held, sems) = refs[:parts], refs[parts:]
        which = grid.step("c", grid.place()["c"], away)
        copies = {}
        for l in range(local):
            for r in range(rest):
                copies[l, r] = pltpu.make_async_copy(
                    mant.at[l, r, :, which], held.at[l, r], sems.at[l, r]
                )
                copies[l, r].start()
        spread = lax.broadcasted_iota(jnp.int32, (nblocks, columns), 1) // blocksize
        spread = spread == lax.broadcasted_iota(jnp.int32, (nblocks, columns), 0)
        spread = spread.astype(bf16)
        for l in range(local):
            for r in range(rest):
                copies[l, r].wait()
                for i in range(pair):
                    start = (((l * rest + r) * pair + i) * cores + which) * rows
                    power = exps[:, pl.ds(pl.multiple_of(start, 128), rows)].astype(f32)
                    factor = lax.dot_general(
                        jnp.exp2(power).astype(bf16),
                        spread,
                        (((0,), (0,)), ((), ())),
                        preferred_element_type=f32,
                    )
                    scaled = (held[l, r, i].astype(f32) * factor).astype(bf16)
                    for out, piece in zip(outs, pieces):
                        out[l, r // lead[2], r % lead[2], i] = scaled[piece]

    mant = values.reshape(local, rest, pair, cores, rows, columns)
    return pl.pallas_call(
        kernel,
        out_shape=[pltpu.VMEM(shape, bf16) for shape in shapes],
        in_specs=[
            pl.BlockSpec(memory_space=pltpu.VMEM),
            pl.BlockSpec(memory_space=pl.ANY),
        ],
        out_specs=[pl.BlockSpec(memory_space=pltpu.VMEM)] * parts,
        scratch_shapes=[
            pltpu.VMEM((local, rest, pair, rows, columns), bf16),
            pltpu.SemaphoreType.DMA((local, rest)),
        ],
        compiler_params=pltpu.CompilerParams(vmem_limit_bytes=16 * MIB),
        cost_estimate=pl.CostEstimate(flops=0, bytes_accessed=1, transcendentals=0),
        name="dequant",
    )(vmem(exponents), pltpu.with_memory_space_constraint(mant, pltpu.HBM))


class Unit:
    def __init__(self, grid, terms):
        self.grid, self.left = grid, "yvwx"
        self.terms = [(t, "yvwx") for t in terms]

    @staticmethod
    def entry(axes, where):
        return tuple(where.get(a, ALL) for a in axes)

    def hop(self, axis):
        grid, left = self.grid, self.left.replace(axis, "")
        arrays = [t for t, _ in self.terms]
        shape = tuple(grid.size[a] for a in left) + arrays[0].shape[-2:]

        def kernel(*refs):
            held, outs = refs[: len(arrays)], refs[len(arrays) :]
            place = grid.place()
            for d, out in zip(grid.others(axis), outs):
                where = {a: i for a, i in place.items() if a not in self.left}
                where[axis] = grid.step(axis, place[axis], d)
                parts = [t[self.entry(axes, where)] for t, (_, axes) in zip(held, self.terms)]
                out[...] = total(parts).astype(bf16)

        outs = [pltpu.VMEM(shape, bf16) for _ in grid.others(axis)]
        if outs:
            outs = call(kernel, "fold_" + axis, arrays, outs)
        self.left = left
        for d, out in zip(grid.others(axis), outs):
            self.terms.append((grid.send(out, **{axis: d}), left))


def project(grid, units, pieces, packs, rows, ranks, columns):
    size = grid.size
    each = ranks // grid.nodes
    arrays = [t for u in units for t, _ in u.terms]

    def kernel(*refs):
        held, refs = iter(refs[: len(arrays)]), refs[len(arrays) :]
        projs, refs = refs[: size["v"]], refs[size["v"] :]
        sends, outs, acc = refs[: size["v"]], refs[size["v"] : -1], refs[-1]
        place = grid.place()
        dims = (((0,), (0,)), ((), ()))
        for unit, piece in zip(units, pieces):
            terms = [(next(held), axes) for _, axes in unit.terms]
            for d, send in enumerate(sends):
                where = place | {"v": grid.step("v", place["v"], d)}
                value = total([t[Unit.entry(axes, where)] for t, axes in terms])
                send[piece] = value.astype(bf16)
        acc[...] = total(
            [
                lax.dot_general(came[:rows], send[...], dims, preferred_element_type=f32)
                for came, send in zip(projs, sends)
            ]
        )
        for d, out in enumerate(outs):
            there = {"c": grid.step("c", place["c"], d)}
            for e in range(size["x"]):
                there["x"] = grid.step("x", place["x"], e)
                for f in range(size["w"]):
                    there["w"] = grid.step("w", place["w"], f)
                    for v in range(size["v"]):
                        start = pl.multiple_of(grid.node(there | {"v": v}) * each, each)
                        out[e, f, v * each : (v + 1) * each] = acc[pl.ds(start, each)]

    out = call(
        kernel,
        "project",
        arrays + packs,
        [pltpu.VMEM((rows, columns), bf16)] * size["v"]
        + [pltpu.VMEM((size["x"], size["w"], size["v"] * each, columns), f32)] * size["c"],
        [pltpu.VMEM((ranks, columns), f32)],
        limit=12,
    )
    return out[: size["v"]], out[size["v"] :]


def add_cut(terms, name, run=1):
    count = terms[0].shape[0]

    def kernel(*refs):
        arrays, outs = refs[: len(terms)], refs[len(terms) :]
        for e, out in enumerate(outs):
            parts = [a[e] for a in arrays]
            runs = [total(parts[i : i + run]) for i in range(0, len(parts), run)]
            out[...] = total(runs).astype(out.dtype)

    return call(kernel, name, terms, [pltpu.VMEM(terms[0].shape[1:], bf16)] * count)


def add(terms, name, dtype):
    def kernel(*refs):
        *arrays, out = refs
        out[...] = total([a[...] for a in arrays]).astype(dtype)

    return call(kernel, name, terms, pltpu.VMEM(terms[0].shape, dtype))


def pack(proj, moments):
    rows, ranks = proj.shape
    each, columns = moments[0].shape
    cuts = columns // ranks

    def kernel(proj, moment1, moment2, out):
        out[:rows] = proj[...].astype(bf16)
        both = jnp.concatenate([moment1[...], moment2[...]], 0).astype(bf16)
        for h in range(cuts):
            start = rows + h * 2 * each
            out[start : start + 2 * each] = both[:, h * ranks : (h + 1) * ranks]

    shape = (rows + cuts * 2 * each, ranks)
    return call(kernel, "pack", [proj, *moments], pltpu.VMEM(shape, bf16))


def normalize(grid, parts, packs, rows, first, columns):
    ranks = packs[0].shape[1]
    group = parts[0].shape[1]
    each = ranks // grid.nodes
    cuts = columns // ranks
    rest = grid.size["v"]

    def kernel(*refs):
        v = grid.place()["v"]
        arrays, held = refs[: len(parts)], refs[len(parts) : len(parts) + rest]
        sums, mine, scratch = refs[len(parts) + rest :]
        scratch[...] = total([a[...] for a in arrays]).reshape(scratch.shape)
        mine[...] = scratch[v]
        raw, tilde = 0.0, 0.0
        for d in range(rest):
            value = scratch[grid.step("v", v, d)]
            old = []
            for h in range(cuts):
                start = rows + h * 2 * each
                old.append(held[d][start : start + 2 * each].astype(f32))
            old = jnp.concatenate(old, 1)[:, first : first + group]
            m1 = 0.9 * old[:each] + 0.1 * value
            m2 = 0.999 * old[each:] + 0.001 * value * value
            ratio = m1 / bias_first / (jnp.sqrt(m2 / bias_second) + 1e-08)
            raw += jnp.sum(value * value, 0, keepdims=True)
            tilde += jnp.sum(ratio * ratio, 0, keepdims=True)
        sums[...] = jnp.concatenate([raw, tilde, jnp.zeros((6, group), f32)], 0)

    return call(
        kernel,
        "normalize",
        parts + packs,
        [pltpu.VMEM((8, group), f32), pltpu.VMEM((each, group), f32)],
        [pltpu.VMEM((rest, each, group), f32)],
    )


def update(weights, moments, grads, sums, mine, blocksize):
    rows, columns = weights.shape

    def kernel(weights, moment1, moment2, *refs):
        grad_refs, refs = refs[: len(grads)], refs[len(grads) :]
        sum_refs, refs = refs[: len(sums)], refs[len(sums) :]
        mine, new_out, new1, new2, packed = refs
        packed[rows:, :] = jnp.zeros((PAD, columns), bf16)
        lane = lax.broadcasted_iota(jnp.int32, (rows, 128), 1)
        scales = jnp.zeros((rows, 128), f32)
        added = total([s[...] for s in sum_refs])
        col_scale = jnp.sqrt(added[1:2]) / jnp.sqrt(added[0:1] + 1e-06)
        for k in range(columns // blocksize):
            cols = slice(k * blocksize, (k + 1) * blocksize)
            grad = total([t[:, cols] for t in grad_refs])
            new = weights[:, cols] - 8.0 * grad * col_scale[:, cols]
            new_out[:, cols] = new
            scale = (jnp.max(jnp.abs(new), 1, keepdims=True) + 1e-06).astype(bf16).astype(f32)
            packed[:rows, cols] = (new / scale).astype(bf16)
            scales = jnp.where(lane == k, scale, scales)
        new1[...] = 0.9 * moment1[...] + 0.1 * mine[...]
        new2[...] = 0.999 * moment2[...] + 0.001 * mine[...] * mine[...]
        packed[rows:, :rows] = jnp.transpose(scales)[:PAD].astype(bf16)

    return call(
        kernel,
        "update",
        [weights, *moments, *grads, *sums, mine],
        [
            jax.ShapeDtypeStruct((rows, columns), f32),
            jax.ShapeDtypeStruct(moments[0].shape, f32),
            jax.ShapeDtypeStruct(moments[0].shape, f32),
            pltpu.VMEM((rows + PAD, columns), bf16),
        ],
    )


def lay(grid, held, nblocks, *begun):
    shards, steps = [t for t, _ in held], [step for _, step in held]
    rows, columns = shards[0].shape[0] - PAD, shards[0].shape[1]
    count = len(shards)

    def node_of(k):
        place = grid.place()
        return grid.node({a: grid.step(a, place[a], -steps[k][a]) for a in "vwxc"})

    if rows % 128:
        places = jnp.stack([node_of(k) for k in range(count)])
        order = jnp.zeros(count, jnp.int32).at[places].set(jnp.arange(count, dtype=jnp.int32))
        stacked = jnp.take(jnp.stack(shards), order, axis=0)
        values = stacked[:, :rows].reshape(count * rows, columns)
        scales = jnp.moveaxis(stacked[:, rows : rows + nblocks, :rows], 0, 1)
        return values, scales.reshape(nblocks, count * rows)

    def kernel(*refs):
        held, (values, scales, sems) = refs[:count], refs[count + len(begun) :]
        if begun:
            scales[...] = refs[count + 1][...]
        copies = []
        for k in range(count):
            start = pl.multiple_of(node_of(k) * rows, 128)
            copies.append(
                pltpu.make_async_copy(
                    held[k].at[pl.ds(0, rows)], values.at[pl.ds(start, rows)], sems.at[k]
                )
            )
            copies[-1].start()
        for k in range(count):
            start = pl.multiple_of(node_of(k) * rows, 128)
            tail = held[k][rows:, :rows].astype(f32)[:nblocks]
            scales[:, pl.ds(start, rows)] = tail.astype(bf16)
        for copy in copies:
            copy.wait()

    in_vmem, anywhere = (pl.BlockSpec(memory_space=m) for m in (pltpu.VMEM, pl.ANY))
    scales_shape = (nblocks, grid.nodes * rows)
    return pl.pallas_call(
        kernel,
        out_shape=[
            pltpu.HBM((grid.nodes * rows, columns), bf16),
            jax.ShapeDtypeStruct(scales_shape, bf16) if begun else pltpu.VMEM(scales_shape, bf16),
        ],
        in_specs=[in_vmem] * count + [anywhere, in_vmem][: len(begun)],
        out_specs=[anywhere, in_vmem],
        input_output_aliases={count: 0} if begun else {},
        scratch_shapes=[pltpu.SemaphoreType.DMA((count,))],
        compiler_params=pltpu.CompilerParams(vmem_limit_bytes=8 * MIB),
        cost_estimate=pl.CostEstimate(flops=0, bytes_accessed=1, transcendentals=0),
        name="lay",
    )(*[vmem(s) for s in shards], *begun)


def shards(grad_values, grad_exponents, proj, weights, moment1, moment2):
    grid = Grid()
    size = grid.size
    values, exponents = grad_values[0], grad_exponents[0]
    width, columns = values.shape
    nblocks = exponents.shape[0]
    blocksize = columns // nblocks
    rows = width // grid.nodes // size["y"]
    ranks = proj.shape[1]
    pieces = []
    for block, blocks, half, halves in PIECES:
        n, m = rows // halves, columns // blocks
        pieces.append((slice(half * n, (half + 1) * n), slice(block * m, (block + 1) * m)))

    other = dequant(grid, values, exponents, 1, rows, blocksize, pieces) if size["c"] > 1 else []
    other = [grid.send(t, c=1) for t in other]
    mine = dequant(grid, values, exponents, 0, rows, blocksize, pieces)
    units = [Unit(grid, list(terms)) for terms in zip(mine, *([other] if other else []))]
    for turn in range(3):
        for unit, order in zip(units, ORDERS):
            unit.hop(order[turn])

    packs = [pack(proj, [moment1, moment2])]
    packs += [grid.send(packs[0], v=-d) for d in grid.others("v")]

    parts, projected = project(grid, units, pieces, packs, rows, ranks, columns)
    received = [grid.send(t, v=d) for d, t in zip(grid.others("v"), parts[1:])]

    terms = [projected[0]] + [grid.send(projected[d], c=d) for d in grid.others("c")]
    by_x = add_cut(terms, "add_cores")
    by_y = []
    for dy in range(size["y"]):
        for dx in range(size["x"]):
            by_y.append(grid.send(by_x[dx], x=dx, y=dy) if dx or dy else by_x[0])
    if size["y"] > 2:
        stacked = jnp.stack(by_y).reshape((size["y"], -1) + by_y[0].shape)
        came = jnp.stack([grid.step("y", grid.place()["y"], -d) for d in range(size["y"])])
        order = jnp.zeros(size["y"], jnp.int32).at[came].set(jnp.arange(size["y"], dtype=jnp.int32))
        stacked = jnp.take(stacked, order, axis=0)
        by_y = [stacked[i, j] for i in range(size["y"]) for j in range(stacked.shape[1])]
    by_w = add_cut(by_y, "add_chips", size["x"])
    summed = [
        grid.send(by_w[dw], w=dw, v=dv) if dw or dv else by_w[0]
        for dv in range(size["v"])
        for dw in range(size["w"])
    ]
    added, kept = normalize(grid, summed, packs, rows, 0, columns)
    added = add([added] + [grid.send(added, c=d) for d in grid.others("c")], "add_sums", f32)
    sums = [
        grid.send(added, x=dx, w=dw) if dx or dw else added
        for dx in range(size["x"])
        for dw in range(size["w"])
    ]
    new, new1, new2, packed = update(
        weights, [moment1, moment2], [parts[0], *received], sums, kept, blocksize
    )

    along_v = [packed] + [grid.send(packed, v=d) for d in grid.others("v")]
    held = []
    for dv, over_v in enumerate(along_v):
        along_w = [over_v] + [grid.send(over_v, w=d) for d in grid.others("w")]
        for dw, over_w in enumerate(along_w):
            along_x = [over_w] + [grid.send(over_w, x=d) for d in grid.others("x")]
            for dx, over_x in enumerate(along_x):
                along_c = [over_x] + [grid.send(over_x, c=d) for d in grid.others("c")]
                for dc, shard in enumerate(along_c):
                    held.append((shard, {"v": dv, "w": dw, "x": dx, "c": dc}))
    late = [t for t in held if t[1]["v"] and t[1]["w"]]
    if late and rows % 128 == 0:
        early = [t for t in held if not (t[1]["v"] and t[1]["w"])]
        begun = lay(grid, early, nblocks)
        quant, scales = lay(grid, late, nblocks, *begun)
    else:
        quant, scales = lay(grid, held, nblocks)
    return quant, scales, new, new1, new2


def solution(mesh):
    return jax.shard_map(
        shards,
        mesh=mesh,
        in_specs=(
            P(("node", "local"), None, None),
            P(("node", "local"), None, None),
            P(("local", "node"), None),
            P(("local", "node"), None),
            P("node", None),
            P("node", None),
        ),
        out_specs=(
            P("local", None),
            P(None, "local"),
            P(("local", "node"), None),
            P("node", None),
            P("node", None),
        ),
        check_vma=False,
    )
```

time: 119 us -> 115 us (0.966)
  waiting for transfers between devices: 48 us -> 38 us
  starting transfers between devices: 55.3 us -> 61.1 us
    ppermute x43 -> x48, waiting for transfers between devices: 48 us -> 38 us  [send(): return lax.ppermute(array, AXES, pairs)]
    ppermute x43 -> x48, starting transfers between devices: 55.3 us -> 61.1 us  [send(): return lax.ppermute(array, AXES, pairs)]
    pallas_call x24 -> x26, Pallas kernels: 13.4 us -> 14.1 us  [the longest x2 7.49 us: dequant(): pl.pallas_call(kernel, out_shape=[pltpu.VMEM(shape, bf16) for shape in sh...]
  transfers between devices with their start and end apart: 43 -> 48, of which waited for: 18 -> 17; matrix products, arithmetic and copies ran while one was open for 0% -> 0% of each run, Pallas kernels for 6% -> 6%
where the time goes in v3:
time: 115 us
  starting transfers between devices  61.1 us (53%)
  waiting for transfers between devices  38 us (33%)
  Pallas kernels  14.1 us (12%)
    ppermute x48, starting transfers between devices, send(): return lax.ppermute(array, AXES, pairs)  61.1 us
    ppermute x48, waiting for transfers between devices, send(): return lax.ppermute(array, AXES, pairs)  38 us
    pallas_call x2, Pallas kernels, dequant(): pl.pallas_call(kernel, out_shape=[pltpu.VMEM(shape, bf16) for shape in sh...  7.49 us
    pallas_call x2, Pallas kernels, lay(): pl.pallas_call(kernel, out_shape=[pltpu.HBM((grid.nodes * rows, columns),...  3.42 us
    pallas_call x22, Pallas kernels, call(): pl.pallas_call(kernel, out_shape=outs, in_specs=[pl.BlockSpec(memory_spac...  3.19 us
  transfers between devices with their start and end apart: 48, of which 17 were waited for; matrix products, arithmetic and copies ran while one was open for 0% of the time, Pallas kernels for 6%

profile of v3, /device:TPU:1, one launch (start us, length us, event | category | flops | bytes accessed | tf_op | source)
XLA Modules:
  0.0 115.1 jit_solution(15275309105561534834)
XLA Ops:
  1.5 3.7 %dequant.3 = (bf16[2,2,2,2,256,128]{5,4,3,2,1,0:T(8,128)(2,1)S(1)}, bf16[2,2,2,2,256,128]{5,4,3,2,1,0:T(8,128)(2,1)S(1)}, bf16[2,2,2,2,256,128]{5,4,3,2,1,0:T(8,...) custom-call(s32[4,8192]{1,0:T(4,128)S(1)} %bitcast.2, ...), custom_call_target="tpu_custom_call" | custom-call | bytes 1 | tf_op jit(solution)/shard_map/dequant/pallas_call | solution.py:143
  6.5 3.7 %dequant.2 = (bf16[2,2,2,2,256,128]{5,4,3,2,1,0:T(8,128)(2,1)S(1)}, bf16[2,2,2,2,256,128]{5,4,3,2,1,0:T(8,128)(2,1)S(1)}, bf16[2,2,2,2,256,128]{5,4,3,2,1,0:T(8,...) custom-call(s32[4,8192]{1,0:T(4,128)S(1)} %bitcast.3, ...), custom_call_target="tpu_custom_call" | custom-call | bytes 1 | tf_op jit(solution)/shard_map/dequant/pallas_call | solution.py:143
  10.4 2.8 %collective-permute-start.9 = (bf16[2,2,2,256,128]{4,3,2,1,0:T(8,128)(2,1)S(1)}, bf16[2,2,2,256,128]{4,3,2,1,0:T(8,128)(2,1)S(1)}, u32[]{:S(2)}, u32[]{:S(2)}) collective-permute-start(bf16[2,2,2,256,128]{4,3,2,1,0:T(8,128)(2,1)S(1)} %fold_w.7), channel_id=1, source_target_pairs={{0,8},{1,9},{2,10},{3,11},{4,12},{5,13},{6,14},{7,15},{8,0},{9,1},... | collective-permute-start | bytes 1572872 | tf_op jit(solution)/shard_map/ppermute | solution.py:82
  16.7 8.7 %collective-permute-done.9.refs_2_.refs_12_ = bf16[2,2,2,256,128]{4,3,2,1,0:T(8,128)(2,1)S(1)} collective-permute-done((bf16[2,2,2,256,128]{4,3,2,1,0:T(8,128)(2,1)S(1)}, bf16[2,2,2,256,128]{4,3,2,1,0:T(8,128)(2,1)S(1)}, u32[]{:S(2)}, u32[]{:S(2)}) %collective-permute-start.9) | collective-permute-done | bytes 524320 | tf_op jit(solution)/shard_map/ppermute | solution.py:82
  26.9 1.4 %collective-permute-start.6 = (bf16[2,2,256,128]{3,2,1,0:T(8,128)(2,1)S(1)}, bf16[2,2,256,128]{3,2,1,0:T(8,128)(2,1)S(1)}, u32[]{:S(2)}, u32[]{:S(2)}) collective-permute-start(bf16[2,2,256,128]{3,2,1,0:T(8,128)(2,1)S(1)} %fold_w.6), channel_id=1, source_target_pairs={{0,8},{1,9},{2,10},{3,11},{4,12},{5,13},{6,14},{7,15},{8,0},{9,1},... | collective-permute-start | bytes 786440 | tf_op jit(solution)/shard_map/ppermute | solution.py:82
  32.4 2.4 %collective-permute-start.20 = (bf16[320,256]{1,0:T(8,128)(2,1)S(1)}, bf16[320,256]{1,0:T(8,128)(2,1)S(1)}, u32[]{:S(2)}, u32[]{:S(2)}) collective-permute-start(bf16[320,256]{1,0:T(8,128)(2,1)S(1)} %pack.1.refs_25_.refs_4_), channel_id=1, source_target_pairs={{0,16},{1,17},{2,18},{3,19},{4,20},{5,21},{6,22},{7,23},{8,24},{9,... | collective-permute-start | bytes 491528 | tf_op jit(solution)/shard_map/ppermute | solution.py:82
  34.8 1.4 %collective-permute-start.14 = (bf16[2,2,128,128]{3,2,1,0:T(8,128)(2,1)S(1)}, bf16[2,2,128,128]{3,2,1,0:T(8,128)(2,1)S(1)}, u32[]{:S(2)}, u32[]{:S(2)}) collective-permute-start(bf16[2,2,128,128]{3,2,1,0:T(8,128)(2,1)S(1)} %fold_w.8), channel_id=1, source_target_pairs={{0,8},{1,9},{2,10},{3,11},{4,12},{5,13},{6,14},{7,15},{8,0},{9,1},... | collective-permute-start | bytes 393224 | tf_op jit(solution)/shard_map/ppermute | solution.py:82
  36.2 1.8 %collective-permute-done.6.refs_3_.refs_8_ = bf16[2,2,256,128]{3,2,1,0:T(8,128)(2,1)S(1)} collective-permute-done((bf16[2,2,256,128]{3,2,1,0:T(8,128)(2,1)S(1)}, bf16[2,2,256,128]{3,2,1,0:T(8,128)(2,1)S(1)}, u32[]{:S(2)}, u32[]{:S(2)}) %collective-permute-start.6) | collective-permute-done | bytes 262176 | tf_op jit(solution)/shard_map/ppermute | solution.py:82
  38.0 2.2 %collective-permute-start.11 = (bf16[2,256,128]{2,1,0:T(8,128)(2,1)S(1)}, bf16[2,256,128]{2,1,0:T(8,128)(2,1)S(1)}, u32[]{:S(2)}, u32[]{:S(2)}) collective-permute-start(bf16[2,256,128]{2,1,0:T(8,128)(2,1)S(1)} %fold_y.7), channel_id=1, source_target_pairs={{0,1},{1,0},{2,3},{3,2},{4,5},{5,4},{6,7},{7,6},{8,9},{9,8},{10,11... | collective-permute-start | bytes 393224 | tf_op jit(solution)/shard_map/ppermute | solution.py:82
  41.8 1.6 %collective-permute-start.19 = (bf16[2,128,128]{2,1,0:T(8,128)(2,1)S(1)}, bf16[2,128,128]{2,1,0:T(8,128)(2,1)S(1)}, u32[]{:S(2)}, u32[]{:S(2)}) collective-permute-start(bf16[2,128,128]{2,1,0:T(8,128)(2,1)S(1)} %fold_y.9), channel_id=1, source_target_pairs={{0,1},{1,0},{2,3},{3,2},{4,5},{5,4},{6,7},{7,6},{8,9},{9,8},{10,11... | collective-permute-start | bytes 196616 | tf_op jit(solution)/shard_map/ppermute | solution.py:82
  45.9 1.7 %collective-permute-done.15.refs_19_ = bf16[2,128,128]{2,1,0:T(8,128)(2,1)S(1)} collective-permute-done((bf16[2,128,128]{2,1,0:T(8,128)(2,1)S(1)}, bf16[2,128,128]{2,1,0:T(8,128)(2,1)S(1)}, u32[]{:S(2)}, u32[]{:S(2)}) %collective-permute-start.15) | collective-permute-done | bytes 65568 | tf_op jit(solution)/shard_map/ppermute | solution.py:82
  48.4 2.5 %collective-permute-start.22 = (f32[2,2,32,512]{3,2,1,0:T(8,128)S(1)}, f32[2,2,32,512]{3,2,1,0:T(8,128)S(1)}, u32[]{:S(2)}, u32[]{:S(2)}) collective-permute-start(f32[2,2,32,512]{3,2,1,0:T(8,128)S(1)} %get-tuple-element.46), channel_id=1, source_target_pairs={{0,2},{1,3},{2,0},{3,1},{4,6},{5,7},{6,4},{7,5},{8,10},{9,11},{10,... | collective-permute-start | bytes 786440 | tf_op jit(solution)/shard_map/ppermute | solution.py:82
  50.9 2.5 %collective-permute-start.21 = (bf16[256,512]{1,0:T(8,128)(2,1)S(1)}, bf16[256,512]{1,0:T(8,128)(2,1)S(1)}, u32[]{:S(2)}, u32[]{:S(2)}) collective-permute-start(bf16[256,512]{1,0:T(8,128)(2,1)S(1)} %get-tuple-element.44), channel_id=1, source_target_pairs={{0,16},{1,17},{2,18},{3,19},{4,20},{5,21},{6,22},{7,23},{8,24},{9,... | collective-permute-start | bytes 786440 | tf_op jit(solution)/shard_map/ppermute | solution.py:82
  54.2 1.6 %collective-permute-start.25 = (bf16[2,32,512]{2,1,0:T(8,128)(2,1)S(1)}, bf16[2,32,512]{2,1,0:T(8,128)(2,1)S(1)}, u32[]{:S(2)}, u32[]{:S(2)}) collective-permute-start(bf16[2,32,512]{2,1,0:T(8,128)(2,1)S(1)} %get-tuple-element.48), channel_id=1, source_target_pairs={{0,5},{1,4},{2,7},{3,6},{4,1},{5,0},{6,3},{7,2},{8,13},{9,12},{10,... | collective-permute-start | bytes 196616 | tf_op jit(solution)/shard_map/ppermute | solution.py:82
  56.8 1.7 %collective-permute-done.25.refs_3_ = bf16[2,32,512]{2,1,0:T(8,128)(2,1)S(1)} collective-permute-done((bf16[2,32,512]{2,1,0:T(8,128)(2,1)S(1)}, bf16[2,32,512]{2,1,0:T(8,128)(2,1)S(1)}, u32[]{:S(2)}, u32[]{:S(2)}) %collective-permute-start.25) | collective-permute-done | bytes 65568 | tf_op jit(solution)/shard_map/ppermute | solution.py:82
  61.1 1.9 %collective-permute-start.28 = (bf16[32,512]{1,0:T(8,128)(2,1)S(1)}, bf16[32,512]{1,0:T(8,128)(2,1)S(1)}, u32[]{:S(2)}, u32[]{:S(2)}) collective-permute-start(bf16[32,512]{1,0:T(8,128)(2,1)S(1)} %get-tuple-element.50), channel_id=1, source_target_pairs={{0,24},{1,25},{2,26},{3,27},{4,28},{5,29},{6,30},{7,31},{8,16},{9,... | collective-permute-start | bytes 98312 | tf_op jit(solution)/shard_map/ppermute | solution.py:82
  63.0 4.2 %collective-permute-done.27.refs_2_ = bf16[32,512]{1,0:T(8,128)(2,1)S(1)} collective-permute-done((bf16[32,512]{1,0:T(8,128)(2,1)S(1)}, bf16[32,512]{1,0:T(8,128)(2,1)S(1)}, u32[]{:S(2)}, u32[]{:S(2)}) %collective-permute-start.27) | collective-permute-done | bytes 32800 | tf_op jit(solution)/shard_map/ppermute | solution.py:82
  67.3 1.8 %collective-permute-start.29 = (f32[8,512]{1,0:T(8,128)S(1)}, f32[8,512]{1,0:T(8,128)S(1)}, u32[]{:S(2)}, u32[]{:S(2)}) collective-permute-start(f32[8,512]{1,0:T(8,128)S(1)} %get-tuple-element.51.refs_0_), channel_id=1, source_target_pairs={{0,2},{1,3},{2,0},{3,1},{4,6},{5,7},{6,4},{7,5},{8,10},{9,11},{10,... | collective-permute-start | bytes 49160 | tf_op jit(solution)/shard_map/ppermute | solution.py:82
  70.0 1.5 %collective-permute-start.32 = (f32[8,512]{1,0:T(8,128)S(1)}, f32[8,512]{1,0:T(8,128)S(1)}, u32[]{:S(2)}, u32[]{:S(2)}) collective-permute-start(f32[8,512]{1,0:T(8,128)S(1)} %add_sums.1.refs_2_), channel_id=1, source_target_pairs={{0,12},{1,13},{2,14},{3,15},{4,8},{5,9},{6,10},{7,11},{8,4},{9,5},... | collective-permute-start | bytes 49160 | tf_op jit(solution)/shard_map/ppermute | solution.py:82
  75.6 2.4 %collective-permute-start.33 = (bf16[272,512]{1,0:T(8,128)(2,1)S(1)}, bf16[272,512]{1,0:T(8,128)(2,1)S(1)}, u32[]{:S(2)}, u32[]{:S(2)}) collective-permute-start(bf16[272,512]{1,0:T(8,128)(2,1)S(1)} %get-tuple-element.53.refs_0_), channel_id=1, source_target_pairs={{0,16},{1,17},{2,18},{3,19},{4,20},{5,21},{6,22},{7,23},{8,24},{9,... | collective-permute-start | bytes 835592 | tf_op jit(solution)/shard_map/ppermute | solution.py:82
  78.7 1.5 %collective-permute-start.39 = (bf16[272,512]{1,0:T(8,128)(2,1)S(1)}, bf16[272,512]{1,0:T(8,128)(2,1)S(1)}, u32[]{:S(2)}, u32[]{:S(2)}) collective-permute-start(bf16[272,512]{1,0:T(8,128)(2,1)S(1)} %get-tuple-element.53.refs_0_), channel_id=1, source_target_pairs={{0,4},{1,5},{2,6},{3,7},{4,0},{5,1},{6,2},{7,3},{8,12},{9,13},{10,... | collective-permute-start | bytes 835592 | tf_op jit(solution)/shard_map/ppermute | solution.py:82
  80.1 2.7 %collective-permute-start.38 = (bf16[272,512]{1,0:T(8,128)(2,1)S(1)}, bf16[272,512]{1,0:T(8,128)(2,1)S(1)}, u32[]{:S(2)}, u32[]{:S(2)}) collective-permute-start(bf16[272,512]{1,0:T(8,128)(2,1)S(1)} %get-tuple-element.53.refs_0_), channel_id=1, source_target_pairs={{0,2},{1,3},{2,0},{3,1},{4,6},{5,7},{6,4},{7,5},{8,10},{9,11},{10,... | collective-permute-start | bytes 835592 | tf_op jit(solution)/shard_map/ppermute | solution.py:82
  82.8 7.8 %collective-permute-done.33.refs_8_ = bf16[272,512]{1,0:T(8,128)(2,1)S(1)} collective-permute-done((bf16[272,512]{1,0:T(8,128)(2,1)S(1)}, bf16[272,512]{1,0:T(8,128)(2,1)S(1)}, u32[]{:S(2)}, u32[]{:S(2)}) %collective-permute-start.33) | collective-permute-done | bytes 278560 | tf_op jit(solution)/shard_map/ppermute | solution.py:82
  90.6 1.4 %collective-permute-start.43 = (bf16[272,512]{1,0:T(8,128)(2,1)S(1)}, bf16[272,512]{1,0:T(8,128)(2,1)S(1)}, u32[]{:S(2)}, u32[]{:S(2)}) collective-permute-start(bf16[272,512]{1,0:T(8,128)(2,1)S(1)} %collective-permute-done.41.refs_4_), channel_id=1, source_target_pairs={{0,4},{1,5},{2,6},{3,7},{4,0},{5,1},{6,2},{7,3},{8,12},{9,13},{10,... | collective-permute-start | bytes 835592 | tf_op jit(solution)/shard_map/ppermute | solution.py:82
  92.0 2.1 %collective-permute-start.42 = (bf16[272,512]{1,0:T(8,128)(2,1)S(1)}, bf16[272,512]{1,0:T(8,128)(2,1)S(1)}, u32[]{:S(2)}, u32[]{:S(2)}) collective-permute-start(bf16[272,512]{1,0:T(8,128)(2,1)S(1)} %collective-permute-done.41.refs_4_), channel_id=1, source_target_pairs={{0,2},{1,3},{2,0},{3,1},{4,6},{5,7},{6,4},{7,5},{8,10},{9,11},{10,... | collective-permute-start | bytes 835592 | tf_op jit(solution)/shard_map/ppermute | solution.py:82
  94.5 3.2 %collective-permute-done.34.refs_0_ = bf16[272,512]{1,0:T(8,128)(2,1)S(1)} collective-permute-done((bf16[272,512]{1,0:T(8,128)(2,1)S(1)}, bf16[272,512]{1,0:T(8,128)(2,1)S(1)}, u32[]{:S(2)}, u32[]{:S(2)}) %collective-permute-start.34) | collective-permute-done | bytes 278560 | tf_op jit(solution)/shard_map/ppermute | solution.py:82
  97.7 1.4 %collective-permute-start.36 = (bf16[272,512]{1,0:T(8,128)(2,1)S(1)}, bf16[272,512]{1,0:T(8,128)(2,1)S(1)}, u32[]{:S(2)}, u32[]{:S(2)}) collective-permute-start(bf16[272,512]{1,0:T(8,128)(2,1)S(1)} %collective-permute-done.34.refs_0_), channel_id=1, source_target_pairs={{0,4},{1,5},{2,6},{3,7},{4,0},{5,1},{6,2},{7,3},{8,12},{9,13},{10,... | collective-permute-start | bytes 835592 | tf_op jit(solution)/shard_map/ppermute | solution.py:82
  99.1 3.0 %collective-permute-start.45 = (bf16[272,512]{1,0:T(8,128)(2,1)S(1)}, bf16[272,512]{1,0:T(8,128)(2,1)S(1)}, u32[]{:S(2)}, u32[]{:S(2)}) collective-permute-start(bf16[272,512]{1,0:T(8,128)(2,1)S(1)} %collective-permute-done.33.refs_8_), channel_id=1, source_target_pairs={{0,2},{1,3},{2,0},{3,1},{4,6},{5,7},{6,4},{7,5},{8,10},{9,11},{10,... | collective-permute-start | bytes 835592 | tf_op jit(solution)/shard_map/ppermute | solution.py:82
  102.9 5.2 %collective-permute-start.47 = (bf16[272,512]{1,0:T(8,128)(2,1)S(1)}, bf16[272,512]{1,0:T(8,128)(2,1)S(1)}, u32[]{:S(2)}, u32[]{:S(2)}) collective-permute-start(bf16[272,512]{1,0:T(8,128)(2,1)S(1)} %collective-permute-done.46.refs_10_), channel_id=1, source_target_pairs={{0,2},{1,3},{2,0},{3,1},{4,6},{5,7},{6,4},{7,5},{8,10},{9,11},{10,... | collective-permute-start | bytes 835592 | tf_op jit(solution)/shard_map/ppermute | solution.py:82
  108.8 2.8 %collective-permute-start.37 = (bf16[272,512]{1,0:T(8,128)(2,1)S(1)}, bf16[272,512]{1,0:T(8,128)(2,1)S(1)}, u32[]{:S(2)}, u32[]{:S(2)}) collective-permute-start(bf16[272,512]{1,0:T(8,128)(2,1)S(1)} %collective-permute-done.36.refs_2_), channel_id=1, source_target_pairs={{0,2},{1,3},{2,0},{3,1},{4,6},{5,7},{6,4},{7,5},{8,10},{9,11},{10,... | collective-permute-start | bytes 835592 | tf_op jit(solution)/shard_map/ppermute | solution.py:82
  111.6 1.8 %lay.2 = (bf16[4096,512]{1,0:T(8,128)(2,1)}, bf16[4,4096]{1,0:T(4,128)(2,1)S(1)}) custom-call(bf16[272,512]{1,0:T(8,128)(2,1)S(1)} %get-tuple-element.53.refs_0_, bf16[272,512]{1,0:T(8,128)(2,1)S(1)} %collective-permute-done.38.refs_1_, bf16[272,512]{1,0:T(8,128)(2,1)S(1)} %collective-permute-done.39.refs_2_, ...), custom_call_target="tpu_custom_call" | custom-call | bytes 1 | tf_op jit(solution)/shard_map/lay/pallas_call | solution.py:387
  113.4 1.6 %lay.3 = (bf16[4096,512]{1,0:T(8,128)(2,1)}, bf16[4,4096]{1,0:T(4,128)(2,1)}) custom-call(bf16[272,512]{1,0:T(8,128)(2,1)S(1)} %collective-permute-done.34.refs_0_, bf16[272,512]{1,0:T(8,128)(2,1)S(1)} %collective-permute-done.35.refs_1_, bf16[272,512]{1,0:T(8,128)(2,1)S(1)} %collective-permute-done.36.refs_2_, ...), custom_call_target="tpu_custom_call", output_to_operand_aliasing={{0}: (4, {})} | custom-call | bytes 1 | tf_op jit(solution)/shard_map/lay/pallas_call | solution.py:387
  (100 shorter events, 28.4 us)
Async XLA Ops:
  5.4 7.8 %collective-permute-start.4 = (bf16[2,2,2,2,256,128]{5,4,3,2,1,0:T(8,128)(2,1)S(1)}, bf16[2,2,2,2,256,128]{5,4,3,2,1,0:T(8,128)(2,1)S(1)}, u32[]{:S(2)}, u32[]{:S(2)}) collective-permute-start(bf16[2,2,2,2,256,128]{5,4,3,2,1,0:T(8,128)(2,1)S(1)} %get-tuple-element.36), channel_id=1, source_target_pairs={{0,2},{1,3},{2,0},{3,1},{4,6},{5,7},{6,4},{7,5},{8,10},{9,11},{10,... | collective-permute-start | bytes 3145736 | tf_op jit(solution)/shard_map/ppermute | solution.py:82
  5.9 8.7 %collective-permute-start = (bf16[2,2,2,2,256,128]{5,4,3,2,1,0:T(8,128)(2,1)S(1)}, bf16[2,2,2,2,256,128]{5,4,3,2,1,0:T(8,128)(2,1)S(1)}, u32[]{:S(2)}, u32[]{:S(2)}) collective-permute-start(bf16[2,2,2,2,256,128]{5,4,3,2,1,0:T(8,128)(2,1)S(1)} %get-tuple-element.34), channel_id=1, source_target_pairs={{0,2},{1,3},{2,0},{3,1},{4,6},{5,7},{6,4},{7,5},{8,10},{9,11},{10,... | collective-permute-start | bytes 3145736 | tf_op jit(solution)/shard_map/ppermute | solution.py:82
  5.9 10.1 %collective-permute-start.16 = (bf16[2,2,2,2,128,128]{5,4,3,2,1,0:T(8,128)(2,1)S(1)}, bf16[2,2,2,2,128,128]{5,4,3,2,1,0:T(8,128)(2,1)S(1)}, u32[]{:S(2)}, u32[]{:S(2)}) collective-permute-start(bf16[2,2,2,2,128,128]{5,4,3,2,1,0:T(8,128)(2,1)S(1)} %get-tuple-element.42), channel_id=1, source_target_pairs={{0,2},{1,3},{2,0},{3,1},{4,6},{5,7},{6,4},{7,5},{8,10},{9,11},{10,... | collective-permute-start | bytes 1572872 | tf_op jit(solution)/shard_map/ppermute | solution.py:82
  6.4 9.9 %collective-permute-start.12 = (bf16[2,2,2,2,128,128]{5,4,3,2,1,0:T(8,128)(2,1)S(1)}, bf16[2,2,2,2,128,128]{5,4,3,2,1,0:T(8,128)(2,1)S(1)}, u32[]{:S(2)}, u32[]{:S(2)}) collective-permute-start(bf16[2,2,2,2,128,128]{5,4,3,2,1,0:T(8,128)(2,1)S(1)} %get-tuple-element.40), channel_id=1, source_target_pairs={{0,2},{1,3},{2,0},{3,1},{4,6},{5,7},{6,4},{7,5},{8,10},{9,11},{10,... | collective-permute-start | bytes 1572872 | tf_op jit(solution)/shard_map/ppermute | solution.py:82
  10.4 15.0 %collective-permute-start.9 = (bf16[2,2,2,256,128]{4,3,2,1,0:T(8,128)(2,1)S(1)}, bf16[2,2,2,256,128]{4,3,2,1,0:T(8,128)(2,1)S(1)}, u32[]{:S(2)}, u32[]{:S(2)}) collective-permute-start(bf16[2,2,2,256,128]{4,3,2,1,0:T(8,128)(2,1)S(1)} %fold_w.7), channel_id=1, source_target_pairs={{0,8},{1,9},{2,10},{3,11},{4,12},{5,13},{6,14},{7,15},{8,0},{9,1},... | collective-permute-start | bytes 1572872 | tf_op jit(solution)/shard_map/ppermute | solution.py:82
  13.3 13.5 %collective-permute-start.5 = (bf16[2,2,2,256,128]{4,3,2,1,0:T(8,128)(2,1)S(1)}, bf16[2,2,2,256,128]{4,3,2,1,0:T(8,128)(2,1)S(1)}, u32[]{:S(2)}, u32[]{:S(2)}) collective-permute-start(bf16[2,2,2,256,128]{4,3,2,1,0:T(8,128)(2,1)S(1)} %fold_y.6), channel_id=1, source_target_pairs={{0,1},{1,0},{2,3},{3,2},{4,5},{5,4},{6,7},{7,6},{8,9},{9,8},{10,11... | collective-permute-start | bytes 1572872 | tf_op jit(solution)/shard_map/ppermute | solution.py:82
  14.7 13.5 %collective-permute-start.1 = (bf16[2,2,2,256,128]{4,3,2,1,0:T(8,128)(2,1)S(1)}, bf16[2,2,2,256,128]{4,3,2,1,0:T(8,128)(2,1)S(1)}, u32[]{:S(2)}, u32[]{:S(2)}) collective-permute-start(bf16[2,2,2,256,128]{4,3,2,1,0:T(8,128)(2,1)S(1)} %fold_x.5), channel_id=1, source_target_pairs={{0,4},{1,5},{2,6},{3,7},{4,0},{5,1},{6,2},{7,3},{8,12},{9,13},{10,... | collective-permute-start | bytes 1572872 | tf_op jit(solution)/shard_map/ppermute | solution.py:82
  16.1 14.9 %collective-permute-start.17 = (bf16[2,2,2,128,128]{4,3,2,1,0:T(8,128)(2,1)S(1)}, bf16[2,2,2,128,128]{4,3,2,1,0:T(8,128)(2,1)S(1)}, u32[]{:S(2)}, u32[]{:S(2)}) collective-permute-start(bf16[2,2,2,128,128]{4,3,2,1,0:T(8,128)(2,1)S(1)} %fold_w.9), channel_id=1, source_target_pairs={{0,8},{1,9},{2,10},{3,11},{4,12},{5,13},{6,14},{7,15},{8,0},{9,1},... | collective-permute-start | bytes 786440 | tf_op jit(solution)/shard_map/ppermute | solution.py:82
  16.4 16.0 %collective-permute-start.13 = (bf16[2,2,2,128,128]{4,3,2,1,0:T(8,128)(2,1)S(1)}, bf16[2,2,2,128,128]{4,3,2,1,0:T(8,128)(2,1)S(1)}, u32[]{:S(2)}, u32[]{:S(2)}) collective-permute-start(bf16[2,2,2,128,128]{4,3,2,1,0:T(8,128)(2,1)S(1)} %fold_y.8), channel_id=1, source_target_pairs={{0,1},{1,0},{2,3},{3,2},{4,5},{5,4},{6,7},{7,6},{8,9},{9,8},{10,11... | collective-permute-start | bytes 786440 | tf_op jit(solution)/shard_map/ppermute | solution.py:82
  25.5 9.3 %collective-permute-start.10 = (bf16[2,2,256,128]{3,2,1,0:T(8,128)(2,1)S(1)}, bf16[2,2,256,128]{3,2,1,0:T(8,128)(2,1)S(1)}, u32[]{:S(2)}, u32[]{:S(2)}) collective-permute-start(bf16[2,2,256,128]{3,2,1,0:T(8,128)(2,1)S(1)} %fold_x.7), channel_id=1, source_target_pairs={{0,4},{1,5},{2,6},{3,7},{4,0},{5,1},{6,2},{7,3},{8,12},{9,13},{10,... | collective-permute-start | bytes 786440 | tf_op jit(solution)/shard_map/ppermute | solution.py:82
  26.9 11.1 %collective-permute-start.6 = (bf16[2,2,256,128]{3,2,1,0:T(8,128)(2,1)S(1)}, bf16[2,2,256,128]{3,2,1,0:T(8,128)(2,1)S(1)}, u32[]{:S(2)}, u32[]{:S(2)}) collective-permute-start(bf16[2,2,256,128]{3,2,1,0:T(8,128)(2,1)S(1)} %fold_w.6), channel_id=1, source_target_pairs={{0,8},{1,9},{2,10},{3,11},{4,12},{5,13},{6,14},{7,15},{8,0},{9,1},... | collective-permute-start | bytes 786440 | tf_op jit(solution)/shard_map/ppermute | solution.py:82
  28.4 12.0 %collective-permute-start.2 = (bf16[2,2,256,128]{3,2,1,0:T(8,128)(2,1)S(1)}, bf16[2,2,256,128]{3,2,1,0:T(8,128)(2,1)S(1)}, u32[]{:S(2)}, u32[]{:S(2)}) collective-permute-start(bf16[2,2,256,128]{3,2,1,0:T(8,128)(2,1)S(1)} %fold_y.5), channel_id=1, source_target_pairs={{0,1},{1,0},{2,3},{3,2},{4,5},{5,4},{6,7},{7,6},{8,9},{9,8},{10,11... | collective-permute-start | bytes 786440 | tf_op jit(solution)/shard_map/ppermute | solution.py:82
  31.1 10.6 %collective-permute-start.18 = (bf16[2,2,128,128]{3,2,1,0:T(8,128)(2,1)S(1)}, bf16[2,2,128,128]{3,2,1,0:T(8,128)(2,1)S(1)}, u32[]{:S(2)}, u32[]{:S(2)}) collective-permute-start(bf16[2,2,128,128]{3,2,1,0:T(8,128)(2,1)S(1)} %fold_x.9), channel_id=1, source_target_pairs={{0,4},{1,5},{2,6},{3,7},{4,0},{5,1},{6,2},{7,3},{8,12},{9,13},{10,... | collective-permute-start | bytes 393224 | tf_op jit(solution)/shard_map/ppermute | solution.py:82
  32.4 11.1 %collective-permute-start.20 = (bf16[320,256]{1,0:T(8,128)(2,1)S(1)}, bf16[320,256]{1,0:T(8,128)(2,1)S(1)}, u32[]{:S(2)}, u32[]{:S(2)}) collective-permute-start(bf16[320,256]{1,0:T(8,128)(2,1)S(1)} %pack.1.refs_25_.refs_4_), channel_id=1, source_target_pairs={{0,16},{1,17},{2,18},{3,19},{4,20},{5,21},{6,22},{7,23},{8,24},{9,... | collective-permute-start | bytes 491528 | tf_op jit(solution)/shard_map/ppermute | solution.py:82
  34.8 7.1 %collective-permute-start.14 = (bf16[2,2,128,128]{3,2,1,0:T(8,128)(2,1)S(1)}, bf16[2,2,128,128]{3,2,1,0:T(8,128)(2,1)S(1)}, u32[]{:S(2)}, u32[]{:S(2)}) collective-permute-start(bf16[2,2,128,128]{3,2,1,0:T(8,128)(2,1)S(1)} %fold_w.8), channel_id=1, source_target_pairs={{0,8},{1,9},{2,10},{3,11},{4,12},{5,13},{6,14},{7,15},{8,0},{9,1},... | collective-permute-start | bytes 393224 | tf_op jit(solution)/shard_map/ppermute | solution.py:82
  38.0 9.6 %collective-permute-start.11 = (bf16[2,256,128]{2,1,0:T(8,128)(2,1)S(1)}, bf16[2,256,128]{2,1,0:T(8,128)(2,1)S(1)}, u32[]{:S(2)}, u32[]{:S(2)}) collective-permute-start(bf16[2,256,128]{2,1,0:T(8,128)(2,1)S(1)} %fold_y.7), channel_id=1, source_target_pairs={{0,1},{1,0},{2,3},{3,2},{4,5},{5,4},{6,7},{7,6},{8,9},{9,8},{10,11... | collective-permute-start | bytes 393224 | tf_op jit(solution)/shard_map/ppermute | solution.py:82
  40.3 7.3 %collective-permute-start.7 = (bf16[2,256,128]{2,1,0:T(8,128)(2,1)S(1)}, bf16[2,256,128]{2,1,0:T(8,128)(2,1)S(1)}, u32[]{:S(2)}, u32[]{:S(2)}) collective-permute-start(bf16[2,256,128]{2,1,0:T(8,128)(2,1)S(1)} %fold_x.6), channel_id=1, source_target_pairs={{0,4},{1,5},{2,6},{3,7},{4,0},{5,1},{6,2},{7,3},{8,12},{9,13},{10,... | collective-permute-start | bytes 393224 | tf_op jit(solution)/shard_map/ppermute | solution.py:82
  50.9 21.8 %collective-permute-start.21 = (bf16[256,512]{1,0:T(8,128)(2,1)S(1)}, bf16[256,512]{1,0:T(8,128)(2,1)S(1)}, u32[]{:S(2)}, u32[]{:S(2)}) collective-permute-start(bf16[256,512]{1,0:T(8,128)(2,1)S(1)} %get-tuple-element.44), channel_id=1, source_target_pairs={{0,16},{1,17},{2,18},{3,19},{4,20},{5,21},{6,22},{7,23},{8,24},{9,... | collective-permute-start | bytes 786440 | tf_op jit(solution)/shard_map/ppermute | solution.py:82
  59.9 7.4 %collective-permute-start.27 = (bf16[32,512]{1,0:T(8,128)(2,1)S(1)}, bf16[32,512]{1,0:T(8,128)(2,1)S(1)}, u32[]{:S(2)}, u32[]{:S(2)}) collective-permute-start(bf16[32,512]{1,0:T(8,128)(2,1)S(1)} %get-tuple-element.49.refs_0_), channel_id=1, source_target_pairs={{0,16},{1,17},{2,18},{3,19},{4,20},{5,21},{6,22},{7,23},{8,24},{9,... | collective-permute-start | bytes 98312 | tf_op jit(solution)/shard_map/ppermute | solution.py:82
  75.6 15.0 %collective-permute-start.33 = (bf16[272,512]{1,0:T(8,128)(2,1)S(1)}, bf16[272,512]{1,0:T(8,128)(2,1)S(1)}, u32[]{:S(2)}, u32[]{:S(2)}) collective-permute-start(bf16[272,512]{1,0:T(8,128)(2,1)S(1)} %get-tuple-element.53.refs_0_), channel_id=1, source_target_pairs={{0,16},{1,17},{2,18},{3,19},{4,20},{5,21},{6,22},{7,23},{8,24},{9,... | collective-permute-start | bytes 835592 | tf_op jit(solution)/shard_map/ppermute | solution.py:82
  78.0 12.6 %collective-permute-start.41 = (bf16[272,512]{1,0:T(8,128)(2,1)S(1)}, bf16[272,512]{1,0:T(8,128)(2,1)S(1)}, u32[]{:S(2)}, u32[]{:S(2)}) collective-permute-start(bf16[272,512]{1,0:T(8,128)(2,1)S(1)} %get-tuple-element.53.refs_0_), channel_id=1, source_target_pairs={{0,8},{1,9},{2,10},{3,11},{4,12},{5,13},{6,14},{7,15},{8,0},{9,1},... | collective-permute-start | bytes 835592 | tf_op jit(solution)/shard_map/ppermute | solution.py:82
  78.7 15.5 %collective-permute-start.39 = (bf16[272,512]{1,0:T(8,128)(2,1)S(1)}, bf16[272,512]{1,0:T(8,128)(2,1)S(1)}, u32[]{:S(2)}, u32[]{:S(2)}) collective-permute-start(bf16[272,512]{1,0:T(8,128)(2,1)S(1)} %get-tuple-element.53.refs_0_), channel_id=1, source_target_pairs={{0,4},{1,5},{2,6},{3,7},{4,0},{5,1},{6,2},{7,3},{8,12},{9,13},{10,... | collective-permute-start | bytes 835592 | tf_op jit(solution)/shard_map/ppermute | solution.py:82
  80.1 14.1 %collective-permute-start.38 = (bf16[272,512]{1,0:T(8,128)(2,1)S(1)}, bf16[272,512]{1,0:T(8,128)(2,1)S(1)}, u32[]{:S(2)}, u32[]{:S(2)}) collective-permute-start(bf16[272,512]{1,0:T(8,128)(2,1)S(1)} %get-tuple-element.53.refs_0_), channel_id=1, source_target_pairs={{0,2},{1,3},{2,0},{3,1},{4,6},{5,7},{6,4},{7,5},{8,10},{9,11},{10,... | collective-permute-start | bytes 835592 | tf_op jit(solution)/shard_map/ppermute | solution.py:82
  90.6 7.1 %collective-permute-start.34 = (bf16[272,512]{1,0:T(8,128)(2,1)S(1)}, bf16[272,512]{1,0:T(8,128)(2,1)S(1)}, u32[]{:S(2)}, u32[]{:S(2)}) collective-permute-start(bf16[272,512]{1,0:T(8,128)(2,1)S(1)} %collective-permute-done.33.refs_8_), channel_id=1, source_target_pairs={{0,8},{1,9},{2,10},{3,11},{4,12},{5,13},{6,14},{7,15},{8,0},{9,1},... | collective-permute-start | bytes 835592 | tf_op jit(solution)/shard_map/ppermute | solution.py:82
  90.6 8.5 %collective-permute-start.43 = (bf16[272,512]{1,0:T(8,128)(2,1)S(1)}, bf16[272,512]{1,0:T(8,128)(2,1)S(1)}, u32[]{:S(2)}, u32[]{:S(2)}) collective-permute-start(bf16[272,512]{1,0:T(8,128)(2,1)S(1)} %collective-permute-done.41.refs_4_), channel_id=1, source_target_pairs={{0,4},{1,5},{2,6},{3,7},{4,0},{5,1},{6,2},{7,3},{8,12},{9,13},{10,... | collective-permute-start | bytes 835592 | tf_op jit(solution)/shard_map/ppermute | solution.py:82
  92.0 10.1 %collective-permute-start.42 = (bf16[272,512]{1,0:T(8,128)(2,1)S(1)}, bf16[272,512]{1,0:T(8,128)(2,1)S(1)}, u32[]{:S(2)}, u32[]{:S(2)}) collective-permute-start(bf16[272,512]{1,0:T(8,128)(2,1)S(1)} %collective-permute-done.41.refs_4_), channel_id=1, source_target_pairs={{0,2},{1,3},{2,0},{3,1},{4,6},{5,7},{6,4},{7,5},{8,10},{9,11},{10,... | collective-permute-start | bytes 835592 | tf_op jit(solution)/shard_map/ppermute | solution.py:82
  94.2 8.7 %collective-permute-start.46 = (bf16[272,512]{1,0:T(8,128)(2,1)S(1)}, bf16[272,512]{1,0:T(8,128)(2,1)S(1)}, u32[]{:S(2)}, u32[]{:S(2)}) collective-permute-start(bf16[272,512]{1,0:T(8,128)(2,1)S(1)} %collective-permute-done.33.refs_8_), channel_id=1, source_target_pairs={{0,4},{1,5},{2,6},{3,7},{4,0},{5,1},{6,2},{7,3},{8,12},{9,13},{10,... | collective-permute-start | bytes 835592 | tf_op jit(solution)/shard_map/ppermute | solution.py:82
  94.2 13.8 %collective-permute-start.40 = (bf16[272,512]{1,0:T(8,128)(2,1)S(1)}, bf16[272,512]{1,0:T(8,128)(2,1)S(1)}, u32[]{:S(2)}, u32[]{:S(2)}) collective-permute-start(bf16[272,512]{1,0:T(8,128)(2,1)S(1)} %collective-permute-done.39.refs_2_), channel_id=1, source_target_pairs={{0,2},{1,3},{2,0},{3,1},{4,6},{5,7},{6,4},{7,5},{8,10},{9,11},{10,... | collective-permute-start | bytes 835592 | tf_op jit(solution)/shard_map/ppermute | solution.py:82
  97.7 11.1 %collective-permute-start.36 = (bf16[272,512]{1,0:T(8,128)(2,1)S(1)}, bf16[272,512]{1,0:T(8,128)(2,1)S(1)}, u32[]{:S(2)}, u32[]{:S(2)}) collective-permute-start(bf16[272,512]{1,0:T(8,128)(2,1)S(1)} %collective-permute-done.34.refs_0_), channel_id=1, source_target_pairs={{0,4},{1,5},{2,6},{3,7},{4,0},{5,1},{6,2},{7,3},{8,12},{9,13},{10,... | collective-permute-start | bytes 835592 | tf_op jit(solution)/shard_map/ppermute | solution.py:82
  99.1 12.5 %collective-permute-start.45 = (bf16[272,512]{1,0:T(8,128)(2,1)S(1)}, bf16[272,512]{1,0:T(8,128)(2,1)S(1)}, u32[]{:S(2)}, u32[]{:S(2)}) collective-permute-start(bf16[272,512]{1,0:T(8,128)(2,1)S(1)} %collective-permute-done.33.refs_8_), channel_id=1, source_target_pairs={{0,2},{1,3},{2,0},{3,1},{4,6},{5,7},{6,4},{7,5},{8,10},{9,11},{10,... | collective-permute-start | bytes 835592 | tf_op jit(solution)/shard_map/ppermute | solution.py:82
  102.1 9.5 %collective-permute-start.44 = (bf16[272,512]{1,0:T(8,128)(2,1)S(1)}, bf16[272,512]{1,0:T(8,128)(2,1)S(1)}, u32[]{:S(2)}, u32[]{:S(2)}) collective-permute-start(bf16[272,512]{1,0:T(8,128)(2,1)S(1)} %collective-permute-done.43.refs_6_), channel_id=1, source_target_pairs={{0,2},{1,3},{2,0},{3,1},{4,6},{5,7},{6,4},{7,5},{8,10},{9,11},{10,... | collective-permute-start | bytes 835592 | tf_op jit(solution)/shard_map/ppermute | solution.py:82
  102.9 8.8 %collective-permute-start.47 = (bf16[272,512]{1,0:T(8,128)(2,1)S(1)}, bf16[272,512]{1,0:T(8,128)(2,1)S(1)}, u32[]{:S(2)}, u32[]{:S(2)}) collective-permute-start(bf16[272,512]{1,0:T(8,128)(2,1)S(1)} %collective-permute-done.46.refs_10_), channel_id=1, source_target_pairs={{0,2},{1,3},{2,0},{3,1},{4,6},{5,7},{6,4},{7,5},{8,10},{9,11},{10,... | collective-permute-start | bytes 835592 | tf_op jit(solution)/shard_map/ppermute | solution.py:82
  (21 other events, 120.6 us)

commit v4 on v3

--- a/solution.py
+++ b/solution.py
@@ -12,7 +12,7 @@
 bias_second = 1.0 - 0.999**10
 AXES = ("node", "local")
 PIECES = ((0, 4, 0, 1), (1, 4, 0, 1), (2, 4, 0, 1), (3, 4, 0, 2), (3, 4, 1, 2))
-ORDERS = ("xyw", "ywx", "wxy", "ywx", "wxy")
+ORDERS = ("xyw", "ywx", "wxy", "wyx", "yxw")
 PAD = 16
 ALL = slice(None)
 MIB = 2**20

time: 115 us -> 114 us (level)
  starting transfers between devices: 61.1 us -> 57.6 us
  waiting for transfers between devices: 38 us -> 40.4 us
    ppermute x48, starting transfers between devices: 61.1 us -> 57.6 us  [send(): return lax.ppermute(array, AXES, pairs)]
    ppermute x48, waiting for transfers between devices: 38 us -> 40.4 us  [send(): return lax.ppermute(array, AXES, pairs)]
  transfers between devices with their start and end apart: 48 -> 48, of which waited for: 17 -> 15; matrix products, arithmetic and copies ran while one was open for 0% -> 0% of each run, Pallas kernels for 6% -> 6%
where the time goes in v4:
time: 114 us
  starting transfers between devices  57.6 us (51%)
  waiting for transfers between devices  40.4 us (35%)
  Pallas kernels  14.1 us (12%)
    ppermute x48, starting transfers between devices, send(): return lax.ppermute(array, AXES, pairs)  57.6 us
    ppermute x48, waiting for transfers between devices, send(): return lax.ppermute(array, AXES, pairs)  40.4 us
    pallas_call x2, Pallas kernels, dequant(): pl.pallas_call(kernel, out_shape=[pltpu.VMEM(shape, bf16) for shape in sh...  7.49 us
    pallas_call x2, Pallas kernels, lay(): pl.pallas_call(kernel, out_shape=[pltpu.HBM((grid.nodes * rows, columns),...  3.42 us
    pallas_call x22, Pallas kernels, call(): pl.pallas_call(kernel, out_shape=outs, in_specs=[pl.BlockSpec(memory_spac...  3.2 us
  transfers between devices with their start and end apart: 48, of which 15 were waited for; matrix products, arithmetic and copies ran while one was open for 0% of the time, Pallas kernels for 6%

profile of v4, /device:TPU:1, one launch (start us, length us, event | category | flops | bytes accessed | tf_op | source)
XLA Modules:
  0.0 113.9 jit_solution(1332342107382497787)
XLA Ops:
  1.5 3.7 %dequant.3 = (bf16[2,2,2,2,256,128]{5,4,3,2,1,0:T(8,128)(2,1)S(1)}, bf16[2,2,2,2,256,128]{5,4,3,2,1,0:T(8,128)(2,1)S(1)}, bf16[2,2,2,2,256,128]{5,4,3,2,1,0:T(8,...) custom-call(s32[4,8192]{1,0:T(4,128)S(1)} %bitcast.2, ...), custom_call_target="tpu_custom_call" | custom-call | bytes 1 | tf_op jit(solution)/shard_map/dequant/pallas_call | solution.py:143
  6.5 3.7 %dequant.2 = (bf16[2,2,2,2,256,128]{5,4,3,2,1,0:T(8,128)(2,1)S(1)}, bf16[2,2,2,2,256,128]{5,4,3,2,1,0:T(8,128)(2,1)S(1)}, bf16[2,2,2,2,256,128]{5,4,3,2,1,0:T(8,...) custom-call(s32[4,8192]{1,0:T(4,128)S(1)} %bitcast.3, ...), custom_call_target="tpu_custom_call" | custom-call | bytes 1 | tf_op jit(solution)/shard_map/dequant/pallas_call | solution.py:143
  10.4 2.8 %collective-permute-start.9 = (bf16[2,2,2,256,128]{4,3,2,1,0:T(8,128)(2,1)S(1)}, bf16[2,2,2,256,128]{4,3,2,1,0:T(8,128)(2,1)S(1)}, u32[]{:S(2)}, u32[]{:S(2)}) collective-permute-start(bf16[2,2,2,256,128]{4,3,2,1,0:T(8,128)(2,1)S(1)} %fold_w.7), channel_id=1, source_target_pairs={{0,8},{1,9},{2,10},{3,11},{4,12},{5,13},{6,14},{7,15},{8,0},{9,1},... | collective-permute-start | bytes 1572872 | tf_op jit(solution)/shard_map/ppermute | solution.py:82
  13.3 1.3 %collective-permute-start.5 = (bf16[2,2,2,256,128]{4,3,2,1,0:T(8,128)(2,1)S(1)}, bf16[2,2,2,256,128]{4,3,2,1,0:T(8,128)(2,1)S(1)}, u32[]{:S(2)}, u32[]{:S(2)}) collective-permute-start(bf16[2,2,2,256,128]{4,3,2,1,0:T(8,128)(2,1)S(1)} %fold_y.6), channel_id=1, source_target_pairs={{0,1},{1,0},{2,3},{3,2},{4,5},{5,4},{6,7},{7,6},{8,9},{9,8},{10,11... | collective-permute-start | bytes 1572872 | tf_op jit(solution)/shard_map/ppermute | solution.py:82
  14.7 1.3 %collective-permute-start.1 = (bf16[2,2,2,256,128]{4,3,2,1,0:T(8,128)(2,1)S(1)}, bf16[2,2,2,256,128]{4,3,2,1,0:T(8,128)(2,1)S(1)}, u32[]{:S(2)}, u32[]{:S(2)}) collective-permute-start(bf16[2,2,2,256,128]{4,3,2,1,0:T(8,128)(2,1)S(1)} %fold_x.5), channel_id=1, source_target_pairs={{0,4},{1,5},{2,6},{3,7},{4,0},{5,1},{6,2},{7,3},{8,12},{9,13},{10,... | collective-permute-start | bytes 1572872 | tf_op jit(solution)/shard_map/ppermute | solution.py:82
  16.7 8.7 %collective-permute-done.9.refs_2_.refs_12_ = bf16[2,2,2,256,128]{4,3,2,1,0:T(8,128)(2,1)S(1)} collective-permute-done((bf16[2,2,2,256,128]{4,3,2,1,0:T(8,128)(2,1)S(1)}, bf16[2,2,2,256,128]{4,3,2,1,0:T(8,128)(2,1)S(1)}, u32[]{:S(2)}, u32[]{:S(2)}) %collective-permute-start.9) | collective-permute-done | bytes 524320 | tf_op jit(solution)/shard_map/ppermute | solution.py:82
  26.9 1.4 %collective-permute-start.6 = (bf16[2,2,256,128]{3,2,1,0:T(8,128)(2,1)S(1)}, bf16[2,2,256,128]{3,2,1,0:T(8,128)(2,1)S(1)}, u32[]{:S(2)}, u32[]{:S(2)}) collective-permute-start(bf16[2,2,256,128]{3,2,1,0:T(8,128)(2,1)S(1)} %fold_w.6), channel_id=1, source_target_pairs={{0,8},{1,9},{2,10},{3,11},{4,12},{5,13},{6,14},{7,15},{8,0},{9,1},... | collective-permute-start | bytes 786440 | tf_op jit(solution)/shard_map/ppermute | solution.py:82
  28.4 1.3 %collective-permute-start.2 = (bf16[2,2,256,128]{3,2,1,0:T(8,128)(2,1)S(1)}, bf16[2,2,256,128]{3,2,1,0:T(8,128)(2,1)S(1)}, u32[]{:S(2)}, u32[]{:S(2)}) collective-permute-start(bf16[2,2,256,128]{3,2,1,0:T(8,128)(2,1)S(1)} %fold_y.5), channel_id=1, source_target_pairs={{0,1},{1,0},{2,3},{3,2},{4,5},{5,4},{6,7},{7,6},{8,9},{9,8},{10,11... | collective-permute-start | bytes 786440 | tf_op jit(solution)/shard_map/ppermute | solution.py:82
  29.7 2.5 %collective-permute-done.17.refs_2_.refs_22_ = bf16[2,2,2,128,128]{4,3,2,1,0:T(8,128)(2,1)S(1)} collective-permute-done((bf16[2,2,2,128,128]{4,3,2,1,0:T(8,128)(2,1)S(1)}, bf16[2,2,2,128,128]{4,3,2,1,0:T(8,128)(2,1)S(1)}, u32[]{:S(2)}, u32[]{:S(2)}) %collective-permute-start.17) | collective-permute-done | bytes 262176 | tf_op jit(solution)/shard_map/ppermute | solution.py:82
  32.2 1.3 %collective-permute-start.18 = (bf16[2,2,128,128]{3,2,1,0:T(8,128)(2,1)S(1)}, bf16[2,2,128,128]{3,2,1,0:T(8,128)(2,1)S(1)}, u32[]{:S(2)}, u32[]{:S(2)}) collective-permute-start(bf16[2,2,128,128]{3,2,1,0:T(8,128)(2,1)S(1)} %fold_x.9), channel_id=1, source_target_pairs={{0,4},{1,5},{2,6},{3,7},{4,0},{5,1},{6,2},{7,3},{8,12},{9,13},{10,... | collective-permute-start | bytes 393224 | tf_op jit(solution)/shard_map/ppermute | solution.py:82
  33.5 2.4 %collective-permute-start.20 = (bf16[320,256]{1,0:T(8,128)(2,1)S(1)}, bf16[320,256]{1,0:T(8,128)(2,1)S(1)}, u32[]{:S(2)}, u32[]{:S(2)}) collective-permute-start(bf16[320,256]{1,0:T(8,128)(2,1)S(1)} %pack.1.refs_25_.refs_4_), channel_id=1, source_target_pairs={{0,16},{1,17},{2,18},{3,19},{4,20},{5,21},{6,22},{7,23},{8,24},{9,... | collective-permute-start | bytes 491528 | tf_op jit(solution)/shard_map/ppermute | solution.py:82
  36.0 1.3 %collective-permute-start.14 = (bf16[2,2,128,128]{3,2,1,0:T(8,128)(2,1)S(1)}, bf16[2,2,128,128]{3,2,1,0:T(8,128)(2,1)S(1)}, u32[]{:S(2)}, u32[]{:S(2)}) collective-permute-start(bf16[2,2,128,128]{3,2,1,0:T(8,128)(2,1)S(1)} %fold_y.8), channel_id=1, source_target_pairs={{0,1},{1,0},{2,3},{3,2},{4,5},{5,4},{6,7},{7,6},{8,9},{9,8},{10,11... | collective-permute-start | bytes 393224 | tf_op jit(solution)/shard_map/ppermute | solution.py:82
  37.9 3.0 %collective-permute-start.7 = (bf16[2,256,128]{2,1,0:T(8,128)(2,1)S(1)}, bf16[2,256,128]{2,1,0:T(8,128)(2,1)S(1)}, u32[]{:S(2)}, u32[]{:S(2)}) collective-permute-start(bf16[2,256,128]{2,1,0:T(8,128)(2,1)S(1)} %fold_x.6), channel_id=1, source_target_pairs={{0,4},{1,5},{2,6},{3,7},{4,0},{5,1},{6,2},{7,3},{8,12},{9,13},{10,... | collective-permute-start | bytes 393224 | tf_op jit(solution)/shard_map/ppermute | solution.py:82
  41.2 1.5 %collective-permute-start.19 = (bf16[2,128,128]{2,1,0:T(8,128)(2,1)S(1)}, bf16[2,128,128]{2,1,0:T(8,128)(2,1)S(1)}, u32[]{:S(2)}, u32[]{:S(2)}) collective-permute-start(bf16[2,128,128]{2,1,0:T(8,128)(2,1)S(1)} %fold_w.9), channel_id=1, source_target_pairs={{0,8},{1,9},{2,10},{3,11},{4,12},{5,13},{6,14},{7,15},{8,0},{9,1},... | collective-permute-start | bytes 196616 | tf_op jit(solution)/shard_map/ppermute | solution.py:82
  42.8 4.3 %collective-permute-done.19.refs_24_ = bf16[2,128,128]{2,1,0:T(8,128)(2,1)S(1)} collective-permute-done((bf16[2,128,128]{2,1,0:T(8,128)(2,1)S(1)}, bf16[2,128,128]{2,1,0:T(8,128)(2,1)S(1)}, u32[]{:S(2)}, u32[]{:S(2)}) %collective-permute-start.19) | collective-permute-done | bytes 65568 | tf_op jit(solution)/shard_map/ppermute | solution.py:82
  48.0 2.0 %collective-permute-start.22 = (f32[2,2,32,512]{3,2,1,0:T(8,128)S(1)}, f32[2,2,32,512]{3,2,1,0:T(8,128)S(1)}, u32[]{:S(2)}, u32[]{:S(2)}) collective-permute-start(f32[2,2,32,512]{3,2,1,0:T(8,128)S(1)} %get-tuple-element.46), channel_id=1, source_target_pairs={{0,2},{1,3},{2,0},{3,1},{4,6},{5,7},{6,4},{7,5},{8,10},{9,11},{10,... | collective-permute-start | bytes 786440 | tf_op jit(solution)/shard_map/ppermute | solution.py:82
  49.9 2.0 %collective-permute-start.21 = (bf16[256,512]{1,0:T(8,128)(2,1)S(1)}, bf16[256,512]{1,0:T(8,128)(2,1)S(1)}, u32[]{:S(2)}, u32[]{:S(2)}) collective-permute-start(bf16[256,512]{1,0:T(8,128)(2,1)S(1)} %get-tuple-element.44), channel_id=1, source_target_pairs={{0,16},{1,17},{2,18},{3,19},{4,20},{5,21},{6,22},{7,23},{8,24},{9,... | collective-permute-start | bytes 786440 | tf_op jit(solution)/shard_map/ppermute | solution.py:82
  53.3 1.4 %collective-permute-start.23 = (bf16[2,32,512]{2,1,0:T(8,128)(2,1)S(1)}, bf16[2,32,512]{2,1,0:T(8,128)(2,1)S(1)}, u32[]{:S(2)}, u32[]{:S(2)}) collective-permute-start(bf16[2,32,512]{2,1,0:T(8,128)(2,1)S(1)} %get-tuple-element.48), channel_id=1, source_target_pairs={{0,4},{1,5},{2,6},{3,7},{4,0},{5,1},{6,2},{7,3},{8,12},{9,13},{10,... | collective-permute-start | bytes 196616 | tf_op jit(solution)/shard_map/ppermute | solution.py:82
  55.5 1.3 %collective-permute-done.25.refs_3_ = bf16[2,32,512]{2,1,0:T(8,128)(2,1)S(1)} collective-permute-done((bf16[2,32,512]{2,1,0:T(8,128)(2,1)S(1)}, bf16[2,32,512]{2,1,0:T(8,128)(2,1)S(1)}, u32[]{:S(2)}, u32[]{:S(2)}) %collective-permute-start.25) | collective-permute-done | bytes 65568 | tf_op jit(solution)/shard_map/ppermute | solution.py:82
  58.9 2.7 %collective-permute-start.28 = (bf16[32,512]{1,0:T(8,128)(2,1)S(1)}, bf16[32,512]{1,0:T(8,128)(2,1)S(1)}, u32[]{:S(2)}, u32[]{:S(2)}) collective-permute-start(bf16[32,512]{1,0:T(8,128)(2,1)S(1)} %get-tuple-element.50), channel_id=1, source_target_pairs={{0,24},{1,25},{2,26},{3,27},{4,28},{5,29},{6,30},{7,31},{8,16},{9,... | collective-permute-start | bytes 98312 | tf_op jit(solution)/shard_map/ppermute | solution.py:82
  61.5 4.9 %collective-permute-done.27.refs_2_ = bf16[32,512]{1,0:T(8,128)(2,1)S(1)} collective-permute-done((bf16[32,512]{1,0:T(8,128)(2,1)S(1)}, bf16[32,512]{1,0:T(8,128)(2,1)S(1)}, u32[]{:S(2)}, u32[]{:S(2)}) %collective-permute-start.27) | collective-permute-done | bytes 32800 | tf_op jit(solution)/shard_map/ppermute | solution.py:82
  66.5 1.4 %collective-permute-start.29 = (f32[8,512]{1,0:T(8,128)S(1)}, f32[8,512]{1,0:T(8,128)S(1)}, u32[]{:S(2)}, u32[]{:S(2)}) collective-permute-start(f32[8,512]{1,0:T(8,128)S(1)} %get-tuple-element.51.refs_0_), channel_id=1, source_target_pairs={{0,2},{1,3},{2,0},{3,1},{4,6},{5,7},{6,4},{7,5},{8,10},{9,11},{10,... | collective-permute-start | bytes 49160 | tf_op jit(solution)/shard_map/ppermute | solution.py:82
  74.4 2.4 %collective-permute-start.33 = (bf16[272,512]{1,0:T(8,128)(2,1)S(1)}, bf16[272,512]{1,0:T(8,128)(2,1)S(1)}, u32[]{:S(2)}, u32[]{:S(2)}) collective-permute-start(bf16[272,512]{1,0:T(8,128)(2,1)S(1)} %get-tuple-element.53.refs_0_), channel_id=1, source_target_pairs={{0,16},{1,17},{2,18},{3,19},{4,20},{5,21},{6,22},{7,23},{8,24},{9,... | collective-permute-start | bytes 835592 | tf_op jit(solution)/shard_map/ppermute | solution.py:82
  77.5 2.5 %collective-permute-start.38 = (bf16[272,512]{1,0:T(8,128)(2,1)S(1)}, bf16[272,512]{1,0:T(8,128)(2,1)S(1)}, u32[]{:S(2)}, u32[]{:S(2)}) collective-permute-start(bf16[272,512]{1,0:T(8,128)(2,1)S(1)} %get-tuple-element.53.refs_0_), channel_id=1, source_target_pairs={{0,2},{1,3},{2,0},{3,1},{4,6},{5,7},{6,4},{7,5},{8,10},{9,11},{10,... | collective-permute-start | bytes 835592 | tf_op jit(solution)/shard_map/ppermute | solution.py:82
  80.0 9.5 %collective-permute-done.33.refs_8_ = bf16[272,512]{1,0:T(8,128)(2,1)S(1)} collective-permute-done((bf16[272,512]{1,0:T(8,128)(2,1)S(1)}, bf16[272,512]{1,0:T(8,128)(2,1)S(1)}, u32[]{:S(2)}, u32[]{:S(2)}) %collective-permute-start.33) | collective-permute-done | bytes 278560 | tf_op jit(solution)/shard_map/ppermute | solution.py:82
  91.7 1.3 %collective-permute-start.46 = (bf16[272,512]{1,0:T(8,128)(2,1)S(1)}, bf16[272,512]{1,0:T(8,128)(2,1)S(1)}, u32[]{:S(2)}, u32[]{:S(2)}) collective-permute-start(bf16[272,512]{1,0:T(8,128)(2,1)S(1)} %collective-permute-done.33.refs_8_), channel_id=1, source_target_pairs={{0,4},{1,5},{2,6},{3,7},{4,0},{5,1},{6,2},{7,3},{8,12},{9,13},{10,... | collective-permute-start | bytes 835592 | tf_op jit(solution)/shard_map/ppermute | solution.py:82
  93.4 3.2 %collective-permute-done.34.refs_0_ = bf16[272,512]{1,0:T(8,128)(2,1)S(1)} collective-permute-done((bf16[272,512]{1,0:T(8,128)(2,1)S(1)}, bf16[272,512]{1,0:T(8,128)(2,1)S(1)}, u32[]{:S(2)}, u32[]{:S(2)}) %collective-permute-start.34) | collective-permute-done | bytes 278560 | tf_op jit(solution)/shard_map/ppermute | solution.py:82
  97.7 3.2 %collective-permute-start.45 = (bf16[272,512]{1,0:T(8,128)(2,1)S(1)}, bf16[272,512]{1,0:T(8,128)(2,1)S(1)}, u32[]{:S(2)}, u32[]{:S(2)}) collective-permute-start(bf16[272,512]{1,0:T(8,128)(2,1)S(1)} %collective-permute-done.33.refs_8_), channel_id=1, source_target_pairs={{0,2},{1,3},{2,0},{3,1},{4,6},{5,7},{6,4},{7,5},{8,10},{9,11},{10,... | collective-permute-start | bytes 835592 | tf_op jit(solution)/shard_map/ppermute | solution.py:82
  101.7 5.2 %collective-permute-start.47 = (bf16[272,512]{1,0:T(8,128)(2,1)S(1)}, bf16[272,512]{1,0:T(8,128)(2,1)S(1)}, u32[]{:S(2)}, u32[]{:S(2)}) collective-permute-start(bf16[272,512]{1,0:T(8,128)(2,1)S(1)} %collective-permute-done.46.refs_10_), channel_id=1, source_target_pairs={{0,2},{1,3},{2,0},{3,1},{4,6},{5,7},{6,4},{7,5},{8,10},{9,11},{10,... | collective-permute-start | bytes 835592 | tf_op jit(solution)/shard_map/ppermute | solution.py:82
  107.7 2.8 %collective-permute-start.37 = (bf16[272,512]{1,0:T(8,128)(2,1)S(1)}, bf16[272,512]{1,0:T(8,128)(2,1)S(1)}, u32[]{:S(2)}, u32[]{:S(2)}) collective-permute-start(bf16[272,512]{1,0:T(8,128)(2,1)S(1)} %collective-permute-done.36.refs_2_), channel_id=1, source_target_pairs={{0,2},{1,3},{2,0},{3,1},{4,6},{5,7},{6,4},{7,5},{8,10},{9,11},{10,... | collective-permute-start | bytes 835592 | tf_op jit(solution)/shard_map/ppermute | solution.py:82
  110.5 1.8 %lay.2 = (bf16[4096,512]{1,0:T(8,128)(2,1)}, bf16[4,4096]{1,0:T(4,128)(2,1)S(1)}) custom-call(bf16[272,512]{1,0:T(8,128)(2,1)S(1)} %get-tuple-element.53.refs_0_, bf16[272,512]{1,0:T(8,128)(2,1)S(1)} %collective-permute-done.38.refs_1_, bf16[272,512]{1,0:T(8,128)(2,1)S(1)} %collective-permute-done.39.refs_2_, ...), custom_call_target="tpu_custom_call" | custom-call | bytes 1 | tf_op jit(solution)/shard_map/lay/pallas_call | solution.py:387
  112.3 1.6 %lay.3 = (bf16[4096,512]{1,0:T(8,128)(2,1)}, bf16[4,4096]{1,0:T(4,128)(2,1)}) custom-call(bf16[272,512]{1,0:T(8,128)(2,1)S(1)} %collective-permute-done.34.refs_0_, bf16[272,512]{1,0:T(8,128)(2,1)S(1)} %collective-permute-done.35.refs_1_, bf16[272,512]{1,0:T(8,128)(2,1)S(1)} %collective-permute-done.36.refs_2_, ...), custom_call_target="tpu_custom_call", output_to_operand_aliasing={{0}: (4, {})} | custom-call | bytes 1 | tf_op jit(solution)/shard_map/lay/pallas_call | solution.py:387
  (100 shorter events, 23.3 us)
Async XLA Ops:
  5.4 7.8 %collective-permute-start.4 = (bf16[2,2,2,2,256,128]{5,4,3,2,1,0:T(8,128)(2,1)S(1)}, bf16[2,2,2,2,256,128]{5,4,3,2,1,0:T(8,128)(2,1)S(1)}, u32[]{:S(2)}, u32[]{:S(2)}) collective-permute-start(bf16[2,2,2,2,256,128]{5,4,3,2,1,0:T(8,128)(2,1)S(1)} %get-tuple-element.36), channel_id=1, source_target_pairs={{0,2},{1,3},{2,0},{3,1},{4,6},{5,7},{6,4},{7,5},{8,10},{9,11},{10,... | collective-permute-start | bytes 3145736 | tf_op jit(solution)/shard_map/ppermute | solution.py:82
  5.9 8.7 %collective-permute-start = (bf16[2,2,2,2,256,128]{5,4,3,2,1,0:T(8,128)(2,1)S(1)}, bf16[2,2,2,2,256,128]{5,4,3,2,1,0:T(8,128)(2,1)S(1)}, u32[]{:S(2)}, u32[]{:S(2)}) collective-permute-start(bf16[2,2,2,2,256,128]{5,4,3,2,1,0:T(8,128)(2,1)S(1)} %get-tuple-element.34), channel_id=1, source_target_pairs={{0,2},{1,3},{2,0},{3,1},{4,6},{5,7},{6,4},{7,5},{8,10},{9,11},{10,... | collective-permute-start | bytes 3145736 | tf_op jit(solution)/shard_map/ppermute | solution.py:82
  5.9 10.1 %collective-permute-start.16 = (bf16[2,2,2,2,128,128]{5,4,3,2,1,0:T(8,128)(2,1)S(1)}, bf16[2,2,2,2,128,128]{5,4,3,2,1,0:T(8,128)(2,1)S(1)}, u32[]{:S(2)}, u32[]{:S(2)}) collective-permute-start(bf16[2,2,2,2,128,128]{5,4,3,2,1,0:T(8,128)(2,1)S(1)} %get-tuple-element.42), channel_id=1, source_target_pairs={{0,2},{1,3},{2,0},{3,1},{4,6},{5,7},{6,4},{7,5},{8,10},{9,11},{10,... | collective-permute-start | bytes 1572872 | tf_op jit(solution)/shard_map/ppermute | solution.py:82
  6.4 10.0 %collective-permute-start.12 = (bf16[2,2,2,2,128,128]{5,4,3,2,1,0:T(8,128)(2,1)S(1)}, bf16[2,2,2,2,128,128]{5,4,3,2,1,0:T(8,128)(2,1)S(1)}, u32[]{:S(2)}, u32[]{:S(2)}) collective-permute-start(bf16[2,2,2,2,128,128]{5,4,3,2,1,0:T(8,128)(2,1)S(1)} %get-tuple-element.40), channel_id=1, source_target_pairs={{0,2},{1,3},{2,0},{3,1},{4,6},{5,7},{6,4},{7,5},{8,10},{9,11},{10,... | collective-permute-start | bytes 1572872 | tf_op jit(solution)/shard_map/ppermute | solution.py:82
  10.4 15.0 %collective-permute-start.9 = (bf16[2,2,2,256,128]{4,3,2,1,0:T(8,128)(2,1)S(1)}, bf16[2,2,2,256,128]{4,3,2,1,0:T(8,128)(2,1)S(1)}, u32[]{:S(2)}, u32[]{:S(2)}) collective-permute-start(bf16[2,2,2,256,128]{4,3,2,1,0:T(8,128)(2,1)S(1)} %fold_w.7), channel_id=1, source_target_pairs={{0,8},{1,9},{2,10},{3,11},{4,12},{5,13},{6,14},{7,15},{8,0},{9,1},... | collective-permute-start | bytes 1572872 | tf_op jit(solution)/shard_map/ppermute | solution.py:82
  13.3 13.5 %collective-permute-start.5 = (bf16[2,2,2,256,128]{4,3,2,1,0:T(8,128)(2,1)S(1)}, bf16[2,2,2,256,128]{4,3,2,1,0:T(8,128)(2,1)S(1)}, u32[]{:S(2)}, u32[]{:S(2)}) collective-permute-start(bf16[2,2,2,256,128]{4,3,2,1,0:T(8,128)(2,1)S(1)} %fold_y.6), channel_id=1, source_target_pairs={{0,1},{1,0},{2,3},{3,2},{4,5},{5,4},{6,7},{7,6},{8,9},{9,8},{10,11... | collective-permute-start | bytes 1572872 | tf_op jit(solution)/shard_map/ppermute | solution.py:82
  14.7 13.5 %collective-permute-start.1 = (bf16[2,2,2,256,128]{4,3,2,1,0:T(8,128)(2,1)S(1)}, bf16[2,2,2,256,128]{4,3,2,1,0:T(8,128)(2,1)S(1)}, u32[]{:S(2)}, u32[]{:S(2)}) collective-permute-start(bf16[2,2,2,256,128]{4,3,2,1,0:T(8,128)(2,1)S(1)} %fold_x.5), channel_id=1, source_target_pairs={{0,4},{1,5},{2,6},{3,7},{4,0},{5,1},{6,2},{7,3},{8,12},{9,13},{10,... | collective-permute-start | bytes 1572872 | tf_op jit(solution)/shard_map/ppermute | solution.py:82
  16.1 16.1 %collective-permute-start.17 = (bf16[2,2,2,128,128]{4,3,2,1,0:T(8,128)(2,1)S(1)}, bf16[2,2,2,128,128]{4,3,2,1,0:T(8,128)(2,1)S(1)}, u32[]{:S(2)}, u32[]{:S(2)}) collective-permute-start(bf16[2,2,2,128,128]{4,3,2,1,0:T(8,128)(2,1)S(1)} %fold_y.9), channel_id=1, source_target_pairs={{0,1},{1,0},{2,3},{3,2},{4,5},{5,4},{6,7},{7,6},{8,9},{9,8},{10,11... | collective-permute-start | bytes 786440 | tf_op jit(solution)/shard_map/ppermute | solution.py:82
  16.4 17.1 %collective-permute-start.13 = (bf16[2,2,2,128,128]{4,3,2,1,0:T(8,128)(2,1)S(1)}, bf16[2,2,2,128,128]{4,3,2,1,0:T(8,128)(2,1)S(1)}, u32[]{:S(2)}, u32[]{:S(2)}) collective-permute-start(bf16[2,2,2,128,128]{4,3,2,1,0:T(8,128)(2,1)S(1)} %fold_w.8), channel_id=1, source_target_pairs={{0,8},{1,9},{2,10},{3,11},{4,12},{5,13},{6,14},{7,15},{8,0},{9,1},... | collective-permute-start | bytes 786440 | tf_op jit(solution)/shard_map/ppermute | solution.py:82
  25.5 10.4 %collective-permute-start.10 = (bf16[2,2,256,128]{3,2,1,0:T(8,128)(2,1)S(1)}, bf16[2,2,256,128]{3,2,1,0:T(8,128)(2,1)S(1)}, u32[]{:S(2)}, u32[]{:S(2)}) collective-permute-start(bf16[2,2,256,128]{3,2,1,0:T(8,128)(2,1)S(1)} %fold_x.7), channel_id=1, source_target_pairs={{0,4},{1,5},{2,6},{3,7},{4,0},{5,1},{6,2},{7,3},{8,12},{9,13},{10,... | collective-permute-start | bytes 786440 | tf_op jit(solution)/shard_map/ppermute | solution.py:82
  26.9 10.5 %collective-permute-start.6 = (bf16[2,2,256,128]{3,2,1,0:T(8,128)(2,1)S(1)}, bf16[2,2,256,128]{3,2,1,0:T(8,128)(2,1)S(1)}, u32[]{:S(2)}, u32[]{:S(2)}) collective-permute-start(bf16[2,2,256,128]{3,2,1,0:T(8,128)(2,1)S(1)} %fold_w.6), channel_id=1, source_target_pairs={{0,8},{1,9},{2,10},{3,11},{4,12},{5,13},{6,14},{7,15},{8,0},{9,1},... | collective-permute-start | bytes 786440 | tf_op jit(solution)/shard_map/ppermute | solution.py:82
  28.4 9.6 %collective-permute-start.2 = (bf16[2,2,256,128]{3,2,1,0:T(8,128)(2,1)S(1)}, bf16[2,2,256,128]{3,2,1,0:T(8,128)(2,1)S(1)}, u32[]{:S(2)}, u32[]{:S(2)}) collective-permute-start(bf16[2,2,256,128]{3,2,1,0:T(8,128)(2,1)S(1)} %fold_y.5), channel_id=1, source_target_pairs={{0,1},{1,0},{2,3},{3,2},{4,5},{5,4},{6,7},{7,6},{8,9},{9,8},{10,11... | collective-permute-start | bytes 786440 | tf_op jit(solution)/shard_map/ppermute | solution.py:82
  32.2 8.8 %collective-permute-start.18 = (bf16[2,2,128,128]{3,2,1,0:T(8,128)(2,1)S(1)}, bf16[2,2,128,128]{3,2,1,0:T(8,128)(2,1)S(1)}, u32[]{:S(2)}, u32[]{:S(2)}) collective-permute-start(bf16[2,2,128,128]{3,2,1,0:T(8,128)(2,1)S(1)} %fold_x.9), channel_id=1, source_target_pairs={{0,4},{1,5},{2,6},{3,7},{4,0},{5,1},{6,2},{7,3},{8,12},{9,13},{10,... | collective-permute-start | bytes 393224 | tf_op jit(solution)/shard_map/ppermute | solution.py:82
  33.5 9.2 %collective-permute-start.20 = (bf16[320,256]{1,0:T(8,128)(2,1)S(1)}, bf16[320,256]{1,0:T(8,128)(2,1)S(1)}, u32[]{:S(2)}, u32[]{:S(2)}) collective-permute-start(bf16[320,256]{1,0:T(8,128)(2,1)S(1)} %pack.1.refs_25_.refs_4_), channel_id=1, source_target_pairs={{0,16},{1,17},{2,18},{3,19},{4,20},{5,21},{6,22},{7,23},{8,24},{9,... | collective-permute-start | bytes 491528 | tf_op jit(solution)/shard_map/ppermute | solution.py:82
  37.4 9.8 %collective-permute-start.11 = (bf16[2,256,128]{2,1,0:T(8,128)(2,1)S(1)}, bf16[2,256,128]{2,1,0:T(8,128)(2,1)S(1)}, u32[]{:S(2)}, u32[]{:S(2)}) collective-permute-start(bf16[2,256,128]{2,1,0:T(8,128)(2,1)S(1)} %fold_y.7), channel_id=1, source_target_pairs={{0,1},{1,0},{2,3},{3,2},{4,5},{5,4},{6,7},{7,6},{8,9},{9,8},{10,11... | collective-permute-start | bytes 393224 | tf_op jit(solution)/shard_map/ppermute | solution.py:82
  37.9 9.3 %collective-permute-start.7 = (bf16[2,256,128]{2,1,0:T(8,128)(2,1)S(1)}, bf16[2,256,128]{2,1,0:T(8,128)(2,1)S(1)}, u32[]{:S(2)}, u32[]{:S(2)}) collective-permute-start(bf16[2,256,128]{2,1,0:T(8,128)(2,1)S(1)} %fold_x.6), channel_id=1, source_target_pairs={{0,4},{1,5},{2,6},{3,7},{4,0},{5,1},{6,2},{7,3},{8,12},{9,13},{10,... | collective-permute-start | bytes 393224 | tf_op jit(solution)/shard_map/ppermute | solution.py:82
  49.9 21.5 %collective-permute-start.21 = (bf16[256,512]{1,0:T(8,128)(2,1)S(1)}, bf16[256,512]{1,0:T(8,128)(2,1)S(1)}, u32[]{:S(2)}, u32[]{:S(2)}) collective-permute-start(bf16[256,512]{1,0:T(8,128)(2,1)S(1)} %get-tuple-element.44), channel_id=1, source_target_pairs={{0,16},{1,17},{2,18},{3,19},{4,20},{5,21},{6,22},{7,23},{8,24},{9,... | collective-permute-start | bytes 786440 | tf_op jit(solution)/shard_map/ppermute | solution.py:82
  57.7 8.7 %collective-permute-start.27 = (bf16[32,512]{1,0:T(8,128)(2,1)S(1)}, bf16[32,512]{1,0:T(8,128)(2,1)S(1)}, u32[]{:S(2)}, u32[]{:S(2)}) collective-permute-start(bf16[32,512]{1,0:T(8,128)(2,1)S(1)} %get-tuple-element.49.refs_0_), channel_id=1, source_target_pairs={{0,16},{1,17},{2,18},{3,19},{4,20},{5,21},{6,22},{7,23},{8,24},{9,... | collective-permute-start | bytes 98312 | tf_op jit(solution)/shard_map/ppermute | solution.py:82
  58.9 7.6 %collective-permute-start.28 = (bf16[32,512]{1,0:T(8,128)(2,1)S(1)}, bf16[32,512]{1,0:T(8,128)(2,1)S(1)}, u32[]{:S(2)}, u32[]{:S(2)}) collective-permute-start(bf16[32,512]{1,0:T(8,128)(2,1)S(1)} %get-tuple-element.50), channel_id=1, source_target_pairs={{0,24},{1,25},{2,26},{3,27},{4,28},{5,29},{6,30},{7,31},{8,16},{9,... | collective-permute-start | bytes 98312 | tf_op jit(solution)/shard_map/ppermute | solution.py:82
  74.4 15.1 %collective-permute-start.33 = (bf16[272,512]{1,0:T(8,128)(2,1)S(1)}, bf16[272,512]{1,0:T(8,128)(2,1)S(1)}, u32[]{:S(2)}, u32[]{:S(2)}) collective-permute-start(bf16[272,512]{1,0:T(8,128)(2,1)S(1)} %get-tuple-element.53.refs_0_), channel_id=1, source_target_pairs={{0,16},{1,17},{2,18},{3,19},{4,20},{5,21},{6,22},{7,23},{8,24},{9,... | collective-permute-start | bytes 835592 | tf_op jit(solution)/shard_map/ppermute | solution.py:82
  76.8 12.7 %collective-permute-start.41 = (bf16[272,512]{1,0:T(8,128)(2,1)S(1)}, bf16[272,512]{1,0:T(8,128)(2,1)S(1)}, u32[]{:S(2)}, u32[]{:S(2)}) collective-permute-start(bf16[272,512]{1,0:T(8,128)(2,1)S(1)} %get-tuple-element.53.refs_0_), channel_id=1, source_target_pairs={{0,8},{1,9},{2,10},{3,11},{4,12},{5,13},{6,14},{7,15},{8,0},{9,1},... | collective-permute-start | bytes 835592 | tf_op jit(solution)/shard_map/ppermute | solution.py:82
  77.5 14.2 %collective-permute-start.39 = (bf16[272,512]{1,0:T(8,128)(2,1)S(1)}, bf16[272,512]{1,0:T(8,128)(2,1)S(1)}, u32[]{:S(2)}, u32[]{:S(2)}) collective-permute-start(bf16[272,512]{1,0:T(8,128)(2,1)S(1)} %get-tuple-element.53.refs_0_), channel_id=1, source_target_pairs={{0,4},{1,5},{2,6},{3,7},{4,0},{5,1},{6,2},{7,3},{8,12},{9,13},{10,... | collective-permute-start | bytes 835592 | tf_op jit(solution)/shard_map/ppermute | solution.py:82
  77.5 15.6 %collective-permute-start.38 = (bf16[272,512]{1,0:T(8,128)(2,1)S(1)}, bf16[272,512]{1,0:T(8,128)(2,1)S(1)}, u32[]{:S(2)}, u32[]{:S(2)}) collective-permute-start(bf16[272,512]{1,0:T(8,128)(2,1)S(1)} %get-tuple-element.53.refs_0_), channel_id=1, source_target_pairs={{0,2},{1,3},{2,0},{3,1},{4,6},{5,7},{6,4},{7,5},{8,10},{9,11},{10,... | collective-permute-start | bytes 835592 | tf_op jit(solution)/shard_map/ppermute | solution.py:82
  89.5 7.1 %collective-permute-start.34 = (bf16[272,512]{1,0:T(8,128)(2,1)S(1)}, bf16[272,512]{1,0:T(8,128)(2,1)S(1)}, u32[]{:S(2)}, u32[]{:S(2)}) collective-permute-start(bf16[272,512]{1,0:T(8,128)(2,1)S(1)} %collective-permute-done.33.refs_8_), channel_id=1, source_target_pairs={{0,8},{1,9},{2,10},{3,11},{4,12},{5,13},{6,14},{7,15},{8,0},{9,1},... | collective-permute-start | bytes 835592 | tf_op jit(solution)/shard_map/ppermute | solution.py:82
  89.5 8.2 %collective-permute-start.43 = (bf16[272,512]{1,0:T(8,128)(2,1)S(1)}, bf16[272,512]{1,0:T(8,128)(2,1)S(1)}, u32[]{:S(2)}, u32[]{:S(2)}) collective-permute-start(bf16[272,512]{1,0:T(8,128)(2,1)S(1)} %collective-permute-done.41.refs_4_), channel_id=1, source_target_pairs={{0,4},{1,5},{2,6},{3,7},{4,0},{5,1},{6,2},{7,3},{8,12},{9,13},{10,... | collective-permute-start | bytes 835592 | tf_op jit(solution)/shard_map/ppermute | solution.py:82
  90.5 10.5 %collective-permute-start.42 = (bf16[272,512]{1,0:T(8,128)(2,1)S(1)}, bf16[272,512]{1,0:T(8,128)(2,1)S(1)}, u32[]{:S(2)}, u32[]{:S(2)}) collective-permute-start(bf16[272,512]{1,0:T(8,128)(2,1)S(1)} %collective-permute-done.41.refs_4_), channel_id=1, source_target_pairs={{0,2},{1,3},{2,0},{3,1},{4,6},{5,7},{6,4},{7,5},{8,10},{9,11},{10,... | collective-permute-start | bytes 835592 | tf_op jit(solution)/shard_map/ppermute | solution.py:82
  91.7 10.0 %collective-permute-start.46 = (bf16[272,512]{1,0:T(8,128)(2,1)S(1)}, bf16[272,512]{1,0:T(8,128)(2,1)S(1)}, u32[]{:S(2)}, u32[]{:S(2)}) collective-permute-start(bf16[272,512]{1,0:T(8,128)(2,1)S(1)} %collective-permute-done.33.refs_8_), channel_id=1, source_target_pairs={{0,4},{1,5},{2,6},{3,7},{4,0},{5,1},{6,2},{7,3},{8,12},{9,13},{10,... | collective-permute-start | bytes 835592 | tf_op jit(solution)/shard_map/ppermute | solution.py:82
  93.1 13.8 %collective-permute-start.40 = (bf16[272,512]{1,0:T(8,128)(2,1)S(1)}, bf16[272,512]{1,0:T(8,128)(2,1)S(1)}, u32[]{:S(2)}, u32[]{:S(2)}) collective-permute-start(bf16[272,512]{1,0:T(8,128)(2,1)S(1)} %collective-permute-done.39.refs_2_), channel_id=1, source_target_pairs={{0,2},{1,3},{2,0},{3,1},{4,6},{5,7},{6,4},{7,5},{8,10},{9,11},{10,... | collective-permute-start | bytes 835592 | tf_op jit(solution)/shard_map/ppermute | solution.py:82
  96.6 11.1 %collective-permute-start.36 = (bf16[272,512]{1,0:T(8,128)(2,1)S(1)}, bf16[272,512]{1,0:T(8,128)(2,1)S(1)}, u32[]{:S(2)}, u32[]{:S(2)}) collective-permute-start(bf16[272,512]{1,0:T(8,128)(2,1)S(1)} %collective-permute-done.34.refs_0_), channel_id=1, source_target_pairs={{0,4},{1,5},{2,6},{3,7},{4,0},{5,1},{6,2},{7,3},{8,12},{9,13},{10,... | collective-permute-start | bytes 835592 | tf_op jit(solution)/shard_map/ppermute | solution.py:82
  97.7 12.8 %collective-permute-start.45 = (bf16[272,512]{1,0:T(8,128)(2,1)S(1)}, bf16[272,512]{1,0:T(8,128)(2,1)S(1)}, u32[]{:S(2)}, u32[]{:S(2)}) collective-permute-start(bf16[272,512]{1,0:T(8,128)(2,1)S(1)} %collective-permute-done.33.refs_8_), channel_id=1, source_target_pairs={{0,2},{1,3},{2,0},{3,1},{4,6},{5,7},{6,4},{7,5},{8,10},{9,11},{10,... | collective-permute-start | bytes 835592 | tf_op jit(solution)/shard_map/ppermute | solution.py:82
  100.9 9.5 %collective-permute-start.44 = (bf16[272,512]{1,0:T(8,128)(2,1)S(1)}, bf16[272,512]{1,0:T(8,128)(2,1)S(1)}, u32[]{:S(2)}, u32[]{:S(2)}) collective-permute-start(bf16[272,512]{1,0:T(8,128)(2,1)S(1)} %collective-permute-done.43.refs_6_), channel_id=1, source_target_pairs={{0,2},{1,3},{2,0},{3,1},{4,6},{5,7},{6,4},{7,5},{8,10},{9,11},{10,... | collective-permute-start | bytes 835592 | tf_op jit(solution)/shard_map/ppermute | solution.py:82
  101.7 8.8 %collective-permute-start.47 = (bf16[272,512]{1,0:T(8,128)(2,1)S(1)}, bf16[272,512]{1,0:T(8,128)(2,1)S(1)}, u32[]{:S(2)}, u32[]{:S(2)}) collective-permute-start(bf16[272,512]{1,0:T(8,128)(2,1)S(1)} %collective-permute-done.46.refs_10_), channel_id=1, source_target_pairs={{0,2},{1,3},{2,0},{3,1},{4,6},{5,7},{6,4},{7,5},{8,10},{9,11},{10,... | collective-permute-start | bytes 835592 | tf_op jit(solution)/shard_map/ppermute | solution.py:82
  (21 other events, 124.4 us)

commit v5 on v4

--- a/solution.py
+++ b/solution.py
@@ -13,7 +13,7 @@
 AXES = ("node", "local")
 PIECES = ((0, 4, 0, 1), (1, 4, 0, 1), (2, 4, 0, 1), (3, 4, 0, 2), (3, 4, 1, 2))
 ORDERS = ("xyw", "ywx", "wxy", "wyx", "yxw")
-PAD = 16
+PAD = 8
 ALL = slice(None)
 MIB = 2**20
 

time: 114 us -> 113 us (level)
  no operation moved by 1% of the time
where the time goes in v5:
time: 113 us
  starting transfers between devices  57.6 us (51%)
  waiting for transfers between devices  39.5 us (35%)
  Pallas kernels  14.1 us (12%)
    ppermute x48, starting transfers between devices, send(): return lax.ppermute(array, AXES, pairs)  57.6 us
    ppermute x48, waiting for transfers between devices, send(): return lax.ppermute(array, AXES, pairs)  39.5 us
    pallas_call x2, Pallas kernels, dequant(): pl.pallas_call(kernel, out_shape=[pltpu.VMEM(shape, bf16) for shape in sh...  7.49 us
    pallas_call x2, Pallas kernels, lay(): pl.pallas_call(kernel, out_shape=[pltpu.HBM((grid.nodes * rows, columns),...  3.42 us
    pallas_call x22, Pallas kernels, call(): pl.pallas_call(kernel, out_shape=outs, in_specs=[pl.BlockSpec(memory_spac...  3.15 us
  transfers between devices with their start and end apart: 48, of which 15 were waited for; matrix products, arithmetic and copies ran while one was open for 0% of the time, Pallas kernels for 6%

profile of v5, /device:TPU:1, one launch (start us, length us, event | category | flops | bytes accessed | tf_op | source)
XLA Modules:
  0.0 113.0 jit_solution(13933747504417005225)
XLA Ops:
  1.5 3.7 %dequant.3 = (bf16[2,2,2,2,256,128]{5,4,3,2,1,0:T(8,128)(2,1)S(1)}, bf16[2,2,2,2,256,128]{5,4,3,2,1,0:T(8,128)(2,1)S(1)}, bf16[2,2,2,2,256,128]{5,4,3,2,1,0:T(8,...) custom-call(s32[4,8192]{1,0:T(4,128)S(1)} %bitcast.2, ...), custom_call_target="tpu_custom_call" | custom-call | bytes 1 | tf_op jit(solution)/shard_map/dequant/pallas_call | solution.py:143
  6.5 3.7 %dequant.2 = (bf16[2,2,2,2,256,128]{5,4,3,2,1,0:T(8,128)(2,1)S(1)}, bf16[2,2,2,2,256,128]{5,4,3,2,1,0:T(8,128)(2,1)S(1)}, bf16[2,2,2,2,256,128]{5,4,3,2,1,0:T(8,...) custom-call(s32[4,8192]{1,0:T(4,128)S(1)} %bitcast.3, ...), custom_call_target="tpu_custom_call" | custom-call | bytes 1 | tf_op jit(solution)/shard_map/dequant/pallas_call | solution.py:143
  10.4 2.8 %collective-permute-start.9 = (bf16[2,2,2,256,128]{4,3,2,1,0:T(8,128)(2,1)S(1)}, bf16[2,2,2,256,128]{4,3,2,1,0:T(8,128)(2,1)S(1)}, u32[]{:S(2)}, u32[]{:S(2)}) collective-permute-start(bf16[2,2,2,256,128]{4,3,2,1,0:T(8,128)(2,1)S(1)} %fold_w.7), channel_id=1, source_target_pairs={{0,8},{1,9},{2,10},{3,11},{4,12},{5,13},{6,14},{7,15},{8,0},{9,1},... | collective-permute-start | bytes 1572872 | tf_op jit(solution)/shard_map/ppermute | solution.py:82
  13.3 1.3 %collective-permute-start.5 = (bf16[2,2,2,256,128]{4,3,2,1,0:T(8,128)(2,1)S(1)}, bf16[2,2,2,256,128]{4,3,2,1,0:T(8,128)(2,1)S(1)}, u32[]{:S(2)}, u32[]{:S(2)}) collective-permute-start(bf16[2,2,2,256,128]{4,3,2,1,0:T(8,128)(2,1)S(1)} %fold_y.6), channel_id=1, source_target_pairs={{0,1},{1,0},{2,3},{3,2},{4,5},{5,4},{6,7},{7,6},{8,9},{9,8},{10,11... | collective-permute-start | bytes 1572872 | tf_op jit(solution)/shard_map/ppermute | solution.py:82
  14.7 1.3 %collective-permute-start.1 = (bf16[2,2,2,256,128]{4,3,2,1,0:T(8,128)(2,1)S(1)}, bf16[2,2,2,256,128]{4,3,2,1,0:T(8,128)(2,1)S(1)}, u32[]{:S(2)}, u32[]{:S(2)}) collective-permute-start(bf16[2,2,2,256,128]{4,3,2,1,0:T(8,128)(2,1)S(1)} %fold_x.5), channel_id=1, source_target_pairs={{0,4},{1,5},{2,6},{3,7},{4,0},{5,1},{6,2},{7,3},{8,12},{9,13},{10,... | collective-permute-start | bytes 1572872 | tf_op jit(solution)/shard_map/ppermute | solution.py:82
  16.7 8.7 %collective-permute-done.9.refs_2_.refs_12_ = bf16[2,2,2,256,128]{4,3,2,1,0:T(8,128)(2,1)S(1)} collective-permute-done((bf16[2,2,2,256,128]{4,3,2,1,0:T(8,128)(2,1)S(1)}, bf16[2,2,2,256,128]{4,3,2,1,0:T(8,128)(2,1)S(1)}, u32[]{:S(2)}, u32[]{:S(2)}) %collective-permute-start.9) | collective-permute-done | bytes 524320 | tf_op jit(solution)/shard_map/ppermute | solution.py:82
  26.9 1.4 %collective-permute-start.6 = (bf16[2,2,256,128]{3,2,1,0:T(8,128)(2,1)S(1)}, bf16[2,2,256,128]{3,2,1,0:T(8,128)(2,1)S(1)}, u32[]{:S(2)}, u32[]{:S(2)}) collective-permute-start(bf16[2,2,256,128]{3,2,1,0:T(8,128)(2,1)S(1)} %fold_w.6), channel_id=1, source_target_pairs={{0,8},{1,9},{2,10},{3,11},{4,12},{5,13},{6,14},{7,15},{8,0},{9,1},... | collective-permute-start | bytes 786440 | tf_op jit(solution)/shard_map/ppermute | solution.py:82
  28.4 1.3 %collective-permute-start.2 = (bf16[2,2,256,128]{3,2,1,0:T(8,128)(2,1)S(1)}, bf16[2,2,256,128]{3,2,1,0:T(8,128)(2,1)S(1)}, u32[]{:S(2)}, u32[]{:S(2)}) collective-permute-start(bf16[2,2,256,128]{3,2,1,0:T(8,128)(2,1)S(1)} %fold_y.5), channel_id=1, source_target_pairs={{0,1},{1,0},{2,3},{3,2},{4,5},{5,4},{6,7},{7,6},{8,9},{9,8},{10,11... | collective-permute-start | bytes 786440 | tf_op jit(solution)/shard_map/ppermute | solution.py:82
  29.7 2.5 %collective-permute-done.17.refs_2_.refs_22_ = bf16[2,2,2,128,128]{4,3,2,1,0:T(8,128)(2,1)S(1)} collective-permute-done((bf16[2,2,2,128,128]{4,3,2,1,0:T(8,128)(2,1)S(1)}, bf16[2,2,2,128,128]{4,3,2,1,0:T(8,128)(2,1)S(1)}, u32[]{:S(2)}, u32[]{:S(2)}) %collective-permute-start.17) | collective-permute-done | bytes 262176 | tf_op jit(solution)/shard_map/ppermute | solution.py:82
  32.2 1.3 %collective-permute-start.18 = (bf16[2,2,128,128]{3,2,1,0:T(8,128)(2,1)S(1)}, bf16[2,2,128,128]{3,2,1,0:T(8,128)(2,1)S(1)}, u32[]{:S(2)}, u32[]{:S(2)}) collective-permute-start(bf16[2,2,128,128]{3,2,1,0:T(8,128)(2,1)S(1)} %fold_x.9), channel_id=1, source_target_pairs={{0,4},{1,5},{2,6},{3,7},{4,0},{5,1},{6,2},{7,3},{8,12},{9,13},{10,... | collective-permute-start | bytes 393224 | tf_op jit(solution)/shard_map/ppermute | solution.py:82
  33.5 2.4 %collective-permute-start.20 = (bf16[320,256]{1,0:T(8,128)(2,1)S(1)}, bf16[320,256]{1,0:T(8,128)(2,1)S(1)}, u32[]{:S(2)}, u32[]{:S(2)}) collective-permute-start(bf16[320,256]{1,0:T(8,128)(2,1)S(1)} %pack.1.refs_25_.refs_4_), channel_id=1, source_target_pairs={{0,16},{1,17},{2,18},{3,19},{4,20},{5,21},{6,22},{7,23},{8,24},{9,... | collective-permute-start | bytes 491528 | tf_op jit(solution)/shard_map/ppermute | solution.py:82
  36.0 1.3 %collective-permute-start.14 = (bf16[2,2,128,128]{3,2,1,0:T(8,128)(2,1)S(1)}, bf16[2,2,128,128]{3,2,1,0:T(8,128)(2,1)S(1)}, u32[]{:S(2)}, u32[]{:S(2)}) collective-permute-start(bf16[2,2,128,128]{3,2,1,0:T(8,128)(2,1)S(1)} %fold_y.8), channel_id=1, source_target_pairs={{0,1},{1,0},{2,3},{3,2},{4,5},{5,4},{6,7},{7,6},{8,9},{9,8},{10,11... | collective-permute-start | bytes 393224 | tf_op jit(solution)/shard_map/ppermute | solution.py:82
  37.9 3.0 %collective-permute-start.7 = (bf16[2,256,128]{2,1,0:T(8,128)(2,1)S(1)}, bf16[2,256,128]{2,1,0:T(8,128)(2,1)S(1)}, u32[]{:S(2)}, u32[]{:S(2)}) collective-permute-start(bf16[2,256,128]{2,1,0:T(8,128)(2,1)S(1)} %fold_x.6), channel_id=1, source_target_pairs={{0,4},{1,5},{2,6},{3,7},{4,0},{5,1},{6,2},{7,3},{8,12},{9,13},{10,... | collective-permute-start | bytes 393224 | tf_op jit(solution)/shard_map/ppermute | solution.py:82
  41.2 1.5 %collective-permute-start.19 = (bf16[2,128,128]{2,1,0:T(8,128)(2,1)S(1)}, bf16[2,128,128]{2,1,0:T(8,128)(2,1)S(1)}, u32[]{:S(2)}, u32[]{:S(2)}) collective-permute-start(bf16[2,128,128]{2,1,0:T(8,128)(2,1)S(1)} %fold_w.9), channel_id=1, source_target_pairs={{0,8},{1,9},{2,10},{3,11},{4,12},{5,13},{6,14},{7,15},{8,0},{9,1},... | collective-permute-start | bytes 196616 | tf_op jit(solution)/shard_map/ppermute | solution.py:82
  42.8 4.3 %collective-permute-done.19.refs_24_ = bf16[2,128,128]{2,1,0:T(8,128)(2,1)S(1)} collective-permute-done((bf16[2,128,128]{2,1,0:T(8,128)(2,1)S(1)}, bf16[2,128,128]{2,1,0:T(8,128)(2,1)S(1)}, u32[]{:S(2)}, u32[]{:S(2)}) %collective-permute-start.19) | collective-permute-done | bytes 65568 | tf_op jit(solution)/shard_map/ppermute | solution.py:82
  48.0 2.0 %collective-permute-start.22 = (f32[2,2,32,512]{3,2,1,0:T(8,128)S(1)}, f32[2,2,32,512]{3,2,1,0:T(8,128)S(1)}, u32[]{:S(2)}, u32[]{:S(2)}) collective-permute-start(f32[2,2,32,512]{3,2,1,0:T(8,128)S(1)} %get-tuple-element.46), channel_id=1, source_target_pairs={{0,2},{1,3},{2,0},{3,1},{4,6},{5,7},{6,4},{7,5},{8,10},{9,11},{10,... | collective-permute-start | bytes 786440 | tf_op jit(solution)/shard_map/ppermute | solution.py:82
  49.9 2.0 %collective-permute-start.21 = (bf16[256,512]{1,0:T(8,128)(2,1)S(1)}, bf16[256,512]{1,0:T(8,128)(2,1)S(1)}, u32[]{:S(2)}, u32[]{:S(2)}) collective-permute-start(bf16[256,512]{1,0:T(8,128)(2,1)S(1)} %get-tuple-element.44), channel_id=1, source_target_pairs={{0,16},{1,17},{2,18},{3,19},{4,20},{5,21},{6,22},{7,23},{8,24},{9,... | collective-permute-start | bytes 786440 | tf_op jit(solution)/shard_map/ppermute | solution.py:82
  53.3 1.4 %collective-permute-start.23 = (bf16[2,32,512]{2,1,0:T(8,128)(2,1)S(1)}, bf16[2,32,512]{2,1,0:T(8,128)(2,1)S(1)}, u32[]{:S(2)}, u32[]{:S(2)}) collective-permute-start(bf16[2,32,512]{2,1,0:T(8,128)(2,1)S(1)} %get-tuple-element.48), channel_id=1, source_target_pairs={{0,4},{1,5},{2,6},{3,7},{4,0},{5,1},{6,2},{7,3},{8,12},{9,13},{10,... | collective-permute-start | bytes 196616 | tf_op jit(solution)/shard_map/ppermute | solution.py:82
  55.5 1.3 %collective-permute-done.25.refs_3_ = bf16[2,32,512]{2,1,0:T(8,128)(2,1)S(1)} collective-permute-done((bf16[2,32,512]{2,1,0:T(8,128)(2,1)S(1)}, bf16[2,32,512]{2,1,0:T(8,128)(2,1)S(1)}, u32[]{:S(2)}, u32[]{:S(2)}) %collective-permute-start.25) | collective-permute-done | bytes 65568 | tf_op jit(solution)/shard_map/ppermute | solution.py:82
  58.9 2.7 %collective-permute-start.28 = (bf16[32,512]{1,0:T(8,128)(2,1)S(1)}, bf16[32,512]{1,0:T(8,128)(2,1)S(1)}, u32[]{:S(2)}, u32[]{:S(2)}) collective-permute-start(bf16[32,512]{1,0:T(8,128)(2,1)S(1)} %get-tuple-element.50), channel_id=1, source_target_pairs={{0,24},{1,25},{2,26},{3,27},{4,28},{5,29},{6,30},{7,31},{8,16},{9,... | collective-permute-start | bytes 98312 | tf_op jit(solution)/shard_map/ppermute | solution.py:82
  61.5 4.9 %collective-permute-done.27.refs_2_ = bf16[32,512]{1,0:T(8,128)(2,1)S(1)} collective-permute-done((bf16[32,512]{1,0:T(8,128)(2,1)S(1)}, bf16[32,512]{1,0:T(8,128)(2,1)S(1)}, u32[]{:S(2)}, u32[]{:S(2)}) %collective-permute-start.27) | collective-permute-done | bytes 32800 | tf_op jit(solution)/shard_map/ppermute | solution.py:82
  66.5 1.4 %collective-permute-start.29 = (f32[8,512]{1,0:T(8,128)S(1)}, f32[8,512]{1,0:T(8,128)S(1)}, u32[]{:S(2)}, u32[]{:S(2)}) collective-permute-start(f32[8,512]{1,0:T(8,128)S(1)} %get-tuple-element.51.refs_0_), channel_id=1, source_target_pairs={{0,2},{1,3},{2,0},{3,1},{4,6},{5,7},{6,4},{7,5},{8,10},{9,11},{10,... | collective-permute-start | bytes 49160 | tf_op jit(solution)/shard_map/ppermute | solution.py:82
  74.3 2.4 %collective-permute-start.33 = (bf16[264,512]{1,0:T(8,128)(2,1)S(1)}, bf16[264,512]{1,0:T(8,128)(2,1)S(1)}, u32[]{:S(2)}, u32[]{:S(2)}) collective-permute-start(bf16[264,512]{1,0:T(8,128)(2,1)S(1)} %get-tuple-element.53.refs_0_), channel_id=1, source_target_pairs={{0,16},{1,17},{2,18},{3,19},{4,20},{5,21},{6,22},{7,23},{8,24},{9,... | collective-permute-start | bytes 811016 | tf_op jit(solution)/shard_map/ppermute | solution.py:82
  77.4 2.5 %collective-permute-start.38 = (bf16[264,512]{1,0:T(8,128)(2,1)S(1)}, bf16[264,512]{1,0:T(8,128)(2,1)S(1)}, u32[]{:S(2)}, u32[]{:S(2)}) collective-permute-start(bf16[264,512]{1,0:T(8,128)(2,1)S(1)} %get-tuple-element.53.refs_0_), channel_id=1, source_target_pairs={{0,2},{1,3},{2,0},{3,1},{4,6},{5,7},{6,4},{7,5},{8,10},{9,11},{10,... | collective-permute-start | bytes 811016 | tf_op jit(solution)/shard_map/ppermute | solution.py:82
  79.9 9.2 %collective-permute-done.33.refs_8_ = bf16[264,512]{1,0:T(8,128)(2,1)S(1)} collective-permute-done((bf16[264,512]{1,0:T(8,128)(2,1)S(1)}, bf16[264,512]{1,0:T(8,128)(2,1)S(1)}, u32[]{:S(2)}, u32[]{:S(2)}) %collective-permute-start.33) | collective-permute-done | bytes 270368 | tf_op jit(solution)/shard_map/ppermute | solution.py:82
  91.3 1.3 %collective-permute-start.46 = (bf16[264,512]{1,0:T(8,128)(2,1)S(1)}, bf16[264,512]{1,0:T(8,128)(2,1)S(1)}, u32[]{:S(2)}, u32[]{:S(2)}) collective-permute-start(bf16[264,512]{1,0:T(8,128)(2,1)S(1)} %collective-permute-done.33.refs_8_), channel_id=1, source_target_pairs={{0,4},{1,5},{2,6},{3,7},{4,0},{5,1},{6,2},{7,3},{8,12},{9,13},{10,... | collective-permute-start | bytes 811016 | tf_op jit(solution)/shard_map/ppermute | solution.py:82
  93.0 3.0 %collective-permute-done.34.refs_0_ = bf16[264,512]{1,0:T(8,128)(2,1)S(1)} collective-permute-done((bf16[264,512]{1,0:T(8,128)(2,1)S(1)}, bf16[264,512]{1,0:T(8,128)(2,1)S(1)}, u32[]{:S(2)}, u32[]{:S(2)}) %collective-permute-start.34) | collective-permute-done | bytes 270368 | tf_op jit(solution)/shard_map/ppermute | solution.py:82
  97.1 3.2 %collective-permute-start.45 = (bf16[264,512]{1,0:T(8,128)(2,1)S(1)}, bf16[264,512]{1,0:T(8,128)(2,1)S(1)}, u32[]{:S(2)}, u32[]{:S(2)}) collective-permute-start(bf16[264,512]{1,0:T(8,128)(2,1)S(1)} %collective-permute-done.33.refs_8_), channel_id=1, source_target_pairs={{0,2},{1,3},{2,0},{3,1},{4,6},{5,7},{6,4},{7,5},{8,10},{9,11},{10,... | collective-permute-start | bytes 811016 | tf_op jit(solution)/shard_map/ppermute | solution.py:82
  101.0 5.2 %collective-permute-start.47 = (bf16[264,512]{1,0:T(8,128)(2,1)S(1)}, bf16[264,512]{1,0:T(8,128)(2,1)S(1)}, u32[]{:S(2)}, u32[]{:S(2)}) collective-permute-start(bf16[264,512]{1,0:T(8,128)(2,1)S(1)} %collective-permute-done.46.refs_10_), channel_id=1, source_target_pairs={{0,2},{1,3},{2,0},{3,1},{4,6},{5,7},{6,4},{7,5},{8,10},{9,11},{10,... | collective-permute-start | bytes 811016 | tf_op jit(solution)/shard_map/ppermute | solution.py:82
  106.7 2.8 %collective-permute-start.37 = (bf16[264,512]{1,0:T(8,128)(2,1)S(1)}, bf16[264,512]{1,0:T(8,128)(2,1)S(1)}, u32[]{:S(2)}, u32[]{:S(2)}) collective-permute-start(bf16[264,512]{1,0:T(8,128)(2,1)S(1)} %collective-permute-done.36.refs_2_), channel_id=1, source_target_pairs={{0,2},{1,3},{2,0},{3,1},{4,6},{5,7},{6,4},{7,5},{8,10},{9,11},{10,... | collective-permute-start | bytes 811016 | tf_op jit(solution)/shard_map/ppermute | solution.py:82
  109.6 1.8 %lay.2 = (bf16[4096,512]{1,0:T(8,128)(2,1)}, bf16[4,4096]{1,0:T(4,128)(2,1)S(1)}) custom-call(bf16[264,512]{1,0:T(8,128)(2,1)S(1)} %get-tuple-element.53.refs_0_, bf16[264,512]{1,0:T(8,128)(2,1)S(1)} %collective-permute-done.38.refs_1_, bf16[264,512]{1,0:T(8,128)(2,1)S(1)} %collective-permute-done.39.refs_2_, ...), custom_call_target="tpu_custom_call" | custom-call | bytes 1 | tf_op jit(solution)/shard_map/lay/pallas_call | solution.py:387
  111.4 1.6 %lay.3 = (bf16[4096,512]{1,0:T(8,128)(2,1)}, bf16[4,4096]{1,0:T(4,128)(2,1)}) custom-call(bf16[264,512]{1,0:T(8,128)(2,1)S(1)} %collective-permute-done.34.refs_0_, bf16[264,512]{1,0:T(8,128)(2,1)S(1)} %collective-permute-done.35.refs_1_, bf16[264,512]{1,0:T(8,128)(2,1)S(1)} %collective-permute-done.36.refs_2_, ...), custom_call_target="tpu_custom_call", output_to_operand_aliasing={{0}: (4, {})} | custom-call | bytes 1 | tf_op jit(solution)/shard_map/lay/pallas_call | solution.py:387
  (100 shorter events, 22.9 us)
Async XLA Ops:
  5.4 7.8 %collective-permute-start.4 = (bf16[2,2,2,2,256,128]{5,4,3,2,1,0:T(8,128)(2,1)S(1)}, bf16[2,2,2,2,256,128]{5,4,3,2,1,0:T(8,128)(2,1)S(1)}, u32[]{:S(2)}, u32[]{:S(2)}) collective-permute-start(bf16[2,2,2,2,256,128]{5,4,3,2,1,0:T(8,128)(2,1)S(1)} %get-tuple-element.36), channel_id=1, source_target_pairs={{0,2},{1,3},{2,0},{3,1},{4,6},{5,7},{6,4},{7,5},{8,10},{9,11},{10,... | collective-permute-start | bytes 3145736 | tf_op jit(solution)/shard_map/ppermute | solution.py:82
  5.9 8.7 %collective-permute-start = (bf16[2,2,2,2,256,128]{5,4,3,2,1,0:T(8,128)(2,1)S(1)}, bf16[2,2,2,2,256,128]{5,4,3,2,1,0:T(8,128)(2,1)S(1)}, u32[]{:S(2)}, u32[]{:S(2)}) collective-permute-start(bf16[2,2,2,2,256,128]{5,4,3,2,1,0:T(8,128)(2,1)S(1)} %get-tuple-element.34), channel_id=1, source_target_pairs={{0,2},{1,3},{2,0},{3,1},{4,6},{5,7},{6,4},{7,5},{8,10},{9,11},{10,... | collective-permute-start | bytes 3145736 | tf_op jit(solution)/shard_map/ppermute | solution.py:82
  5.9 10.1 %collective-permute-start.16 = (bf16[2,2,2,2,128,128]{5,4,3,2,1,0:T(8,128)(2,1)S(1)}, bf16[2,2,2,2,128,128]{5,4,3,2,1,0:T(8,128)(2,1)S(1)}, u32[]{:S(2)}, u32[]{:S(2)}) collective-permute-start(bf16[2,2,2,2,128,128]{5,4,3,2,1,0:T(8,128)(2,1)S(1)} %get-tuple-element.42), channel_id=1, source_target_pairs={{0,2},{1,3},{2,0},{3,1},{4,6},{5,7},{6,4},{7,5},{8,10},{9,11},{10,... | collective-permute-start | bytes 1572872 | tf_op jit(solution)/shard_map/ppermute | solution.py:82
  6.4 10.0 %collective-permute-start.12 = (bf16[2,2,2,2,128,128]{5,4,3,2,1,0:T(8,128)(2,1)S(1)}, bf16[2,2,2,2,128,128]{5,4,3,2,1,0:T(8,128)(2,1)S(1)}, u32[]{:S(2)}, u32[]{:S(2)}) collective-permute-start(bf16[2,2,2,2,128,128]{5,4,3,2,1,0:T(8,128)(2,1)S(1)} %get-tuple-element.40), channel_id=1, source_target_pairs={{0,2},{1,3},{2,0},{3,1},{4,6},{5,7},{6,4},{7,5},{8,10},{9,11},{10,... | collective-permute-start | bytes 1572872 | tf_op jit(solution)/shard_map/ppermute | solution.py:82
  10.4 15.0 %collective-permute-start.9 = (bf16[2,2,2,256,128]{4,3,2,1,0:T(8,128)(2,1)S(1)}, bf16[2,2,2,256,128]{4,3,2,1,0:T(8,128)(2,1)S(1)}, u32[]{:S(2)}, u32[]{:S(2)}) collective-permute-start(bf16[2,2,2,256,128]{4,3,2,1,0:T(8,128)(2,1)S(1)} %fold_w.7), channel_id=1, source_target_pairs={{0,8},{1,9},{2,10},{3,11},{4,12},{5,13},{6,14},{7,15},{8,0},{9,1},... | collective-permute-start | bytes 1572872 | tf_op jit(solution)/shard_map/ppermute | solution.py:82
  13.3 13.5 %collective-permute-start.5 = (bf16[2,2,2,256,128]{4,3,2,1,0:T(8,128)(2,1)S(1)}, bf16[2,2,2,256,128]{4,3,2,1,0:T(8,128)(2,1)S(1)}, u32[]{:S(2)}, u32[]{:S(2)}) collective-permute-start(bf16[2,2,2,256,128]{4,3,2,1,0:T(8,128)(2,1)S(1)} %fold_y.6), channel_id=1, source_target_pairs={{0,1},{1,0},{2,3},{3,2},{4,5},{5,4},{6,7},{7,6},{8,9},{9,8},{10,11... | collective-permute-start | bytes 1572872 | tf_op jit(solution)/shard_map/ppermute | solution.py:82
  14.7 13.5 %collective-permute-start.1 = (bf16[2,2,2,256,128]{4,3,2,1,0:T(8,128)(2,1)S(1)}, bf16[2,2,2,256,128]{4,3,2,1,0:T(8,128)(2,1)S(1)}, u32[]{:S(2)}, u32[]{:S(2)}) collective-permute-start(bf16[2,2,2,256,128]{4,3,2,1,0:T(8,128)(2,1)S(1)} %fold_x.5), channel_id=1, source_target_pairs={{0,4},{1,5},{2,6},{3,7},{4,0},{5,1},{6,2},{7,3},{8,12},{9,13},{10,... | collective-permute-start | bytes 1572872 | tf_op jit(solution)/shard_map/ppermute | solution.py:82
  16.1 16.1 %collective-permute-start.17 = (bf16[2,2,2,128,128]{4,3,2,1,0:T(8,128)(2,1)S(1)}, bf16[2,2,2,128,128]{4,3,2,1,0:T(8,128)(2,1)S(1)}, u32[]{:S(2)}, u32[]{:S(2)}) collective-permute-start(bf16[2,2,2,128,128]{4,3,2,1,0:T(8,128)(2,1)S(1)} %fold_y.9), channel_id=1, source_target_pairs={{0,1},{1,0},{2,3},{3,2},{4,5},{5,4},{6,7},{7,6},{8,9},{9,8},{10,11... | collective-permute-start | bytes 786440 | tf_op jit(solution)/shard_map/ppermute | solution.py:82
  16.4 17.1 %collective-permute-start.13 = (bf16[2,2,2,128,128]{4,3,2,1,0:T(8,128)(2,1)S(1)}, bf16[2,2,2,128,128]{4,3,2,1,0:T(8,128)(2,1)S(1)}, u32[]{:S(2)}, u32[]{:S(2)}) collective-permute-start(bf16[2,2,2,128,128]{4,3,2,1,0:T(8,128)(2,1)S(1)} %fold_w.8), channel_id=1, source_target_pairs={{0,8},{1,9},{2,10},{3,11},{4,12},{5,13},{6,14},{7,15},{8,0},{9,1},... | collective-permute-start | bytes 786440 | tf_op jit(solution)/shard_map/ppermute | solution.py:82
  25.5 10.4 %collective-permute-start.10 = (bf16[2,2,256,128]{3,2,1,0:T(8,128)(2,1)S(1)}, bf16[2,2,256,128]{3,2,1,0:T(8,128)(2,1)S(1)}, u32[]{:S(2)}, u32[]{:S(2)}) collective-permute-start(bf16[2,2,256,128]{3,2,1,0:T(8,128)(2,1)S(1)} %fold_x.7), channel_id=1, source_target_pairs={{0,4},{1,5},{2,6},{3,7},{4,0},{5,1},{6,2},{7,3},{8,12},{9,13},{10,... | collective-permute-start | bytes 786440 | tf_op jit(solution)/shard_map/ppermute | solution.py:82
  26.9 10.5 %collective-permute-start.6 = (bf16[2,2,256,128]{3,2,1,0:T(8,128)(2,1)S(1)}, bf16[2,2,256,128]{3,2,1,0:T(8,128)(2,1)S(1)}, u32[]{:S(2)}, u32[]{:S(2)}) collective-permute-start(bf16[2,2,256,128]{3,2,1,0:T(8,128)(2,1)S(1)} %fold_w.6), channel_id=1, source_target_pairs={{0,8},{1,9},{2,10},{3,11},{4,12},{5,13},{6,14},{7,15},{8,0},{9,1},... | collective-permute-start | bytes 786440 | tf_op jit(solution)/shard_map/ppermute | solution.py:82
  28.4 9.6 %collective-permute-start.2 = (bf16[2,2,256,128]{3,2,1,0:T(8,128)(2,1)S(1)}, bf16[2,2,256,128]{3,2,1,0:T(8,128)(2,1)S(1)}, u32[]{:S(2)}, u32[]{:S(2)}) collective-permute-start(bf16[2,2,256,128]{3,2,1,0:T(8,128)(2,1)S(1)} %fold_y.5), channel_id=1, source_target_pairs={{0,1},{1,0},{2,3},{3,2},{4,5},{5,4},{6,7},{7,6},{8,9},{9,8},{10,11... | collective-permute-start | bytes 786440 | tf_op jit(solution)/shard_map/ppermute | solution.py:82
  32.2 8.8 %collective-permute-start.18 = (bf16[2,2,128,128]{3,2,1,0:T(8,128)(2,1)S(1)}, bf16[2,2,128,128]{3,2,1,0:T(8,128)(2,1)S(1)}, u32[]{:S(2)}, u32[]{:S(2)}) collective-permute-start(bf16[2,2,128,128]{3,2,1,0:T(8,128)(2,1)S(1)} %fold_x.9), channel_id=1, source_target_pairs={{0,4},{1,5},{2,6},{3,7},{4,0},{5,1},{6,2},{7,3},{8,12},{9,13},{10,... | collective-permute-start | bytes 393224 | tf_op jit(solution)/shard_map/ppermute | solution.py:82
  33.5 9.2 %collective-permute-start.20 = (bf16[320,256]{1,0:T(8,128)(2,1)S(1)}, bf16[320,256]{1,0:T(8,128)(2,1)S(1)}, u32[]{:S(2)}, u32[]{:S(2)}) collective-permute-start(bf16[320,256]{1,0:T(8,128)(2,1)S(1)} %pack.1.refs_25_.refs_4_), channel_id=1, source_target_pairs={{0,16},{1,17},{2,18},{3,19},{4,20},{5,21},{6,22},{7,23},{8,24},{9,... | collective-permute-start | bytes 491528 | tf_op jit(solution)/shard_map/ppermute | solution.py:82
  37.4 9.8 %collective-permute-start.11 = (bf16[2,256,128]{2,1,0:T(8,128)(2,1)S(1)}, bf16[2,256,128]{2,1,0:T(8,128)(2,1)S(1)}, u32[]{:S(2)}, u32[]{:S(2)}) collective-permute-start(bf16[2,256,128]{2,1,0:T(8,128)(2,1)S(1)} %fold_y.7), channel_id=1, source_target_pairs={{0,1},{1,0},{2,3},{3,2},{4,5},{5,4},{6,7},{7,6},{8,9},{9,8},{10,11... | collective-permute-start | bytes 393224 | tf_op jit(solution)/shard_map/ppermute | solution.py:82
  37.9 9.3 %collective-permute-start.7 = (bf16[2,256,128]{2,1,0:T(8,128)(2,1)S(1)}, bf16[2,256,128]{2,1,0:T(8,128)(2,1)S(1)}, u32[]{:S(2)}, u32[]{:S(2)}) collective-permute-start(bf16[2,256,128]{2,1,0:T(8,128)(2,1)S(1)} %fold_x.6), channel_id=1, source_target_pairs={{0,4},{1,5},{2,6},{3,7},{4,0},{5,1},{6,2},{7,3},{8,12},{9,13},{10,... | collective-permute-start | bytes 393224 | tf_op jit(solution)/shard_map/ppermute | solution.py:82
  49.9 21.5 %collective-permute-start.21 = (bf16[256,512]{1,0:T(8,128)(2,1)S(1)}, bf16[256,512]{1,0:T(8,128)(2,1)S(1)}, u32[]{:S(2)}, u32[]{:S(2)}) collective-permute-start(bf16[256,512]{1,0:T(8,128)(2,1)S(1)} %get-tuple-element.44), channel_id=1, source_target_pairs={{0,16},{1,17},{2,18},{3,19},{4,20},{5,21},{6,22},{7,23},{8,24},{9,... | collective-permute-start | bytes 786440 | tf_op jit(solution)/shard_map/ppermute | solution.py:82
  57.7 8.7 %collective-permute-start.27 = (bf16[32,512]{1,0:T(8,128)(2,1)S(1)}, bf16[32,512]{1,0:T(8,128)(2,1)S(1)}, u32[]{:S(2)}, u32[]{:S(2)}) collective-permute-start(bf16[32,512]{1,0:T(8,128)(2,1)S(1)} %get-tuple-element.49.refs_0_), channel_id=1, source_target_pairs={{0,16},{1,17},{2,18},{3,19},{4,20},{5,21},{6,22},{7,23},{8,24},{9,... | collective-permute-start | bytes 98312 | tf_op jit(solution)/shard_map/ppermute | solution.py:82
  58.9 7.6 %collective-permute-start.28 = (bf16[32,512]{1,0:T(8,128)(2,1)S(1)}, bf16[32,512]{1,0:T(8,128)(2,1)S(1)}, u32[]{:S(2)}, u32[]{:S(2)}) collective-permute-start(bf16[32,512]{1,0:T(8,128)(2,1)S(1)} %get-tuple-element.50), channel_id=1, source_target_pairs={{0,24},{1,25},{2,26},{3,27},{4,28},{5,29},{6,30},{7,31},{8,16},{9,... | collective-permute-start | bytes 98312 | tf_op jit(solution)/shard_map/ppermute | solution.py:82
  74.3 14.7 %collective-permute-start.33 = (bf16[264,512]{1,0:T(8,128)(2,1)S(1)}, bf16[264,512]{1,0:T(8,128)(2,1)S(1)}, u32[]{:S(2)}, u32[]{:S(2)}) collective-permute-start(bf16[264,512]{1,0:T(8,128)(2,1)S(1)} %get-tuple-element.53.refs_0_), channel_id=1, source_target_pairs={{0,16},{1,17},{2,18},{3,19},{4,20},{5,21},{6,22},{7,23},{8,24},{9,... | collective-permute-start | bytes 811016 | tf_op jit(solution)/shard_map/ppermute | solution.py:82
  76.7 12.3 %collective-permute-start.41 = (bf16[264,512]{1,0:T(8,128)(2,1)S(1)}, bf16[264,512]{1,0:T(8,128)(2,1)S(1)}, u32[]{:S(2)}, u32[]{:S(2)}) collective-permute-start(bf16[264,512]{1,0:T(8,128)(2,1)S(1)} %get-tuple-element.53.refs_0_), channel_id=1, source_target_pairs={{0,8},{1,9},{2,10},{3,11},{4,12},{5,13},{6,14},{7,15},{8,0},{9,1},... | collective-permute-start | bytes 811016 | tf_op jit(solution)/shard_map/ppermute | solution.py:82
  77.4 13.9 %collective-permute-start.39 = (bf16[264,512]{1,0:T(8,128)(2,1)S(1)}, bf16[264,512]{1,0:T(8,128)(2,1)S(1)}, u32[]{:S(2)}, u32[]{:S(2)}) collective-permute-start(bf16[264,512]{1,0:T(8,128)(2,1)S(1)} %get-tuple-element.53.refs_0_), channel_id=1, source_target_pairs={{0,4},{1,5},{2,6},{3,7},{4,0},{5,1},{6,2},{7,3},{8,12},{9,13},{10,... | collective-permute-start | bytes 811016 | tf_op jit(solution)/shard_map/ppermute | solution.py:82
  77.4 15.2 %collective-permute-start.38 = (bf16[264,512]{1,0:T(8,128)(2,1)S(1)}, bf16[264,512]{1,0:T(8,128)(2,1)S(1)}, u32[]{:S(2)}, u32[]{:S(2)}) collective-permute-start(bf16[264,512]{1,0:T(8,128)(2,1)S(1)} %get-tuple-element.53.refs_0_), channel_id=1, source_target_pairs={{0,2},{1,3},{2,0},{3,1},{4,6},{5,7},{6,4},{7,5},{8,10},{9,11},{10,... | collective-permute-start | bytes 811016 | tf_op jit(solution)/shard_map/ppermute | solution.py:82
  89.0 6.9 %collective-permute-start.34 = (bf16[264,512]{1,0:T(8,128)(2,1)S(1)}, bf16[264,512]{1,0:T(8,128)(2,1)S(1)}, u32[]{:S(2)}, u32[]{:S(2)}) collective-permute-start(bf16[264,512]{1,0:T(8,128)(2,1)S(1)} %collective-permute-done.33.refs_8_), channel_id=1, source_target_pairs={{0,8},{1,9},{2,10},{3,11},{4,12},{5,13},{6,14},{7,15},{8,0},{9,1},... | collective-permute-start | bytes 811016 | tf_op jit(solution)/shard_map/ppermute | solution.py:82
  89.1 8.1 %collective-permute-start.43 = (bf16[264,512]{1,0:T(8,128)(2,1)S(1)}, bf16[264,512]{1,0:T(8,128)(2,1)S(1)}, u32[]{:S(2)}, u32[]{:S(2)}) collective-permute-start(bf16[264,512]{1,0:T(8,128)(2,1)S(1)} %collective-permute-done.41.refs_4_), channel_id=1, source_target_pairs={{0,4},{1,5},{2,6},{3,7},{4,0},{5,1},{6,2},{7,3},{8,12},{9,13},{10,... | collective-permute-start | bytes 811016 | tf_op jit(solution)/shard_map/ppermute | solution.py:82
  90.1 10.3 %collective-permute-start.42 = (bf16[264,512]{1,0:T(8,128)(2,1)S(1)}, bf16[264,512]{1,0:T(8,128)(2,1)S(1)}, u32[]{:S(2)}, u32[]{:S(2)}) collective-permute-start(bf16[264,512]{1,0:T(8,128)(2,1)S(1)} %collective-permute-done.41.refs_4_), channel_id=1, source_target_pairs={{0,2},{1,3},{2,0},{3,1},{4,6},{5,7},{6,4},{7,5},{8,10},{9,11},{10,... | collective-permute-start | bytes 811016 | tf_op jit(solution)/shard_map/ppermute | solution.py:82
  91.3 9.6 %collective-permute-start.46 = (bf16[264,512]{1,0:T(8,128)(2,1)S(1)}, bf16[264,512]{1,0:T(8,128)(2,1)S(1)}, u32[]{:S(2)}, u32[]{:S(2)}) collective-permute-start(bf16[264,512]{1,0:T(8,128)(2,1)S(1)} %collective-permute-done.33.refs_8_), channel_id=1, source_target_pairs={{0,4},{1,5},{2,6},{3,7},{4,0},{5,1},{6,2},{7,3},{8,12},{9,13},{10,... | collective-permute-start | bytes 811016 | tf_op jit(solution)/shard_map/ppermute | solution.py:82
  92.7 13.5 %collective-permute-start.40 = (bf16[264,512]{1,0:T(8,128)(2,1)S(1)}, bf16[264,512]{1,0:T(8,128)(2,1)S(1)}, u32[]{:S(2)}, u32[]{:S(2)}) collective-permute-start(bf16[264,512]{1,0:T(8,128)(2,1)S(1)} %collective-permute-done.39.refs_2_), channel_id=1, source_target_pairs={{0,2},{1,3},{2,0},{3,1},{4,6},{5,7},{6,4},{7,5},{8,10},{9,11},{10,... | collective-permute-start | bytes 811016 | tf_op jit(solution)/shard_map/ppermute | solution.py:82
  96.0 10.8 %collective-permute-start.36 = (bf16[264,512]{1,0:T(8,128)(2,1)S(1)}, bf16[264,512]{1,0:T(8,128)(2,1)S(1)}, u32[]{:S(2)}, u32[]{:S(2)}) collective-permute-start(bf16[264,512]{1,0:T(8,128)(2,1)S(1)} %collective-permute-done.34.refs_0_), channel_id=1, source_target_pairs={{0,4},{1,5},{2,6},{3,7},{4,0},{5,1},{6,2},{7,3},{8,12},{9,13},{10,... | collective-permute-start | bytes 811016 | tf_op jit(solution)/shard_map/ppermute | solution.py:82
  97.1 12.4 %collective-permute-start.45 = (bf16[264,512]{1,0:T(8,128)(2,1)S(1)}, bf16[264,512]{1,0:T(8,128)(2,1)S(1)}, u32[]{:S(2)}, u32[]{:S(2)}) collective-permute-start(bf16[264,512]{1,0:T(8,128)(2,1)S(1)} %collective-permute-done.33.refs_8_), channel_id=1, source_target_pairs={{0,2},{1,3},{2,0},{3,1},{4,6},{5,7},{6,4},{7,5},{8,10},{9,11},{10,... | collective-permute-start | bytes 811016 | tf_op jit(solution)/shard_map/ppermute | solution.py:82
  100.3 9.2 %collective-permute-start.44 = (bf16[264,512]{1,0:T(8,128)(2,1)S(1)}, bf16[264,512]{1,0:T(8,128)(2,1)S(1)}, u32[]{:S(2)}, u32[]{:S(2)}) collective-permute-start(bf16[264,512]{1,0:T(8,128)(2,1)S(1)} %collective-permute-done.43.refs_6_), channel_id=1, source_target_pairs={{0,2},{1,3},{2,0},{3,1},{4,6},{5,7},{6,4},{7,5},{8,10},{9,11},{10,... | collective-permute-start | bytes 811016 | tf_op jit(solution)/shard_map/ppermute | solution.py:82
  101.0 8.6 %collective-permute-start.47 = (bf16[264,512]{1,0:T(8,128)(2,1)S(1)}, bf16[264,512]{1,0:T(8,128)(2,1)S(1)}, u32[]{:S(2)}, u32[]{:S(2)}) collective-permute-start(bf16[264,512]{1,0:T(8,128)(2,1)S(1)} %collective-permute-done.46.refs_10_), channel_id=1, source_target_pairs={{0,2},{1,3},{2,0},{3,1},{4,6},{5,7},{6,4},{7,5},{8,10},{9,11},{10,... | collective-permute-start | bytes 811016 | tf_op jit(solution)/shard_map/ppermute | solution.py:82
  (21 other events, 124.2 us)
